TPU v7x, 32 devices: a whole 2x2x4 slice. The times are simulated.
32 devices in a mesh: grp: 2 (over x), dap: 16 (over z, y, core).
Axes of the slice: x: 2, y: 2, z: 4, core: 2. Of those that a mesh axis runs over, the one named last changes fastest.
Arguments:
- alignment_rows: bfloat16 [32, 768, 256], P(('grp', 'dap')), parts along dimension 0, may hold values from -6 to 6
- norm_gain_vector: float32 [256], replicated, may hold values from 0.5 to 1.5
- norm_bias_vector: float32 [256], replicated, may hold values from -2 to 2
- left_weight: bfloat16 [256, 32], replicated, may hold values from -0.375 to 0.375
- right_weight: bfloat16 [256, 32], replicated, may hold values from -0.375 to 0.375
- output_weight: bfloat16 [1024, 128], replicated, may hold values from -0.1875 to 0.1875
- pair_output_gradient: bfloat16 [1536, 768, 128], P(('grp', 'dap')), parts along dimension 0, may hold values from -6 to 6
- sequence_real_mask: int32 [32], P('grp'), parts along dimension 0, may hold values 0 or 1
- sequence_chain_index: int32 [32], P('grp'), parts along dimension 0, may hold values from 0 to 4
- residue_real_mask: int32 [1536], P('grp'), parts along dimension 0, may hold values 0 or 1
- residue_chain_index: int32 [1536], P('grp'), parts along dimension 0, may hold values from 0 to 3, never falling along the last dimension, each value on 1 to 384 neighbouring positions
Outputs:
- alignment_gradient: bfloat16 [32, 768, 256], P(('grp', 'dap')), parts along dimension 0
- norm_gain_gradient: float32 [512], P('grp'), parts along dimension 0
- norm_bias_gradient: float32 [512], P('grp'), parts along dimension 0
- left_weight_gradient: float32 [512, 32], P('grp'), parts along dimension 0
- right_weight_gradient: float32 [512, 32], P('grp'), parts along dimension 0
- output_weight_gradient: float32 [2048, 128], P('grp'), parts along dimension 0
There are 2 independent parts, one for each index of `grp`. A program takes and returns all parts, laid end to end along the dimension named above; an argument that names none is the same for every part. Nothing has to cross between parts.
All inputs are finite; a program needn't handle non-finite values.
Results may differ from a plain program's by a relative error of at most 0.0075.
Values may be sent and summed in bfloat16 or wider, within the bound.
No kernel may reach another device: no remote copies, remote signals or barrier semaphores. Data moves between devices by JAX's collectives and lax.ppermute only.
A program may use at most 256 MiB of HBM per device.

v0:
```python
import jax
import jax.numpy as jnp
from jax import lax
from jax.sharding import PartitionSpec as P

CHAINS = 4


EPSILON = 1e-05


def coverage_of(sequence_real_mask, sequence_chain_index, residue_real_mask, residue_chain_index):
    paired = sequence_chain_index[:, None] == CHAINS
    same_chain = sequence_chain_index[:, None] == residue_chain_index[None, :]
    covered = jnp.where(paired | same_chain, 1.0, 0.0).astype(jnp.float32)
    return (
        covered
        * sequence_real_mask[:, None].astype(jnp.float32)
        * residue_real_mask[None, :].astype(jnp.float32)
    )


def expand_pairs(scaled_rows, output_weight, proj_width):
    product = jnp.einsum(
        "ijk,xk->ijx", scaled_rows, output_weight, preferred_element_type=jnp.float32
    )
    shape_now = scaled_rows.shape
    return product.astype(jnp.bfloat16).reshape(shape_now[0], shape_now[1], proj_width, proj_width)


def on_device(
    alignment_rows,
    norm_gain_vector,
    norm_bias_vector,
    left_weight,
    right_weight,
    output_weight,
    pair_output_gradient,
    sequence_real_mask,
    sequence_chain_index,
    residue_real_mask,
    residue_chain_index,
):
    device_index = lax.axis_index("dap")
    local_sequence_rows = alignment_rows.shape[0]
    res_here = pair_output_gradient.shape[0]
    proj_width = left_weight.shape[1]
    pair_width = output_weight.shape[1]
    coverage = coverage_of(
        sequence_real_mask, sequence_chain_index, residue_real_mask, residue_chain_index
    )
    own_cover = lax.dynamic_slice_in_dim(
        coverage, device_index * local_sequence_rows, local_sequence_rows, 0
    )
    input_tensors = alignment_rows.astype(jnp.float32)
    center = input_tensors - jnp.mean(input_tensors, axis=-1, keepdims=True)
    spread = jnp.mean(center * center, axis=-1, keepdims=True)
    inverse_deviation = lax.rsqrt(spread + EPSILON)
    single_entry = center * inverse_deviation
    normed = (single_entry * norm_gain_vector + norm_bias_vector).astype(jnp.bfloat16)
    left = jnp.einsum("sif,fc->sci", normed, left_weight, preferred_element_type=jnp.float32)
    left = (left * own_cover[:, None, :]).astype(jnp.bfloat16)
    right = jnp.einsum("sif,fc->sci", normed, right_weight, preferred_element_type=jnp.float32)
    right = (right * own_cover[:, None, :]).astype(jnp.bfloat16)
    left_cols = lax.all_to_all(left, "dap", split_axis=2, concat_axis=0, tiled=True)
    cover_cols = lax.dynamic_slice_in_dim(coverage, device_index * res_here, res_here, 1)
    count = jnp.dot(cover_cols.T, coverage, precision=lax.Precision.HIGHEST)
    scaled = (
        pair_output_gradient.astype(jnp.float32) / jnp.maximum(count, 1.0)[:, :, None]
    ).astype(jnp.bfloat16)
    out_three = output_weight.reshape(proj_width, proj_width, pair_width)
    proj_sum = jnp.einsum(
        "sej,ijk->seik",
        lax.all_gather(right, "dap", axis=0, tiled=True),
        scaled,
        preferred_element_type=jnp.float32,
    )
    proj_sum = proj_sum.astype(jnp.bfloat16)
    out_acc = jnp.einsum("sci,seik->cek", left_cols, proj_sum, preferred_element_type=jnp.float32)
    left_part = jnp.einsum("seik,cek->sci", proj_sum, out_three, preferred_element_type=jnp.float32)
    out_acc, left_sum = (out_acc, left_part)
    expanded = expand_pairs(scaled, output_weight, proj_width)
    right_sum = lax.psum_scatter(
        jnp.einsum("sci,ijce->jes", left_cols, expanded, preferred_element_type=jnp.float32),
        "dap",
        scatter_dimension=0,
        tiled=True,
    )
    right_cols = jnp.transpose(right_sum, (2, 1, 0))
    left_home, right_home = (
        lax.all_to_all(
            left_sum.astype(jnp.bfloat16), "dap", split_axis=0, concat_axis=2, tiled=True
        ).astype(left_sum.dtype),
        lax.all_to_all(
            right_cols.astype(jnp.bfloat16), "dap", split_axis=0, concat_axis=2, tiled=True
        ).astype(right_cols.dtype),
    )
    left_back = (left_home * own_cover[:, None, :]).astype(jnp.bfloat16)
    right_back = (right_home * own_cover[:, None, :]).astype(jnp.bfloat16)
    normed_grad = jnp.einsum(
        "sci,fc->sif", left_back, left_weight, preferred_element_type=jnp.float32
    )
    normed_grad = normed_grad + jnp.einsum(
        "sci,fc->sif", right_back, right_weight, preferred_element_type=jnp.float32
    )
    left_weight_gradient = jnp.einsum(
        "sif,sci->fc", normed, left_back, preferred_element_type=jnp.float32
    )
    right_weight_gradient = jnp.einsum(
        "sif,sci->fc", normed, right_back, preferred_element_type=jnp.float32
    )
    norm_gain_gradient = jnp.sum(normed_grad * single_entry, axis=(0, 1))
    norm_bias_gradient = jnp.sum(normed_grad, axis=(0, 1))
    (
        left_weight_gradient,
        right_weight_gradient,
        output_weight_gradient,
        norm_gain_gradient,
        norm_bias_gradient,
    ) = lax.psum(
        (
            left_weight_gradient,
            right_weight_gradient,
            out_acc.reshape(proj_width * proj_width, pair_width),
            norm_gain_gradient,
            norm_bias_gradient,
        ),
        "dap",
    )
    rescaled_gradient = normed_grad * norm_gain_vector
    alignment_gradient = inverse_deviation * (
        rescaled_gradient
        - jnp.mean(rescaled_gradient, axis=-1, keepdims=True)
        - single_entry * jnp.mean(rescaled_gradient * single_entry, axis=-1, keepdims=True)
    )
    return (
        alignment_gradient.astype(jnp.bfloat16),
        norm_gain_gradient,
        norm_bias_gradient,
        left_weight_gradient,
        right_weight_gradient,
        output_weight_gradient,
    )


def solution(mesh):
    in_specs = (
        P(("grp", "dap"), None, None),
        P(),
        P(),
        P(),
        P(),
        P(),
        P(("grp", "dap"), None, None),
        P("grp"),
        P("grp"),
        P("grp"),
        P("grp"),
    )
    out_specs = (
        P(("grp", "dap"), None, None),
        P("grp"),
        P("grp"),
        P("grp", None),
        P("grp", None),
        P("grp", None),
    )
    return jax.shard_map(
        on_device, mesh=mesh, in_specs=in_specs, out_specs=out_specs, check_vma=False
    )
```

profile of v0, /device:TPU:0, one launch (start us, length us, event | category | flops | bytes accessed | tf_op | source)
XLA Modules:
  0.0 559.9 jit_solution(10131881415864676241)
XLA Ops:
  9.2 1.2 convert_reduce_fusion
  10.4 1.3 fusion.43
  12.5 1.3 fusion.44
  13.8 1.0 fusion.28
  15.7 1.9 reduce.9
  18.4 7.4 %all-to-all-start.1 = ((bf16[16,2,768]{2,1,0:T(2,128)(2,1)}), bf16[16,2,768]{2,1,0:T(2,128)(2,1)S(1)}, u32[]{:S(2)}, u32[]{:S(2)}) async-start(bf16[16,2,768]{2,1,0:T(2,128)(2,1)} %reshape.198), calls=%async_computation.1 | async-start | bytes 98304 | tf_op jit(solution)/shard_map/all_to_all | solution.py:65
  26.5 30.8 %convolution_convert_fusion = bf16[48,768,1024]{2,1,0:T(8,128)(2,1)} fusion(bf16[1024,128]{1,0:T(8,128)(2,1)} %param.16, bf16[48,768,128]{2,1,0:T(8,128)(2,1)} %param.17, f32[48,768]{1,0:T(8,128)S(1)} %convolution_maximum_fusion), kind=kOutput, calls=%fused_computation.2 | convolution fusion | flops 9715580928 | bytes 85344256 | tf_op jit(solution)/shard_map/ijk,xk->ijx/dot_general | solution.py:24
  57.3 24.0 %all-gather = bf16[512,768]{1,0:T(8,128)(2,1)S(1)} all-gather(bf16[32,768]{1,0:T(8,128)(2,1)S(1)} %fusion.29), channel_id=2, replica_groups=mesh['grp'=2,'dap'=16] {'dap'}, dimensions={0}, use_global_device_ids=true | all-gather | bytes 835584 | tf_op jit(solution)/shard_map/all_gather | solution.py:74
  81.3 96.6 %copy.38 = bf16[48,768,1024]{1,2,0:T(8,128)(2,1)} copy(bf16[48,768,1024]{2,1,0:T(8,128)(2,1)} %convolution_convert_fusion) | data formatting | bytes 150994944 | tf_op jit(solution)/shard_map/convert_element_type | solution.py:28
  178.6 115.5 %fusion.11 = f32[768,32,16]{0,2,1:T(8,128)S(1)} fusion(bf16[48,768,32,32]{1,3,2,0:T(8,128)(2,1)} %bitcast.14, bf16[1,32,16,48]{3,2,1,0:T(8,128)(2,1)S(1)} %all_to_all.14), kind=kOutput, calls=%fused_computation.11 | convolution fusion | flops 1207959552 | bytes 77119488 | tf_op jit(solution)/shard_map/sci,ijce->jes/dot_general | solution.py:84
  294.0 5.2 copy.53
  299.3 5.5 reshape.192
  304.8 9.3 %fusion.8 = bf16[16,32,48,128]{3,1,2,0:T(8,128)(2,1)S(1)} fusion(bf16[16,32,768,1]{2,1,3,0:T(8,128)(2,1)S(1)} %bitcast.107, bf16[48,768,128]{2,1,0:T(8,128)(2,1)} %param.17, f32[48,768]{1,0:T(8,128)S(1)} %convolution_maximum_fusion), kind=kOutput, calls=%fused_computation.10 | convolution fusion | flops 4849139712 | bytes 16662528 | tf_op jit(solution)/shard_map/sej,ijk->seik/dot_general | solution.py:72
  314.1 2.7 copy-done.5
  316.8 3.8 fusion.23
  321.4 3.5 all-to-all-start
  325.0 4.9 fusion.14
  329.9 1.1 copy.48
  332.1 29.6 %reduce-scatter.4.cloned.1.call-done = f32[48,512]{1,0:T(8,128)} async-done(((f32[768,512]{1,0:T(8,128)}), f32[48,512]{1,0:T(8,128)}) %reduce-scatter.4.cloned.1.call-update) | async-done | bytes 98320
  361.7 1.0 reshape.193
  363.8 3.7 all-to-all-start.2
  368.1 6.2 %all-to-all-done.2 = bf16[16,2,768]{2,1,0:T(2,128)(2,1)S(1)} async-done(((bf16[16,2,768]{2,1,0:T(2,128)(2,1)}), bf16[16,2,768]{2,1,0:T(2,128)(2,1)S(1)}, u32[]{:S(2)}, u32[]{:S(2)}) %all-to-all-start.2) | async-done | bytes 49184 | tf_op jit(solution)/shard_map/all_to_all | solution.py:94
  374.8 0.8 fusion.62
  375.9 1.0 fusion.42
  378.7 1.2 fusion.41
  379.9 75.3 %all-reduce.4.cloned.1.call-done = f32[1024,128]{1,0:T(8,128)} async-done(((f32[1024,128]{1,0:T(8,128)}), f32[1024,128]{1,0:T(8,128)}) %all-reduce.4.cloned.1.call-update) | async-done | bytes 524304 | tf_op jit(solution)/shard_map/psum | solution.py:120
  455.2 90.8 %all-reduce.6.cloned.1.call-done = (f32[256]{0:T(256)}, f32[256]{0:T(256)}, f32[256,32]{0,1:T(8,128)}, f32[256,32]{0,1:T(8,128)}) async-done(((f32[256]{0:T(256)}, f32[256]{0:T(256)}, f32[256,32]{0,1:T(8,128)}, f32[256,32]{0,1:T(8,128)}), (f32[256]{0:T(256)}, f32[256]{0:T(256)}, f32[256,32]{0,1:T(8,128)}, f32[256,32]{0,1:T(8,128)})) %all-reduce.6.cloned.1.call-update) | async-done | bytes 67600 | tf_op jit(solution)/shard_map/psum | solution.py:120
  546.0 1.2 copy.85
  547.3 1.2 copy.86
  548.5 1.4 copy.87
  549.9 1.4 copy.88
  551.2 1.9 copy.89
  (55 shorter events, 12.0 us)
Async XLA Ops:
  7.2 19.1 %copy-start = (bf16[256,32]{0,1:T(8,128)(2,1)S(1)}, bf16[256,32]{0,1:T(8,128)(2,1)}, u32[]{:S(2)}) copy-start(bf16[256,32]{0,1:T(8,128)(2,1)} %param.15) | copy-start | bytes 49156
  18.4 159.5 %all-to-all-start.1 = ((bf16[16,2,768]{2,1,0:T(2,128)(2,1)}), bf16[16,2,768]{2,1,0:T(2,128)(2,1)S(1)}, u32[]{:S(2)}, u32[]{:S(2)}) async-start(bf16[16,2,768]{2,1,0:T(2,128)(2,1)} %reshape.198), calls=%async_computation.1 | async-start | bytes 98304 | tf_op jit(solution)/shard_map/all_to_all | solution.py:65
  25.8 335.9 %reduce-scatter.4.cloned.1.call-start = ((), (), s32[]{:S(2)}) async-start(), calls=%async_computation.5 | async-start | bytes 1671168
  304.8 11.9 %copy-start.4 = (bf16[1024,128]{1,0:T(8,128)(2,1)S(1)}, bf16[1024,128]{1,0:T(8,128)(2,1)}, u32[]{:S(2)}) copy-start(bf16[1024,128]{1,0:T(8,128)(2,1)} %param.16) | copy-start | bytes 786436
  314.1 2.7 copy-start.5
  316.8 51.0 %copy-start.2 = (bf16[256,32]{0,1:T(8,128)(2,1)S(1)}, bf16[256,32]{0,1:T(8,128)(2,1)}, u32[]{:S(2)}) copy-start(bf16[256,32]{0,1:T(8,128)(2,1)} %param.14) | copy-start | bytes 49156
  320.5 55.4 %copy-start.1 = (bf16[1,768,256]{2,1,0:T(8,128)(2,1)S(1)}, bf16[1,768,256]{2,1,0:T(8,128)(2,1)}, u32[]{:S(2)}) copy-start(bf16[1,768,256]{2,1,0:T(8,128)(2,1)} %param.11) | copy-start | bytes 1179652
  320.6 55.4 %copy-start.3 = (f32[256]{0:T(256)S(1)}, f32[256]{0:T(256)}, u32[]{:S(2)}) copy-start(f32[256]{0:T(256)} %param.12) | copy-start | bytes 3076
  321.4 10.2 %all-to-all-start = ((bf16[16,2,768]{2,1,0:T(2,128)(2,1)}), bf16[16,2,768]{2,1,0:T(2,128)(2,1)S(1)}, u32[]{:S(2)}, u32[]{:S(2)}) async-start(bf16[16,2,768]{2,1,0:T(2,128)(2,1)} %reshape.196), calls=%async_computation | async-start | bytes 98304 | tf_op jit(solution)/shard_map/all_to_all | solution.py:91
  324.9 130.3 %all-reduce.4.cloned.1.call-start = ((), (), s32[]{:S(2)}) async-start(), calls=%async_computation.4 | async-start | bytes 1048576 | tf_op jit(solution)/shard_map/psum | solution.py:120
  363.8 10.5 %all-to-all-start.2 = ((bf16[16,2,768]{2,1,0:T(2,128)(2,1)}), bf16[16,2,768]{2,1,0:T(2,128)(2,1)S(1)}, u32[]{:S(2)}, u32[]{:S(2)}) async-start(bf16[16,2,768]{2,1,0:T(2,128)(2,1)} %reshape.200), calls=%async_computation.2 | async-start | bytes 98304 | tf_op jit(solution)/shard_map/all_to_all | solution.py:94
  367.6 178.5 %all-reduce.6.cloned.1.call-start = ((), (), s32[]{:S(2)}) async-start(), calls=%async_computation.6 | async-start | bytes 135168 | tf_op jit(solution)/shard_map/psum | solution.py:120
Sparse Core Ops, SparseCore 0:
  304.9 56.7 reduce-scatter.3
  366.1 89.1 all-reduce.3
  460.2 85.8 all-reduce.5
where the time goes:
time: 570 us; the launch traced here: 560 us
  waiting for transfers between devices  203 us (36%)
  matrix products  169 us (30%)
  local copies, waits for them, and re-layouts  125 us (22%)
  blocking collectives  24 us (4%)
  starting transfers between devices  15 us (3%)
  between operations  14.3 us (3%)
  other arithmetic  10.5 us (2%)
    psum x2, waiting for transfers between devices, on_device(): lax.psum((left_weight_gradient, right_weight_gradient, out_acc.reshape(pr...  166 us
    dot_general x1, matrix products, on_device(): jnp.einsum('sci,ijce->jes', left_cols, expanded, preferred_element_type=j...  115 us
    convert_element_type x1, local copies, waits for them, and re-layouts, expand_pairs(): product.astype(jnp.bfloat16)  96.6 us
    dot_general x1, matrix products, expand_pairs(): jnp.einsum('ijk,xk->ijx', scaled_rows, output_weight, preferred_element_t...  30.8 us
    unnamed x4, waiting for transfers between devices  29.6 us
    unnamed x28, local copies, waits for them, and re-layouts  25.3 us
    all_gather x1, blocking collectives, on_device(): lax.all_gather(right, 'dap', axis=0, tiled=True)  24 us
  transfers between devices with their start and end apart: 6, of which 5 were waited for; matrix products, arithmetic and copies ran while one was open for 28% of the time, Pallas kernels for 0%

commit v1 on v0

v1 whole, which is shorter than its diff:
```python
import functools

import jax
import jax.numpy as jnp
from jax import lax
from jax.experimental import pallas as pl
from jax.experimental.pallas import tpu as pltpu
from jax.sharding import PartitionSpec as P

CHAINS = 4
EPSILON = 1e-05
AXIS = "dap"
F32 = jnp.float32
BF16 = jnp.bfloat16
VMEM_LIMIT = 56 * 1024 * 1024


def mm(a, b, dims=(1, 0)):
    return lax.dot_general(
        a, b, (((dims[0],), (dims[1],)), ((), ())), preferred_element_type=F32
    )


def params(**more):
    return pltpu.CompilerParams(vmem_limit_bytes=VMEM_LIMIT, **more)


def whole(*shape):
    return pl.BlockSpec(shape, lambda *_: (0,) * len(shape))


def normalise(x):
    center = x - jnp.mean(x, axis=-1, keepdims=True)
    inverse = lax.rsqrt(jnp.mean(center * center, axis=-1, keepdims=True) + EPSILON)
    return center * inverse, inverse


def project_kernel(mask_ref, chain_ref, x_ref, gain_ref, bias_ref, lw_ref, rwt_ref,
                   rmask_ref, rchain_ref, left_ref, right_ref):
    me = lax.axis_index(AXIS)
    unit, _ = normalise(x_ref[...].astype(F32))
    normed = (unit * gain_ref[...] + bias_ref[...]).astype(BF16)
    left_ref[...] = mm(normed, lw_ref[...]).astype(BF16)
    chain = chain_ref[me]
    covered = jnp.logical_or(chain == CHAINS, rchain_ref[...] == chain)
    cover = jnp.where(covered, 1.0, 0.0) * (rmask_ref[...] * mask_ref[me]).astype(F32)
    right_ref[...] = (mm(rwt_ref[...], normed, (1, 1)) * cover).astype(BF16)


def project(x, gain, bias, lw, rwt, smask, schain, rmask, rchain):
    rows, _ = x.shape
    width = lw.shape[1]
    smem = pl.BlockSpec(memory_space=pltpu.SMEM)
    vmem = pl.BlockSpec(memory_space=pltpu.VMEM)
    return pl.pallas_call(
        project_kernel,
        out_shape=(
            jax.ShapeDtypeStruct((rows, width), BF16),
            jax.ShapeDtypeStruct((width, rows), BF16),
        ),
        in_specs=[smem, smem] + [vmem] * 7,
        out_specs=(vmem, vmem),
        compiler_params=params(),
        name="project",
    )(smask, schain, x, gain, bias, lw, rwt, rmask, rchain)


def scale_kernel(block, g_ref, r_ref, out_ref):
    pair = g_ref.shape[2]
    factor = jnp.transpose(r_ref[...])
    for b in range(block):
        out_ref[:, b * pair : (b + 1) * pair] = (
            g_ref[b].astype(F32) * factor[:, b : b + 1]
        ).astype(BF16)


def scale(gradient, reciprocal, block):
    rows, cols, pair = gradient.shape
    return pl.pallas_call(
        functools.partial(scale_kernel, block),
        grid=(rows // block,),
        out_shape=jax.ShapeDtypeStruct((cols, rows * pair), BF16),
        in_specs=[
            pl.BlockSpec((block, cols, pair), lambda b: (b, 0, 0)),
            pl.BlockSpec((block, cols), lambda b: (b, 0)),
        ],
        out_specs=pl.BlockSpec((cols, block * pair), lambda b: (0, b)),
        compiler_params=params(),
        cost_estimate=pl.CostEstimate(
            flops=gradient.size, bytes_accessed=4 * gradient.size, transcendentals=0
        ),
        name="scale",
    )(gradient, reciprocal)


def order_left(l_ref, scratch):
    seqs, rows, _ = l_ref.shape
    for s in range(seqs):
        scratch[pl.ds(s, rows, stride=seqs), :] = l_ref[s].astype(F32)


def left_block(scratch, mask_ref, step, size):
    at = pl.ds(pl.multiple_of(step * size, size), size)
    return (scratch[at, :] * mask_ref[at, :]).astype(BF16)


def right_sum_kernel(block, l_ref, mask_ref, w_ref, s_ref, out_ref, ordered, mixed, total):
    step = pl.program_id(0)
    seqs = l_ref.shape[0]
    pair = s_ref.shape[1] // block
    width = w_ref.shape[1] // pair

    @pl.when(step == 0)
    def _():
        order_left(l_ref, ordered)
        total[...] = jnp.zeros_like(total)

    left = left_block(ordered, mask_ref, step, block * seqs)
    group = 8
    for first in range(0, width, group):
        part = mm(left, w_ref[:, first * pair : (first + group) * pair]).astype(BF16)
        for e in range(group):
            for i in range(block):
                mixed[(first + e) * seqs : (first + e + 1) * seqs, i * pair : (i + 1) * pair] = part[
                    i * seqs : (i + 1) * seqs, e * pair : (e + 1) * pair
                ]
    total[...] += mm(s_ref[...], mixed[...], (1, 1))

    @pl.when(step == pl.num_programs(0) - 1)
    def _():
        out_ref[...] = total[...].astype(BF16)


def right_sum(left, mask, weight, scaled, block):
    seqs, rows, width = left.shape
    cols = scaled.shape[0]
    pair = scaled.shape[1] // rows
    wide = weight.shape[1] // pair * seqs
    return pl.pallas_call(
        functools.partial(right_sum_kernel, block),
        grid=(rows // block,),
        out_shape=jax.ShapeDtypeStruct((cols, wide), BF16),
        in_specs=[
            whole(*left.shape),
            whole(*mask.shape),
            whole(*weight.shape),
            pl.BlockSpec((cols, block * pair), lambda b: (0, b)),
        ],
        out_specs=whole(cols, wide),
        scratch_shapes=[
            pltpu.VMEM((rows * seqs, width), F32),
            pltpu.VMEM((wide, block * pair), BF16),
            pltpu.VMEM((cols, wide), F32),
        ],
        compiler_params=params(),
        cost_estimate=pl.CostEstimate(
            flops=2 * cols * wide * rows * pair, bytes_accessed=2 * scaled.size, transcendentals=0
        ),
        name="right_sum",
    )(left, mask, weight, scaled)


def left_side_kernel(block, sorting, *refs):
    if sorting:
        near_ref, far_ref, sort_ref, *refs = refs
        l_ref, mask_ref, w_ref, s_ref, back_ref, out_ref, ordered, proj, total, spread, right = refs
    else:
        right, *refs = refs
        l_ref, mask_ref, w_ref, s_ref, back_ref, out_ref, ordered, proj, total, spread = refs
    step = pl.program_id(0)
    seqs = l_ref.shape[0]
    pair = s_ref.shape[1] // block
    width = w_ref.shape[0] // pair

    @pl.when(step == 0)
    def _():
        order_left(l_ref, ordered)
        total[...] = jnp.zeros_like(total)
        if sorting:
            half = near_ref.shape[0]
            right[...] = (
                mm(sort_ref[:, :half], near_ref[...]) + mm(sort_ref[:, half:], far_ref[...])
            ).astype(BF16)

    for i in range(block):
        part = mm(right[...], s_ref[:, i * pair : (i + 1) * pair]).astype(BF16)
        for e in range(width):
            proj[i * seqs : (i + 1) * seqs, e * pair : (e + 1) * pair] = part[
                e * seqs : (e + 1) * seqs, :
            ]
    left = left_block(ordered, mask_ref, step, block * seqs)
    back_ref[...] = mm(proj[...], w_ref[...])
    total[...] += mm(left, proj[...], (0, 0))

    @pl.when(step == pl.num_programs(0) - 1)
    def _():
        for e in range(width):
            spread[pl.ds(e, total.shape[0], stride=width), :] = total[:, e * pair : (e + 1) * pair]
        out_ref[...] = spread[...].astype(BF16)


def left_side(rights, left, mask, weight, scaled, block):
    seqs, rows, width = left.shape
    cols = scaled.shape[0]
    pair = scaled.shape[1] // rows
    return pl.pallas_call(
        functools.partial(left_side_kernel, block, len(rights) > 1),
        grid=(rows // block,),
        out_shape=(
            jax.ShapeDtypeStruct((rows * seqs, width), F32),
            jax.ShapeDtypeStruct((width * width, pair), BF16),
        ),
        in_specs=[whole(*a.shape) for a in rights]
        + [
            whole(*left.shape),
            whole(*mask.shape),
            whole(*weight.shape),
            pl.BlockSpec((cols, block * pair), lambda b: (0, b)),
        ],
        out_specs=(
            pl.BlockSpec((block * seqs, width), lambda b: (b, 0)),
            whole(width * width, pair),
        ),
        scratch_shapes=[
            pltpu.VMEM((rows * seqs, width), F32),
            pltpu.VMEM((block * seqs, width * pair), BF16),
            pltpu.VMEM((width, width * pair), F32),
            pltpu.VMEM((width * width, pair), F32),
        ]
        + [pltpu.VMEM((width * seqs, cols), BF16)] * (len(rights) > 1),
        compiler_params=params(),
        cost_estimate=pl.CostEstimate(
            flops=2 * cols * width * seqs * rows * pair,
            bytes_accessed=2 * scaled.size,
            transcendentals=0,
        ),
        name="left_side",
    )(*rights, left, mask, weight, scaled)


def owner_kernel(seqs, swapping, *refs):
    if swapping:
        swap_ref, *refs = refs
    (parts_ref, back_ref, lmask_ref, rmask_ref, x_ref, gain_ref, bias_ref, w_ref,
     sums_ref, home_ref, masked, rows_ref) = refs
    count, res, _ = parts_ref.shape
    width = back_ref.shape[1]
    right = parts_ref[0].astype(F32)
    for p in range(1, count):
        right = right + parts_ref[p].astype(F32)
    right = (right * rmask_ref[...]).astype(BF16)
    right = mm(right, swap_ref[...]) if swapping else right.astype(F32)
    masked[...] = back_ref[...] * lmask_ref[...]
    for s in range(seqs):
        rows_ref[s * res : (s + 1) * res, :width] = masked[pl.ds(s, res, stride=seqs), :]
        rows_ref[s * res : (s + 1) * res, width:] = right[:, s * width : (s + 1) * width]
    both = rows_ref[...].astype(BF16)
    home_ref[...] = both
    unit, _ = normalise(x_ref[...].astype(F32))
    normed = (unit * gain_ref[...] + bias_ref[...]).astype(BF16)
    normed_grad = mm(both, w_ref[...], (1, 1))
    sums_ref[: 2 * width, :] = mm(both, normed, (0, 0))
    sums_ref[2 * width : 2 * width + 1, :] = jnp.sum(normed_grad * unit, axis=0, keepdims=True)
    sums_ref[2 * width + 1 : 2 * width + 2, :] = jnp.sum(normed_grad, axis=0, keepdims=True)
    sums_ref[2 * width + 2 :, :] = jnp.zeros((6, sums_ref.shape[1]), F32)


def owner(swap, parts, back, lmask, rmask, x, gain, bias, weights, seqs):
    rows, width = back.shape
    features = x.shape[1]
    vmem = pl.BlockSpec(memory_space=pltpu.VMEM)
    return pl.pallas_call(
        functools.partial(owner_kernel, seqs, bool(swap)),
        out_shape=(
            jax.ShapeDtypeStruct((2 * width + 8, features), F32),
            jax.ShapeDtypeStruct((rows, 2 * width), BF16),
        ),
        in_specs=[vmem] * (8 + len(swap)),
        out_specs=(vmem, vmem),
        scratch_shapes=[pltpu.VMEM((rows, width), F32), pltpu.VMEM((rows, 2 * width), F32)],
        compiler_params=params(),
        name="owner",
    )(*swap, parts, back, lmask, rmask, x, gain, bias, weights)


def home_kernel(both_ref, x_ref, gain_ref, w_ref, out_ref):
    unit, inverse = normalise(x_ref[...].astype(F32))
    d = mm(both_ref[...], w_ref[...], (1, 1)) * gain_ref[...]
    out_ref[...] = (
        inverse
        * (
            d
            - jnp.mean(d, axis=-1, keepdims=True)
            - unit * jnp.mean(d * unit, axis=-1, keepdims=True)
        )
    ).astype(BF16)


def home(both, x, gain, weights):
    vmem = pl.BlockSpec(memory_space=pltpu.VMEM)
    return pl.pallas_call(
        home_kernel,
        out_shape=jax.ShapeDtypeStruct(x.shape, BF16),
        in_specs=[vmem] * 4,
        out_specs=vmem,
        compiler_params=params(),
        name="home",
    )(both, x, gain, weights)


def on_device(
    size,
    alignment_rows,
    norm_gain_vector,
    norm_bias_vector,
    left_weight,
    right_weight,
    output_weight,
    pair_output_gradient,
    sequence_real_mask,
    sequence_chain_index,
    residue_real_mask,
    residue_chain_index,
):
    me = lax.axis_index(AXIS)
    core = me % 2
    chips = size // 2
    same_core = [[d for d in range(size) if d % 2 == c] for c in (0, 1)]
    res, cols, pair = pair_output_gradient.shape
    width = left_weight.shape[1]
    features = left_weight.shape[0]
    seqs = sequence_real_mask.shape[0]
    block = max(b for b in range(1, 9) if res % b == 0)

    def swap_with(value, bit):
        return lax.ppermute(value, AXIS, [(d, d ^ bit) for d in range(size)])

    x = alignment_rows.reshape(cols, features)
    gain = norm_gain_vector.reshape(1, features)
    bias = norm_bias_vector.reshape(1, features)
    left, right = project(
        x, gain, bias, left_weight, right_weight.T,
        sequence_real_mask, sequence_chain_index,
        residue_real_mask.reshape(1, cols), residue_chain_index.reshape(1, cols),
    )
    left_all = lax.all_to_all(left.reshape(size, res, width), AXIS, 0, 0, tiled=True)
    near = lax.all_to_all(
        jnp.broadcast_to(right, (chips, width, cols)), AXIS, 0, 0, tiled=True,
        axis_index_groups=same_core,
    ).reshape(chips * width, cols)
    far = swap_with(near, 1)
    x_own = lax.all_to_all(x.reshape(size, res, features), AXIS, 0, 0, tiled=True)
    x_own = x_own.reshape(size * res, features)

    covered = (sequence_chain_index[:, None] == CHAINS) | (
        sequence_chain_index[:, None] == residue_chain_index[None, :]
    )
    coverage = (
        jnp.where(covered, 1.0, 0.0)
        * sequence_real_mask[:, None].astype(F32)
        * residue_real_mask[None, :].astype(F32)
    )
    own = lax.dynamic_slice_in_dim(coverage, me * res, res, 1)
    count = mm(own.astype(BF16), coverage.astype(BF16), (0, 0))
    reciprocal = 1.0 / jnp.maximum(count, 1.0)
    lmask = own.T.reshape(res * seqs, 1)
    rmask = jnp.tile(own.T, (1, width))

    def place(n, dim):
        return lax.broadcasted_iota(jnp.int32, (n, n), dim)

    wide = width * seqs
    small = wide <= 1024
    if small:
        row, col = place(wide, 0), place(wide, 1)
        from_core, chip, at = col // (chips * width), (col // width) % chips, col % width
        sort = (row == at * seqs + 2 * chip + (from_core ^ core)).astype(BF16)
        rights = [near, far, sort]
        swap = [((row // seqs == col % width) & (row % seqs == col // width)).astype(BF16)]
    else:
        even, odd = jnp.where(core == 0, near, far), jnp.where(core == 0, far, near)
        both = jnp.stack([even.reshape(chips, width, cols), odd.reshape(chips, width, cols)])
        rights = [both.transpose(2, 1, 0, 3).reshape(wide, cols)]
        swap = []

    w_mix = output_weight.reshape(width, width * pair)
    w_back = w_mix.T
    weights = jnp.concatenate([left_weight, right_weight], axis=1)

    scaled = scale(pair_output_gradient, reciprocal, block)
    shares = right_sum(left_all, lmask, w_mix, scaled, block).reshape(chips, 2, res, wide)
    keep = lax.dynamic_index_in_dim(shares, core, 1, keepdims=False)
    give = lax.dynamic_index_in_dim(shares, 1 - core, 1, keepdims=False)
    of_chip = (keep.astype(F32) + swap_with(give, 1).astype(F32)).astype(BF16)
    parts = lax.all_to_all(of_chip, AXIS, 0, 0, tiled=True, axis_index_groups=same_core)

    back, out_share = left_side(rights, left_all, lmask, w_back, scaled, block)
    out_parts = lax.all_to_all(
        out_share.reshape(size, width * width // size, pair), AXIS, 0, 0, tiled=True
    )
    out_piece = jnp.sum(out_parts.astype(F32), axis=0).astype(BF16)[None]

    if not small:
        parts = jnp.sum(parts.astype(F32), axis=0, keepdims=True)
        parts = parts.reshape(1, res, width, seqs).swapaxes(2, 3).reshape(1, res, wide)
        rmask = jnp.repeat(own.T, width, axis=1)
    sums, both = owner(swap, parts, back, lmask, rmask, x_own, gain, bias, weights, seqs)
    both_home = lax.all_to_all(both.reshape(size, res, 2 * width), AXIS, 0, 0, tiled=True)

    bit = size // 2
    while bit:
        sums = sums + swap_with(sums, bit)
        out_piece = jnp.concatenate([out_piece, swap_with(out_piece, bit)], axis=0)
        bit //= 2
    bits = size.bit_length() - 1
    wanted = jnp.arange(size) ^ me
    spot = sum(((wanted >> b) & 1) << (bits - 1 - b) for b in range(bits))
    out_weight_gradient = jnp.take(out_piece, spot, axis=0).astype(F32).reshape(width * width, pair)

    alignment_gradient = home(both_home.reshape(cols, 2 * width), x, gain, weights)
    return (
        alignment_gradient.reshape(alignment_rows.shape),
        sums[2 * width],
        sums[2 * width + 1],
        sums[:width].T,
        sums[width : 2 * width].T,
        out_weight_gradient,
    )


def solution(mesh):
    rows = P(("grp", "dap"), None, None)
    in_specs = (rows, P(), P(), P(), P(), P(), rows, P("grp"), P("grp"), P("grp"), P("grp"))
    out_specs = (rows, P("grp"), P("grp"), P("grp", None), P("grp", None), P("grp", None))
    return jax.shard_map(
        functools.partial(on_device, mesh.shape[AXIS]),
        mesh=mesh,
        in_specs=in_specs,
        out_specs=out_specs,
        check_vma=False,
    )
```

time: 570 us -> 151 us (0.26); the launches traced: 560 us -> 150 us
  waiting for transfers between devices: 203 us -> 26.7 us
  matrix products: 169 us -> 1.76 us
  local copies, waits for them, and re-layouts: 125 us -> 20.5 us
  Pallas kernels: 0 us -> 48.4 us
  starting transfers between devices: 15 us -> 42.2 us
  blocking collectives: 24 us -> 0 us
  between operations: 14.3 us -> 0.86 us
    dot_general x12 -> x1, matrix products: 169 us -> 1.76 us  [mm(): lax.dot_general(a, b, (((dims[0],), (dims[1],)), ((), ())), preferred_ele...]
    psum x2 -> x0, waiting for transfers between devices: 166 us -> none  [on_device(): lax.psum((left_weight_gradient, right_weight_gradient, out_acc.reshape(pr...]
    convert_element_type x10 -> x0, local copies, waits for them, and re-layouts: 98 us -> none  [the longest x1 96.6 us: expand_pairs(): product.astype(jnp.bfloat16)]
    pallas_call x0 -> x6, Pallas kernels: none -> 48.4 us  [the longest x1 17.6 us: left_side(): pl.pallas_call(functools.partial(left_side_kernel, block, len(rights) > 1...]
    unnamed x4 -> x0, waiting for transfers between devices: 29.6 us -> none
    all_gather x1 -> x0, blocking collectives: 24 us -> none  [on_device(): lax.all_gather(right, 'dap', axis=0, tiled=True)]
    ppermute x0 -> x10, waiting for transfers between devices: none -> 19 us  [swap_with(): return lax.ppermute(value, AXIS, [(d, d ^ bit) for d in range(size)])]
    unnamed x28 -> x24, local copies, waits for them, and re-layouts: 25.3 us -> 6.67 us
  transfers between devices with their start and end apart: 6 -> 16, of which waited for: 5 -> 8; matrix products, arithmetic and copies ran while one was open for 28% -> 13% of each run, Pallas kernels for 0% -> 28%
where the time goes in v1:
time: 151 us; the launch traced here: 150 us
  Pallas kernels  48.4 us (32%)
  starting transfers between devices  42.2 us (28%)
  waiting for transfers between devices  26.7 us (18%)
  local copies, waits for them, and re-layouts  20.5 us (14%)
  other arithmetic  9.19 us (6%)
  matrix products  1.76 us (1%)
    ppermute x10, waiting for transfers between devices, swap_with(): return lax.ppermute(value, AXIS, [(d, d ^ bit) for d in range(size)])  19 us
    pallas_call x1, Pallas kernels, left_side(): pl.pallas_call(functools.partial(left_side_kernel, block, len(rights) > 1...  17.6 us
    pallas_call x1, Pallas kernels, right_sum(): pl.pallas_call(functools.partial(right_sum_kernel, block), grid=(rows //...  11.4 us
    pallas_call x1, Pallas kernels, scale(): pl.pallas_call(functools.partial(scale_kernel, block), grid=(rows // bloc...  11 us
    ppermute x10, starting transfers between devices, swap_with(): return lax.ppermute(value, AXIS, [(d, d ^ bit) for d in range(size)])  11 us
    all_to_all x1, starting transfers between devices, on_device(): lax.all_to_all(left.reshape(size, res, width), AXIS, 0, 0, tiled=True)  7.39 us
    unnamed x24, local copies, waits for them, and re-layouts  6.67 us
    all_to_all x1, starting transfers between devices, on_device(): lax.all_to_all(x.reshape(size, res, features), AXIS, 0, 0, tiled=True)  6.12 us
  transfers between devices with their start and end apart: 16, of which 8 were waited for; matrix products, arithmetic and copies ran while one was open for 13% of the time, Pallas kernels for 28%

profile of v1, /device:TPU:0, one launch (start us, length us, event | category | flops | bytes accessed | tf_op | source)
XLA Modules:
  0.0 149.7 jit_solution(6742894018902797309)
XLA Ops:
  0.6 1.4 copy.31.lw_ref
  4.6 2.4 %project.1 = (bf16[768,32]{1,0:T(8,128)(2,1)}, bf16[32,768]{1,0:T(8,128)(2,1)}) custom-call(s32[16]{0:T(128)} %mask_ref.1, s32[16]{0:T(128)} %chain_ref.1, bf16[768,256]{1,0:T(8,128)(2,1)} %bitcast.x_ref, f32[1,256]{1,0:T(1,128)} %bitcast.59, f32[1,256]{1,0:T(1,128)} %bitcast.62, bf16[256,32]{1,0:T(8,128)(2,1)} %copy.31.lw_ref, bf16[32,256]{1,0:T(8,128)(2,1)} %bitcast.58, ...), custom_call_target="tpu_custom_call" | custom-call | tf_op jit(solution)/shard_map/project/pallas_call | solution.py:55
  8.9 7.4 %all-to-all-start = ((bf16[16,2,768]{2,1,0:T(2,128)(2,1)}), bf16[16,2,768]{2,1,0:T(2,128)(2,1)S(1)}, u32[]{:S(2)}, u32[]{:S(2)}) async-start(bf16[16,2,768]{2,1,0:T(2,128)(2,1)} %reshape.165), calls=%async_computation | async-start | bytes 98304 | tf_op jit(solution)/shard_map/all_to_all | solution.py:346
  19.3 1.8 %fusion.r_ref = f32[48,768]{1,0:T(8,128)} fusion(f32[768]{0:T(1024)S(1)} %convert_element_type.40, f32[16]{0:T(128)S(1)} %convert_element_type.39, s32[16]{0:T(128)} %chain_ref.1, s32[768]{0:T(1024)} %param.21, pred[16]{0:T(512)(128)(4,1)S(1)} %broadcast_compare_fusion, f32[16,768]{0,1:T(8,128)S(1)} %multiply_multiply_fusion, s32[]{:T(128)S(6)} %select_n.79), kind=kOutput, calls=%fused_computation.10 | convolution fusion | flops 1327104 | bytes 168004 | tf_op jit(solution)/shard_map/dot_general | solution.py:19
  21.0 2.0 %all-to-all-done = bf16[16,2,768]{2,1,0:T(2,128)(2,1)S(1)} async-done(((bf16[16,2,768]{2,1,0:T(2,128)(2,1)}), bf16[16,2,768]{2,1,0:T(2,128)(2,1)S(1)}, u32[]{:S(2)}, u32[]{:S(2)}) %all-to-all-start) | async-done | bytes 49184 | tf_op jit(solution)/shard_map/all_to_all | solution.py:346
  23.0 1.6 %broadcast_in_dim.35 = bf16[8,32,768]{2,1,0:T(8,128)(2,1)} broadcast(bf16[32,768]{1,0:T(8,128)(2,1)} %get-tuple-element.13), dimensions={1,2} | broadcast | bytes 442368 | tf_op jit(solution)/shard_map/broadcast_in_dim | solution.py:348
  24.6 3.9 %all-to-all-start.2 = ((bf16[8,32,768]{2,1,0:T(8,128)(2,1)}), bf16[8,32,768]{2,1,0:T(8,128)(2,1)S(1)}, u32[]{:S(2)}, u32[]{:S(2)}) async-start(bf16[8,32,768]{2,1,0:T(8,128)(2,1)} %broadcast_in_dim.35), calls=%async_computation.2 | async-start | bytes 786432 | tf_op jit(solution)/shard_map/all_to_all | solution.py:347
  29.5 1.8 %reshape.147.w_ref = bf16[32,4096]{1,0:T(8,128)(2,1)} reshape(bf16[1024,128]{1,0:T(8,128)(2,1)} %param.16) | data formatting | bytes 524288 | tf_op jit(solution)/shard_map/reshape | solution.py:386
  31.3 11.0 %scale.1.s_ref.refs_6_ = bf16[768,6144]{1,0:T(8,128)(2,1)} custom-call(bf16[48,768,128]{2,1,0:T(8,128)(2,1)} %g_ref.1, f32[48,768]{1,0:T(8,128)} %fusion.r_ref), custom_call_target="tpu_custom_call" | custom-call | flops 4718592 | bytes 18874368 | tf_op jit(solution)/shard_map/scale/pallas_call | solution.py:79
  43.3 11.4 %right_sum.1 = bf16[768,512]{1,0:T(8,128)(2,1)} custom-call(bf16[16,48,32]{2,1,0:T(8,128)(2,1)} %copy.33.l_ref.refs_3_, f32[768,1]{1,0:T(8,128)} %reshape.164.mask_ref.refs_4_.refs_3_, bf16[32,4096]{1,0:T(8,128)(2,1)} %reshape.147.w_ref, bf16[768,6144]{1,0:T(8,128)(2,1)} %scale.1.s_ref.refs_6_), custom_call_target="tpu_custom_call" | custom-call | flops 4831838208 | bytes 9437184 | tf_op jit(solution)/shard_map/right_sum/pallas_call | solution.py:139
  54.7 6.1 %all-to-all-start.3 = ((bf16[16,48,256]{2,1,0:T(8,128)(2,1)}), bf16[16,48,256]{2,1,0:T(8,128)(2,1)S(1)}, u32[]{:S(2)}, u32[]{:S(2)}) async-start(bf16[16,48,256]{2,1,0:T(8,128)(2,1)} %bitcast.12), calls=%async_computation.3 | async-start | bytes 786432 | tf_op jit(solution)/shard_map/all_to_all | solution.py:352
  62.3 1.3 copy.36
  65.5 1.9 %fusion.9 = bf16[8,48,512]{2,1,0:T(8,128)(2,1)} fusion(bf16[8,48,512]{2,1,0:T(8,128)(2,1)S(1)} %collective-permute-done, bf16[8,2,48,512]{3,2,1,0:T(8,128)(2,1)} %bitcast.45, s32[]{:T(128)S(6)} %select_n.81), kind=kLoop, calls=%fused_computation.20 | loop fusion | flops 786432 | bytes 1179652 | tf_op jit(solution)/shard_map/convert_element_type | solution.py:394
  67.4 5.7 %all-to-all-done.3 = bf16[16,48,256]{2,1,0:T(8,128)(2,1)S(1)} async-done(((bf16[16,48,256]{2,1,0:T(8,128)(2,1)}), bf16[16,48,256]{2,1,0:T(8,128)(2,1)S(1)}, u32[]{:S(2)}, u32[]{:S(2)}) %all-to-all-start.3) | async-done | bytes 393248 | tf_op jit(solution)/shard_map/all_to_all | solution.py:352
  73.0 3.5 %all-to-all-start.1 = ((bf16[8,48,512]{2,1,0:T(8,128)(2,1)}), bf16[8,48,512]{2,1,0:T(8,128)(2,1)S(1)}, u32[]{:S(2)}, u32[]{:S(2)}) async-start(bf16[8,48,512]{2,1,0:T(8,128)(2,1)} %fusion.9), calls=%async_computation.1 | async-start | bytes 786432 | tf_op jit(solution)/shard_map/all_to_all | solution.py:395
  76.5 1.5 %fusion.8 = (bf16[512,512]{1,0:T(8,128)(2,1)}, bf16[512,512]{1,0:T(8,128)(2,1)}) fusion(s32[]{:T(128)S(6)} %select_n.80, s32[512]{0:T(512)S(1)} %get-tuple-element.26, s32[512]{0:T(512)S(1)} %get-tuple-element.31, s32[512]{0:T(512)S(1)} %get-tuple-element.27, s32[512]{0:T(512)S(1)} %get-tuple-element.36, s32[512]{0:T(512)S(1)} %get-tuple-element.28, ...), kind=kLoop, calls=%fused_computation.18 | loop fusion | flops 7077888 | bytes 1071620 | tf_op jit(solution)/shard_map/convert_element_type | solution.py:377
  78.8 17.6 %left_side.1 = (f32[768,32]{1,0:T(8,128)}, bf16[1024,128]{1,0:T(8,128)(2,1)}) custom-call(bf16[256,768]{1,0:T(8,128)(2,1)} %bitcast.53, bf16[256,768]{1,0:T(8,128)(2,1)} %copy-done.6, bf16[512,512]{1,0:T(8,128)(2,1)} %get-tuple-element.22.refs_2_, bf16[16,48,32]{2,1,0:T(8,128)(2,1)} %copy.33.l_ref.refs_3_, f32[768,1]{1,0:T(8,128)} %reshape.164.mask_ref.refs_4_.refs_3_, ...), custom_call_target="tpu_custom_call" | custom-call | flops 4831838208 | bytes 9437184 | tf_op jit(solution)/shard_map/left_side/pallas_call | solution.py:206
  97.2 3.5 %owner.1 = (f32[72,256]{1,0:T(8,128)}, bf16[768,64]{1,0:T(8,128)(2,1)}) custom-call(bf16[512,512]{1,0:T(8,128)(2,1)} %get-tuple-element.23.refs_0_, bf16[8,48,512]{2,1,0:T(8,128)(2,1)} %copy-done.1, f32[768,32]{1,0:T(8,128)} %get-tuple-element.14.refs_2_, f32[768,1]{1,0:T(8,128)} %reshape.164.mask_ref.refs_4_.refs_3_, f32[48,512]{1,0:T(8,128)} %copy.43.refs_4_, ...), custom_call_target="tpu_custom_call" | custom-call | tf_op jit(solution)/shard_map/owner/pallas_call | solution.py:272
  100.7 1.7 %reshape.167 = bf16[16,2,1536]{2,1,0:T(2,128)(2,1)} reshape(bf16[16,48,64]{2,1,0:T(8,128)(2,1)} %bitcast.56) | data formatting | bytes 196608
  102.4 6.0 %all-to-all-start.4 = ((bf16[16,2,1536]{2,1,0:T(2,128)(2,1)}), bf16[16,2,1536]{2,1,0:T(2,128)(2,1)S(1)}, u32[]{:S(2)}, u32[]{:S(2)}) async-start(bf16[16,2,1536]{2,1,0:T(2,128)(2,1)} %reshape.167), calls=%async_computation.4 | async-start | bytes 196608 | tf_op jit(solution)/shard_map/all_to_all | solution.py:408
  108.4 2.8 %collective-permute-start.2 = (f32[72,256]{1,0:T(8,128)}, f32[72,256]{1,0:T(8,128)S(1)}, u32[]{:S(2)}, u32[]{:S(2)}) collective-permute-start(f32[72,256]{1,0:T(8,128)} %get-tuple-element.16), channel_id=1, source_target_pairs={{0,8},{1,9},{2,10},{3,11},{4,12},{5,13},{6,14},{7,15},{8,0},{9,1},... | collective-permute-start | bytes 221192 | tf_op jit(solution)/shard_map/ppermute | solution.py:336
  111.3 6.5 %collective-permute-done.2 = f32[72,256]{1,0:T(8,128)S(1)} collective-permute-done((f32[72,256]{1,0:T(8,128)}, f32[72,256]{1,0:T(8,128)S(1)}, u32[]{:S(2)}, u32[]{:S(2)}) %collective-permute-start.2) | collective-permute-done | bytes 73760 | tf_op jit(solution)/shard_map/ppermute | solution.py:336
  118.7 4.3 %all-to-all-start.5 = ((bf16[16,64,128]{2,1,0:T(8,128)(2,1)}), bf16[16,64,128]{2,1,0:T(8,128)(2,1)S(1)}, u32[]{:S(2)}, u32[]{:S(2)}) async-start(bf16[16,64,128]{2,1,0:T(8,128)(2,1)} %bitcast.55), calls=%async_computation.5 | async-start | bytes 524288 | tf_op jit(solution)/shard_map/all_to_all | solution.py:398
  123.2 2.0 %collective-permute-start.4 = (f32[72,256]{1,0:T(8,128)S(1)}, f32[72,256]{1,0:T(8,128)S(1)}, u32[]{:S(2)}, u32[]{:S(2)}) collective-permute-start(f32[72,256]{1,0:T(8,128)S(1)} %add.130), channel_id=1, source_target_pairs={{0,2},{1,3},{2,0},{3,1},{4,6},{5,7},{6,4},{7,5},{8,10},{9,11},{10,... | collective-permute-start | bytes 221192 | tf_op jit(solution)/shard_map/ppermute | solution.py:336
  125.2 4.3 %collective-permute-done.4 = f32[72,256]{1,0:T(8,128)S(1)} collective-permute-done((f32[72,256]{1,0:T(8,128)S(1)}, f32[72,256]{1,0:T(8,128)S(1)}, u32[]{:S(2)}, u32[]{:S(2)}) %collective-permute-start.4) | collective-permute-done | bytes 73760 | tf_op jit(solution)/shard_map/ppermute | solution.py:336
  130.5 2.4 %home.1 = bf16[768,256]{1,0:T(8,128)(2,1)} custom-call(bf16[768,64]{1,0:T(8,128)(2,1)} %bitcast.43, bf16[768,256]{1,0:T(8,128)(2,1)} %bitcast.x_ref, f32[1,256]{1,0:T(1,128)} %bitcast.61, bf16[256,64]{1,0:T(8,128)(2,1)} %pad_maximum_fusion.1.refs_8_.w_ref), custom_call_target="tpu_custom_call" | custom-call | tf_op jit(solution)/shard_map/home/pallas_call | solution.py:301
  133.6 2.6 %collective-permute-start.6 = (bf16[1,64,128]{2,1,0:T(8,128)(2,1)S(1)}, bf16[1,64,128]{2,1,0:T(8,128)(2,1)S(1)}, u32[]{:S(2)}, u32[]{:S(2)}) collective-permute-start(bf16[1,64,128]{2,1,0:T(8,128)(2,1)S(1)} %bitcast.48), channel_id=1, source_target_pairs={{0,8},{1,9},{2,10},{3,11},{4,12},{5,13},{6,14},{7,15},{8,0},{9,1},... | collective-permute-start | bytes 49160 | tf_op jit(solution)/shard_map/ppermute | solution.py:336
  136.8 1.6 %collective-permute-done.6 = bf16[1,64,128]{2,1,0:T(8,128)(2,1)S(1)} collective-permute-done((bf16[1,64,128]{2,1,0:T(8,128)(2,1)S(1)}, bf16[1,64,128]{2,1,0:T(8,128)(2,1)S(1)}, u32[]{:S(2)}, u32[]{:S(2)}) %collective-permute-start.6) | collective-permute-done | bytes 16416 | tf_op jit(solution)/shard_map/ppermute | solution.py:336
  138.3 1.6 %collective-permute-start.7 = (bf16[2,64,128]{2,1,0:T(8,128)(2,1)S(1)}, bf16[2,64,128]{2,1,0:T(8,128)(2,1)S(1)}, u32[]{:S(2)}, u32[]{:S(2)}) collective-permute-start(bf16[2,64,128]{2,1,0:T(8,128)(2,1)S(1)} %pad_maximum_fusion.3), channel_id=1, source_target_pairs={{0,4},{1,5},{2,6},{3,7},{4,0},{5,1},{6,2},{7,3},{8,12},{9,13},{10,... | collective-permute-start | bytes 98312 | tf_op jit(solution)/shard_map/ppermute | solution.py:336
  139.9 2.3 %collective-permute-done.7 = bf16[2,64,128]{2,1,0:T(8,128)(2,1)S(1)} collective-permute-done((bf16[2,64,128]{2,1,0:T(8,128)(2,1)S(1)}, bf16[2,64,128]{2,1,0:T(8,128)(2,1)S(1)}, u32[]{:S(2)}, u32[]{:S(2)}) %collective-permute-start.7) | collective-permute-done | bytes 32800 | tf_op jit(solution)/shard_map/ppermute | solution.py:336
  143.6 3.0 %collective-permute-done.8 = bf16[4,64,128]{2,1,0:T(8,128)(2,1)S(1)} collective-permute-done((bf16[4,64,128]{2,1,0:T(8,128)(2,1)S(1)}, bf16[4,64,128]{2,1,0:T(8,128)(2,1)S(1)}, u32[]{:S(2)}, u32[]{:S(2)}) %collective-permute-start.8) | collective-permute-done | bytes 65568 | tf_op jit(solution)/shard_map/ppermute | solution.py:336
  146.7 1.3 collective-permute-done.9
  (77 shorter events, 20.5 us)
Async XLA Ops:
  8.9 14.2 %all-to-all-start = ((bf16[16,2,768]{2,1,0:T(2,128)(2,1)}), bf16[16,2,768]{2,1,0:T(2,128)(2,1)S(1)}, u32[]{:S(2)}, u32[]{:S(2)}) async-start(bf16[16,2,768]{2,1,0:T(2,128)(2,1)} %reshape.165), calls=%async_computation | async-start | bytes 98304 | tf_op jit(solution)/shard_map/all_to_all | solution.py:346
  24.6 30.1 %all-to-all-start.2 = ((bf16[8,32,768]{2,1,0:T(8,128)(2,1)}), bf16[8,32,768]{2,1,0:T(8,128)(2,1)S(1)}, u32[]{:S(2)}, u32[]{:S(2)}) async-start(bf16[8,32,768]{2,1,0:T(8,128)(2,1)} %broadcast_in_dim.35), calls=%async_computation.2 | async-start | bytes 786432 | tf_op jit(solution)/shard_map/all_to_all | solution.py:347
  43.3 19.1 %copy-start.2 = (bf16[32,4096]{1,0:T(8,128)(2,1)S(1)}, bf16[32,4096]{1,0:T(8,128)(2,1)}, u32[]{:S(2)}) copy-start(bf16[32,4096]{1,0:T(8,128)(2,1)} %reshape.147.w_ref) | copy-start | bytes 786436
  43.3 20.5 %copy-start.5 = (bf16[256,32]{0,1:T(8,128)(2,1)S(1)}, bf16[256,32]{0,1:T(8,128)(2,1)}, u32[]{:S(2)}) copy-start(bf16[256,32]{0,1:T(8,128)(2,1)} %param.15) | copy-start | bytes 49156
  43.3 21.4 %copy-start.3 = (bf16[256,32]{1,0:T(8,128)(2,1)S(1)}, bf16[256,32]{1,0:T(8,128)(2,1)}, u32[]{:S(2)}) copy-start(bf16[256,32]{1,0:T(8,128)(2,1)} %copy.31.lw_ref) | copy-start | bytes 49156
  54.7 23.3 %copy-start.4 = (bf16[8,32,768]{2,1,0:T(8,128)(2,1)}, bf16[8,32,768]{2,1,0:T(8,128)(2,1)S(1)}, u32[]{:S(2)}) copy-start(bf16[8,32,768]{2,1,0:T(8,128)(2,1)S(1)} %all-to-all-done.2) | copy-start | bytes 1179652
  54.7 18.3 %all-to-all-start.3 = ((bf16[16,48,256]{2,1,0:T(8,128)(2,1)}), bf16[16,48,256]{2,1,0:T(8,128)(2,1)S(1)}, u32[]{:S(2)}, u32[]{:S(2)}) async-start(bf16[16,48,256]{2,1,0:T(8,128)(2,1)} %bitcast.12), calls=%async_computation.3 | async-start | bytes 786432 | tf_op jit(solution)/shard_map/all_to_all | solution.py:352
  61.8 3.6 %collective-permute-start = (bf16[8,48,512]{2,1,0:T(8,128)(2,1)S(1)}, bf16[8,48,512]{2,1,0:T(8,128)(2,1)S(1)}, u32[]{:S(2)}, u32[]{:S(2)}) collective-permute-start(bf16[8,48,512]{2,1,0:T(8,128)(2,1)S(1)} %dynamic-slice_bitcast_fusion), channel_id=1, source_target_pairs={{0,1},{1,0},{2,3},{3,2},{4,5},{5,4},{6,7},{7,6},{8,9},{9,8},{10,11... | collective-permute-start | bytes 1179656 | tf_op jit(solution)/shard_map/ppermute | solution.py:336
  65.4 12.7 %collective-permute-start.1 = (bf16[256,768]{1,0:T(8,128)(2,1)S(1)}, bf16[256,768]{1,0:T(8,128)(2,1)S(1)}, u32[]{:S(2)}, u32[]{:S(2)}) collective-permute-start(bf16[256,768]{1,0:T(8,128)(2,1)S(1)} %bitcast.52), channel_id=1, source_target_pairs={{0,1},{1,0},{2,3},{3,2},{4,5},{5,4},{6,7},{7,6},{8,9},{9,8},{10,11... | collective-permute-start | bytes 1179656 | tf_op jit(solution)/shard_map/ppermute | solution.py:336
  73.0 23.4 %copy-start = (bf16[16,48,256]{2,1,0:T(8,128)(2,1)}, bf16[16,48,256]{2,1,0:T(8,128)(2,1)S(1)}, u32[]{:S(2)}) copy-start(bf16[16,48,256]{2,1,0:T(8,128)(2,1)S(1)} %all-to-all-done.3) | copy-start | bytes 1179652
  73.0 23.4 %all-to-all-start.1 = ((bf16[8,48,512]{2,1,0:T(8,128)(2,1)}), bf16[8,48,512]{2,1,0:T(8,128)(2,1)S(1)}, u32[]{:S(2)}, u32[]{:S(2)}) async-start(bf16[8,48,512]{2,1,0:T(8,128)(2,1)} %fusion.9), calls=%async_computation.1 | async-start | bytes 786432 | tf_op jit(solution)/shard_map/all_to_all | solution.py:395
  78.0 0.8 copy-start.6
  96.4 0.7 copy-start.1
  102.4 16.3 %all-to-all-start.4 = ((bf16[16,2,1536]{2,1,0:T(2,128)(2,1)}), bf16[16,2,1536]{2,1,0:T(2,128)(2,1)S(1)}, u32[]{:S(2)}, u32[]{:S(2)}) async-start(bf16[16,2,1536]{2,1,0:T(2,128)(2,1)} %reshape.167), calls=%async_computation.4 | async-start | bytes 196608 | tf_op jit(solution)/shard_map/all_to_all | solution.py:408
  108.4 9.3 %collective-permute-start.2 = (f32[72,256]{1,0:T(8,128)}, f32[72,256]{1,0:T(8,128)S(1)}, u32[]{:S(2)}, u32[]{:S(2)}) collective-permute-start(f32[72,256]{1,0:T(8,128)} %get-tuple-element.16), channel_id=1, source_target_pairs={{0,8},{1,9},{2,10},{3,11},{4,12},{5,13},{6,14},{7,15},{8,0},{9,1},... | collective-permute-start | bytes 221192 | tf_op jit(solution)/shard_map/ppermute | solution.py:336
  118.6 4.6 %collective-permute-start.3 = (f32[72,256]{1,0:T(8,128)S(1)}, f32[72,256]{1,0:T(8,128)S(1)}, u32[]{:S(2)}, u32[]{:S(2)}) collective-permute-start(f32[72,256]{1,0:T(8,128)S(1)} %add.129), channel_id=1, source_target_pairs={{0,4},{1,5},{2,6},{3,7},{4,0},{5,1},{6,2},{7,3},{8,12},{9,13},{10,... | collective-permute-start | bytes 221192 | tf_op jit(solution)/shard_map/ppermute | solution.py:336
  118.7 14.9 %all-to-all-start.5 = ((bf16[16,64,128]{2,1,0:T(8,128)(2,1)}), bf16[16,64,128]{2,1,0:T(8,128)(2,1)S(1)}, u32[]{:S(2)}, u32[]{:S(2)}) async-start(bf16[16,64,128]{2,1,0:T(8,128)(2,1)} %bitcast.55), calls=%async_computation.5 | async-start | bytes 524288 | tf_op jit(solution)/shard_map/all_to_all | solution.py:398
  123.2 6.3 %collective-permute-start.4 = (f32[72,256]{1,0:T(8,128)S(1)}, f32[72,256]{1,0:T(8,128)S(1)}, u32[]{:S(2)}, u32[]{:S(2)}) collective-permute-start(f32[72,256]{1,0:T(8,128)S(1)} %add.130), channel_id=1, source_target_pairs={{0,2},{1,3},{2,0},{3,1},{4,6},{5,7},{6,4},{7,5},{8,10},{9,11},{10,... | collective-permute-start | bytes 221192 | tf_op jit(solution)/shard_map/ppermute | solution.py:336
  129.5 3.4 %collective-permute-start.5 = (f32[72,256]{1,0:T(8,128)S(1)}, f32[72,256]{1,0:T(8,128)S(1)}, u32[]{:S(2)}, u32[]{:S(2)}) collective-permute-start(f32[72,256]{1,0:T(8,128)S(1)} %add.131), channel_id=1, source_target_pairs={{0,1},{1,0},{2,3},{3,2},{4,5},{5,4},{6,7},{7,6},{8,9},{9,8},{10,11... | collective-permute-start | bytes 221192 | tf_op jit(solution)/shard_map/ppermute | solution.py:336
  133.6 4.7 %collective-permute-start.6 = (bf16[1,64,128]{2,1,0:T(8,128)(2,1)S(1)}, bf16[1,64,128]{2,1,0:T(8,128)(2,1)S(1)}, u32[]{:S(2)}, u32[]{:S(2)}) collective-permute-start(bf16[1,64,128]{2,1,0:T(8,128)(2,1)S(1)} %bitcast.48), channel_id=1, source_target_pairs={{0,8},{1,9},{2,10},{3,11},{4,12},{5,13},{6,14},{7,15},{8,0},{9,1},... | collective-permute-start | bytes 49160 | tf_op jit(solution)/shard_map/ppermute | solution.py:336
  138.3 3.9 %collective-permute-start.7 = (bf16[2,64,128]{2,1,0:T(8,128)(2,1)S(1)}, bf16[2,64,128]{2,1,0:T(8,128)(2,1)S(1)}, u32[]{:S(2)}, u32[]{:S(2)}) collective-permute-start(bf16[2,64,128]{2,1,0:T(8,128)(2,1)S(1)} %pad_maximum_fusion.3), channel_id=1, source_target_pairs={{0,4},{1,5},{2,6},{3,7},{4,0},{5,1},{6,2},{7,3},{8,12},{9,13},{10,... | collective-permute-start | bytes 98312 | tf_op jit(solution)/shard_map/ppermute | solution.py:336
  142.3 4.3 %collective-permute-start.8 = (bf16[4,64,128]{2,1,0:T(8,128)(2,1)S(1)}, bf16[4,64,128]{2,1,0:T(8,128)(2,1)S(1)}, u32[]{:S(2)}, u32[]{:S(2)}) collective-permute-start(bf16[4,64,128]{2,1,0:T(8,128)(2,1)S(1)} %pad_maximum_fusion.2), channel_id=1, source_target_pairs={{0,2},{1,3},{2,0},{3,1},{4,6},{5,7},{6,4},{7,5},{8,10},{9,11},{10,... | collective-permute-start | bytes 196616 | tf_op jit(solution)/shard_map/ppermute | solution.py:336
  146.6 1.4 collective-permute-start.9

commit v2 on v0

v2 whole, which is shorter than its diff:
```python
import functools

import jax
import jax.numpy as jnp
from jax import lax
from jax.experimental import pallas as pl
from jax.experimental.pallas import tpu as pltpu
from jax.sharding import PartitionSpec as P

CHAINS = 4
EPSILON = 1e-05
AXIS = "dap"
F32 = jnp.float32
BF16 = jnp.bfloat16
LANES = 128
MIB = 1024 * 1024
VMEM = pl.BlockSpec(memory_space=pltpu.VMEM)


def mm(a, b, dims=(1, 0)):
    return lax.dot_general(
        a, b, (((dims[0],), (dims[1],)), ((), ())), preferred_element_type=F32
    )


def in_hbm(value):
    return pltpu.with_memory_space_constraint(value, pltpu.HBM)


def params(mib):
    return pltpu.CompilerParams(vmem_limit_bytes=mib * MIB)


def whole(*shape):
    return pl.BlockSpec(shape, lambda *_: (0,) * len(shape))


def sds(shape, dtype):
    return jax.ShapeDtypeStruct(shape, dtype)


def up(n, to=16):
    return -(-n // to) * to


class Sizes:
    def __init__(self, size, res, cols, pair, width, features, seqs):
        self.size, self.res, self.cols, self.pair = size, res, cols, pair
        self.width, self.features, self.seqs = width, features, seqs
        self.chips = size // 2
        self.planes = cols // LANES
        self.wide = width * seqs
        self.groups = max(g for g in (4, 3, 2, 1) if g == 1 or res % (16 * g) == 0)
        self.rows = res // self.groups
        self.slots = up(self.rows)
        self.piece = width * width // size
        self.piece_slots = up(self.piece)
        self.sum_rows = up(2 * width + 2, 8) * features // LANES
        self.block = max(b for b in range(1, 9) if res % b == 0)
        blocks = res // self.block
        self.pieces = max(n for n in (3, 2, 1) if blocks % n == 0)
        self.per_piece = blocks // self.pieces
        self.mib = 28 if self.wide <= 1024 else 56
        bits = size.bit_length() - 1
        self.masks = [size >> (b + 1) for b in range(bits)]

    def origin(self, p):
        return sum(m * ((p >> b) & 1) for b, m in enumerate(self.masks))


def normalise(x):
    center = x - jnp.mean(x, axis=-1, keepdims=True)
    inverse = lax.rsqrt(jnp.mean(center * center, axis=-1, keepdims=True) + EPSILON)
    return center * inverse, inverse


def project_kernel(z, x_ref, gain_ref, bias_ref, lwt_ref, rwt_ref,
                   left_ref, right_ref, unit_ref, inverse_ref):
    unit, inverse = normalise(x_ref[...].astype(F32))
    normed = (unit * gain_ref[...] + bias_ref[...]).astype(BF16)
    right_ref[...] = mm(rwt_ref[...], normed, (1, 1)).astype(BF16)
    left = mm(normed, lwt_ref[...], (1, 1))
    for d in range(z.size):
        parts = [
            left[d * z.res + g * z.rows : d * z.res + (g + 1) * z.rows] for g in range(z.groups)
        ]
        parts.append(jnp.zeros((z.rows, LANES - z.groups * z.width), F32))
        packed = jnp.concatenate(parts, axis=1)
        if z.slots > z.rows:
            packed = jnp.concatenate([packed, jnp.zeros((z.slots - z.rows, LANES), F32)], axis=0)
        left_ref[d] = packed.astype(BF16)
    unit_ref[...] = unit
    inverse_ref[...] = inverse


def project(z, x, gain, bias, lwt, rwt):
    return pl.pallas_call(
        functools.partial(project_kernel, z),
        out_shape=(
            sds((z.size, z.slots, LANES), BF16),
            sds((z.width, z.cols), BF16),
            sds((z.cols, z.features), F32),
            sds((z.cols, 1), F32),
        ),
        in_specs=[VMEM] * 5,
        out_specs=(VMEM,) * 4,
        compiler_params=params(16),
        name="project",
    )(x, gain, bias, lwt, rwt)


def cover_kernel(z, smask_ref, schain_ref, code_ref, w_ref, cover_ref, own_ref, mine_ref, mix_ref,
                 rows):
    me = lax.axis_index(AXIS)
    code = code_ref[...]
    real = (code >= 8).astype(F32)
    chain = code % 8

    def covered(s):
        same = jnp.logical_or(schain_ref[s] == CHAINS, chain == schain_ref[s])
        return jnp.where(same, real * smask_ref[s].astype(F32), 0.0)

    for s in range(z.seqs):
        cover_ref[s : s + 1, :] = covered(s)
    mine_ref[...] = covered(me)
    turned = pltpu.roll(cover_ref[...], z.cols - me * z.res, 1)
    own_ref[...] = jnp.transpose(turned[:, :LANES])[: z.res, :]
    rows[...] = w_ref[...].astype(F32)
    for e in range(z.width):
        part = rows[pl.ds(e, z.width, stride=z.width), :]
        mix_ref[:, e * z.pair : (e + 1) * z.pair] = part.astype(BF16)


def cover_all(z, smask, schain, code, weight):
    smem = pl.BlockSpec(memory_space=pltpu.SMEM)
    return pl.pallas_call(
        functools.partial(cover_kernel, z),
        out_shape=(
            sds((z.seqs, z.cols), F32),
            sds((z.res, z.seqs), F32),
            sds((1, z.cols), F32),
            sds((z.width, z.width * z.pair), BF16),
        ),
        in_specs=[smem, smem, VMEM, VMEM],
        out_specs=(VMEM,) * 4,
        scratch_shapes=[pltpu.VMEM(weight.shape, F32)],
        compiler_params=params(8),
        name="cover",
    )(smask, schain, code, in_hbm(weight))


def scale_kernel(z, g_ref, own_ref, cover_ref, out_ref):
    block, pair = z.block, z.pair
    count = mm(own_ref[0].astype(BF16), cover_ref[...].astype(BF16))
    factor = 1.0 / jnp.maximum(count, 1.0)
    high = factor.astype(BF16)
    low = (factor - high.astype(F32)).astype(BF16)
    shape = (block, block * pair)
    pick = (
        lax.broadcasted_iota(jnp.int32, shape, 0)
        == lax.broadcasted_iota(jnp.int32, shape, 1) // pair
    ).astype(F32).astype(BF16)
    spread = mm(high, pick, (0, 0)) + mm(low, pick, (0, 0))
    for b in range(block):
        at = slice(b * pair, (b + 1) * pair)
        out_ref[:, at] = (g_ref[b].astype(F32) * spread[:, at]).astype(BF16)


def scale(z, gradient, own, cover, piece):
    steps = z.per_piece
    size = gradient.size // z.pieces
    return pl.pallas_call(
        functools.partial(scale_kernel, z),
        grid=(steps,),
        out_shape=pltpu.HBM((z.cols, steps * z.block * z.pair), BF16),
        in_specs=[
            pl.BlockSpec((z.block, z.cols, z.pair), lambda b: (piece * steps + b, 0, 0)),
            pl.BlockSpec((1, z.block, z.seqs), lambda b: (piece * steps + b, 0, 0)),
            whole(*cover.shape),
        ],
        out_specs=pl.BlockSpec((z.cols, z.block * z.pair), lambda b: (0, b)),
        compiler_params=params(20),
        cost_estimate=pl.CostEstimate(flops=size, bytes_accessed=4 * size, transcendentals=0),
        name="scale",
    )(in_hbm(gradient), own.reshape(z.res // z.block, z.block, z.seqs), cover)


def order_left(z, l_ref, own_ref, scratch):
    for s in range(z.seqs):
        got = l_ref[s].astype(F32)
        for g in range(z.groups):
            at = slice(g * z.rows, (g + 1) * z.rows)
            part = got[: z.rows, g * z.width : (g + 1) * z.width] * own_ref[at, s : s + 1]
            scratch[pl.ds(g * z.rows * z.seqs + s, z.rows, stride=z.seqs), :] = part


def scaled_copy(z, s_refs, here, arrived, piece, step):
    size = z.block * z.pair
    at = piece * z.per_piece + step
    source = pl.ds(pl.multiple_of(step * size, size), size)
    span = pl.ds(pl.multiple_of(at * size, size), size)
    return pltpu.make_async_copy(s_refs[piece].at[:, source], here.at[:, span], arrived.at[at]), span


def fetch_scaled(z, s_refs, here, arrived):
    for piece in range(z.pieces):
        for step in range(z.per_piece):
            scaled_copy(z, s_refs, here, arrived, piece, step)[0].start()


def over_scaled(z, s_refs, here, arrived, body):
    for piece in range(z.pieces):

        @pl.loop(0, z.per_piece)
        def _(step):
            copy, span = scaled_copy(z, s_refs, here, arrived, piece, step)
            copy.wait()
            body(piece * z.per_piece + step, span)


def right_sum_kernel(z, l_ref, own_ref, w_ref, *refs):
    s_refs = refs[: z.pieces]
    keep_ref, give_ref, ordered, mixed, total, here, arrived = refs[z.pieces :]
    core = lax.axis_index(AXIS) % 2
    seqs, pair = z.seqs, z.pair
    fetch_scaled(z, s_refs, here, arrived)
    order_left(z, l_ref, own_ref, ordered)
    left = ordered[...].astype(BF16)
    group = 8
    for first in range(0, z.width, group):
        part = mm(left, w_ref[:, first * pair : (first + group) * pair]).astype(BF16)
        for e in range(group):
            for i in range(z.res):
                mixed[(first + e) * seqs : (first + e + 1) * seqs, i * pair : (i + 1) * pair] = part[
                    i * seqs : (i + 1) * seqs, e * pair : (e + 1) * pair
                ]

    total[...] = jnp.zeros_like(total)

    def add(_, span):
        product = mm(mixed[:, span], here[:, span], (1, 1))
        for c in range(z.planes):
            total[c] += product[:, c * LANES : (c + 1) * LANES]

    over_scaled(z, s_refs, here, arrived, add)
    for chip in range(z.chips):
        for ref, parity in ((keep_ref, core), (give_ref, 1 - core)):
            at = pl.ds(2 * chip + parity, z.width, stride=seqs)
            for c in range(z.planes):
                ref[chip, :, c * LANES : (c + 1) * LANES] = total[c, at, :].astype(BF16)


def right_sum(z, left, own, weight, scaled):
    out = (z.chips, z.width, z.cols)
    return pl.pallas_call(
        functools.partial(right_sum_kernel, z),
        out_shape=(sds(out, BF16), sds(out, BF16)),
        in_specs=[VMEM] * 3 + [pl.BlockSpec(memory_space=pltpu.HBM)] * z.pieces,
        out_specs=(VMEM, VMEM),
        scratch_shapes=[
            pltpu.VMEM((z.res * z.seqs, z.width), F32),
            pltpu.VMEM((z.wide, z.res * z.pair), BF16),
            pltpu.VMEM((z.planes, z.wide, LANES), F32),
            pltpu.VMEM((z.cols, z.res * z.pair), BF16),
            pltpu.SemaphoreType.DMA((z.res // z.block,)),
        ],
        compiler_params=params(z.mib),
        cost_estimate=pl.CostEstimate(
            flops=2 * z.wide * z.cols * z.res * z.pair, bytes_accessed=0, transcendentals=0
        ),
        name="right_sum",
    )(left, own, weight, *[in_hbm(piece) for piece in scaled])


def left_side_kernel(z, here_ref, there_ref, cover_ref, l_ref, own_ref, w_ref, *refs):
    s_refs = refs[: z.pieces]
    out_ref, ordered, right, proj, back, wide_rows, here, arrived = refs[z.pieces :]
    me = lax.axis_index(AXIS)
    seqs, pair, block, width = z.seqs, z.pair, z.block, z.width
    fetch_scaled(z, s_refs, here, arrived)
    order_left(z, l_ref, own_ref, ordered)
    for side, ref in ((0, here_ref), (z.size // 2, there_ref)):

        @pl.loop(0, z.size // 2)
        def _(p):
            at = pl.ds(me ^ z.origin(p + side), width, stride=seqs)
            for c in range(z.planes):
                wide_rows[c, at, :] = ref[p, :, c * LANES : (c + 1) * LANES].astype(F32)

    for e in range(width):
        at = slice(e * seqs, (e + 1) * seqs)
        for c in range(z.planes):
            lanes = slice(c * LANES, (c + 1) * LANES)
            right[at, lanes] = (wide_rows[c, at, :] * cover_ref[:, lanes]).astype(BF16)

    def project_block(step, span):
        group = width // 4
        for first in range(0, width, group):
            part = mm(right[first * seqs : (first + group) * seqs, :], here[:, span])
            part = part.astype(BF16)
            for i in range(block):
                at = pl.ds(pl.multiple_of((step * block + i) * seqs, seqs), seqs)
                for e in range(group):
                    proj[at, (first + e) * pair : (first + e + 1) * pair] = part[
                        e * seqs : (e + 1) * seqs, i * pair : (i + 1) * pair
                    ]

    over_scaled(z, s_refs, here, arrived, project_block)
    back[...] = mm(proj[...], w_ref[...], (1, 1))
    spread = wide_rows.at[0]
    left = ordered[...].astype(BF16)
    for first in range(0, width, 8):
        total = mm(left, proj[:, first * pair : (first + 8) * pair], (0, 0))
        for e in range(8):
            spread[pl.ds(first + e, width, stride=width), :] = total[:, e * pair : (e + 1) * pair]
    for d in range(z.size):
        got = spread[d * z.piece : (d + 1) * z.piece, :]
        if z.piece_slots > z.piece:
            got = jnp.concatenate([got, jnp.zeros((z.piece_slots - z.piece, pair), F32)], axis=0)
        out_ref[d, : z.piece_slots] = got.astype(BF16)
        parts = [
            back[pl.ds(g * z.rows * seqs + d, z.rows, stride=seqs), :] for g in range(z.groups)
        ]
        parts.append(jnp.zeros((z.rows, LANES - z.groups * width), F32))
        packed = jnp.concatenate(parts, axis=1)
        if z.slots > z.rows:
            packed = jnp.concatenate([packed, jnp.zeros((z.slots - z.rows, LANES), F32)], axis=0)
        out_ref[d, z.piece_slots :] = packed.astype(BF16)


def left_side(z, here, there, cover, left, own, weight, scaled):
    return pl.pallas_call(
        functools.partial(left_side_kernel, z),
        out_shape=sds((z.size, z.piece_slots + z.slots, LANES), BF16),
        in_specs=[VMEM] * 6 + [pl.BlockSpec(memory_space=pltpu.HBM)] * z.pieces,
        out_specs=VMEM,
        scratch_shapes=[
            pltpu.VMEM((z.res * z.seqs, z.width), F32),
            pltpu.VMEM((z.wide, z.cols), BF16),
            pltpu.VMEM((z.res * z.seqs, z.width * z.pair), BF16),
            pltpu.VMEM((z.res * z.seqs, z.width), F32),
            pltpu.VMEM((z.planes, max(z.wide, z.width * z.width), LANES), F32),
            pltpu.VMEM((z.cols, z.res * z.pair), BF16),
            pltpu.SemaphoreType.DMA((z.res // z.block,)),
        ],
        compiler_params=params(z.mib),
        cost_estimate=pl.CostEstimate(
            flops=2 * z.wide * z.cols * z.res * z.pair, bytes_accessed=0, transcendentals=0
        ),
        name="left_side",
    )(here, there, cover, left, own, weight, *[in_hbm(piece) for piece in scaled])


def owner_kernel(z, parts_ref, got_ref, cover_ref, unit_ref, gain_ref, bias_ref, lwt_ref, rwt_ref,
                 sums_ref, grad_ref, rows):
    width = z.width
    cover = cover_ref[...]
    right = parts_ref[0].astype(F32)
    for p in range(1, z.chips):
        right = right + parts_ref[p].astype(F32)
    right = (right * cover).astype(BF16)
    piece = got_ref[0, : z.piece_slots].astype(F32)
    for d in range(1, z.size):
        piece = piece + got_ref[d, : z.piece_slots].astype(F32)
    for d in range(z.size):
        got = got_ref[d, z.piece_slots :].astype(F32)
        for g in range(z.groups):
            first = d * z.res + g * z.rows
            rows[first : first + z.rows, :] = got[: z.rows, g * width : (g + 1) * width]
    column = jnp.transpose(jnp.broadcast_to(cover, (8, z.cols)))[:, :1]
    left = (rows[...] * column).astype(BF16)
    unit = unit_ref[...]
    normed = (unit * gain_ref[...] + bias_ref[...]).astype(BF16)
    grad = mm(left, lwt_ref[...]) + mm(right, rwt_ref[...], (0, 0))
    grad_ref[...] = grad
    pad = up(2 * width + 2, 8) - 2 * width - 2
    sums = jnp.concatenate(
        [
            mm(left, normed, (0, 0)),
            mm(right, normed),
            jnp.sum(grad * unit, axis=0, keepdims=True),
            jnp.sum(grad, axis=0, keepdims=True),
            jnp.zeros((pad, z.features), F32),
        ],
        axis=0,
    )
    half = sums.shape[0]
    for part in range(z.features // LANES):
        sums_ref[part * half : (part + 1) * half, :] = sums[
            :, part * LANES : (part + 1) * LANES
        ].astype(BF16)
    sums_ref[z.sum_rows :, :] = piece.astype(BF16)


def owner(z, parts, got, cover, unit, gain, bias, lwt, rwt):
    return pl.pallas_call(
        functools.partial(owner_kernel, z),
        out_shape=(
            sds((z.sum_rows + z.piece_slots, LANES), BF16),
            sds((z.cols, z.features), F32),
        ),
        in_specs=[VMEM] * 8,
        out_specs=(VMEM, VMEM),
        scratch_shapes=[pltpu.VMEM((z.cols, z.width), F32)],
        compiler_params=params(24),
        name="owner",
    )(parts, got, cover, unit, gain, bias, lwt, rwt)


def stack_kernel(here_ref, there_ref, out_ref):
    half = here_ref.shape[0]
    out_ref[:half] = here_ref[...]
    out_ref[half:] = there_ref[...]


def stack(here, there):
    return pl.pallas_call(
        stack_kernel,
        out_shape=sds((2 * here.shape[0],) + here.shape[1:], here.dtype),
        in_specs=[VMEM, VMEM],
        out_specs=VMEM,
        compiler_params=params(16),
        name="stack",
    )(here, there)


def pair_sum_kernel(here_ref, there_ref, out_ref):
    for p in range(here_ref.shape[0]):
        out_ref[p] = (here_ref[p].astype(F32) + there_ref[p].astype(F32)).astype(BF16)


def pair_sum(here, there):
    return pl.pallas_call(
        pair_sum_kernel,
        out_shape=sds(here.shape, BF16),
        in_specs=[VMEM, VMEM],
        out_specs=VMEM,
        compiler_params=params(24),
        name="pair_sum",
    )(here, there)


def join_kernel(z, here_ref, there_ref, out_ref):
    top, more = z.sum_rows, here_ref.shape[0] - z.sum_rows
    out_ref[:top, :] = (here_ref[:top, :].astype(F32) + there_ref[:top, :].astype(F32)).astype(BF16)
    out_ref[top : top + more, :] = here_ref[top:, :]
    out_ref[top + more :, :] = there_ref[top:, :]


def join(z, here, there):
    rows = 2 * here.shape[0] - z.sum_rows
    return pl.pallas_call(
        functools.partial(join_kernel, z),
        out_shape=sds((rows, LANES), BF16),
        in_specs=[VMEM, VMEM],
        out_specs=VMEM,
        compiler_params=params(8),
        name="join",
    )(here, there)


def finish_kernel(z, here_ref, there_ref, lw_ref, rw_ref, gain_ref, bias_ref, out_ref):
    me = lax.axis_index(AXIS)
    top, width = z.sum_rows, z.width
    sums = here_ref[:top, :].astype(F32) + there_ref[:top, :].astype(F32)
    half = top // (z.features // LANES)
    for part in range(z.features // LANES):
        at = slice(part * LANES, (part + 1) * LANES)
        lw_ref[:, at] = sums[part * half : part * half + width]
        rw_ref[:, at] = sums[part * half + width : part * half + 2 * width]
        gain_ref[:, at] = sums[part * half + 2 * width : part * half + 2 * width + 1]
        bias_ref[:, at] = sums[part * half + 2 * width + 1 : part * half + 2 * width + 2]
    for p in range(z.size):
        ref = here_ref if p < z.size // 2 else there_ref
        first = top + (p % (z.size // 2)) * z.piece_slots
        at = pl.ds(pl.multiple_of((me ^ z.origin(p)) * z.piece, z.piece), z.piece)
        out_ref[at, :] = ref[first : first + z.piece_slots, :].astype(F32)[: z.piece]


def finish(z, here, there):
    return pl.pallas_call(
        functools.partial(finish_kernel, z),
        out_shape=(
            sds((z.width, z.features), F32),
            sds((z.width, z.features), F32),
            sds((1, z.features), F32),
            sds((1, z.features), F32),
            sds((z.width * z.width, z.pair), F32),
        ),
        in_specs=[VMEM, VMEM],
        out_specs=(VMEM,) * 5,
        compiler_params=params(8),
        name="finish",
    )(here, there)


def home_kernel(grad_ref, unit_ref, inverse_ref, gain_ref, out_ref):
    unit = unit_ref[...]
    d = grad_ref[...] * gain_ref[...]
    out_ref[...] = (
        inverse_ref[...]
        * (
            d
            - jnp.mean(d, axis=-1, keepdims=True)
            - unit * jnp.mean(d * unit, axis=-1, keepdims=True)
        )
    ).astype(BF16)


def home(z, grad, unit, inverse, gain):
    return pl.pallas_call(
        home_kernel,
        out_shape=sds(unit.shape, BF16),
        in_specs=[VMEM] * 4,
        out_specs=VMEM,
        compiler_params=params(16),
        name="home",
    )(grad, unit, inverse, gain)


def on_device(
    size,
    alignment_rows,
    norm_gain_vector,
    norm_bias_vector,
    left_weight,
    right_weight,
    output_weight,
    pair_output_gradient,
    sequence_real_mask,
    sequence_chain_index,
    residue_real_mask,
    residue_chain_index,
):
    me = lax.axis_index(AXIS)
    res, cols, pair = pair_output_gradient.shape
    features, width = left_weight.shape
    seqs = sequence_real_mask.shape[0]
    z = Sizes(size, res, cols, pair, width, features, seqs)
    same_core = [[d for d in range(size) if d % 2 == c] for c in (0, 1)]

    def swap_with(value, bit):
        return lax.ppermute(value, AXIS, [(d, d ^ bit) for d in range(size)])

    x = alignment_rows.reshape(cols, features)
    gain = norm_gain_vector.reshape(1, features)
    bias = norm_bias_vector.reshape(1, features)
    lwt, rwt = left_weight.T, right_weight.T
    left, right, unit, inverse = project(
        z, in_hbm(x), in_hbm(gain), in_hbm(bias), in_hbm(lwt), in_hbm(rwt)
    )
    left_all = lax.all_to_all(left, AXIS, 0, 0, tiled=True)

    code = (residue_chain_index + 8 * residue_real_mask).reshape(1, cols)
    coverage, own_residues, own_sequence, w_mix = cover_all(
        z, sequence_real_mask, sequence_chain_index, code, output_weight
    )

    here = right[None]
    scaled = []
    for step in range(max(len(z.masks) - 1, z.pieces)):
        there = swap_with(here, z.masks[step]) if step < len(z.masks) - 1 else None
        if step < z.pieces:
            gradient, here = lax.optimization_barrier((pair_output_gradient, here))
            scaled.append(scale(z, gradient, own_residues, coverage, step))
        if there is not None:
            there, scaled[-1] = lax.optimization_barrier((there, scaled[-1]))
            here = stack(here, there)
    left_all, here = lax.optimization_barrier((left_all, here))
    keep, give = right_sum(z, left_all, own_residues, w_mix, scaled)
    there = swap_with(here, z.masks[-1])
    of_chip = pair_sum(keep, swap_with(give, 1))
    of_chip, here = lax.optimization_barrier((of_chip, here))
    parts = lax.all_to_all(of_chip, AXIS, 0, 0, tiled=True, axis_index_groups=same_core)

    shares = left_side(z, here, there, coverage, left_all, own_residues, w_mix, scaled)
    shares, parts = lax.optimization_barrier((shares, parts))
    got = lax.all_to_all(shares, AXIS, 0, 0, tiled=True)

    sums, grad = owner(z, parts, got, own_sequence, unit, gain, bias, lwt, rwt)
    alignment_gradient = home(z, grad, unit, inverse, gain)
    there = swap_with(sums, z.masks[0])
    there, alignment_gradient = lax.optimization_barrier((there, alignment_gradient))
    sums = join(z, sums, there)
    for bit in z.masks[1:-1]:
        sums = join(z, sums, swap_with(sums, bit))
    lw_grad, rw_grad, gain_grad, bias_grad, out_grad = finish(z, sums, swap_with(sums, z.masks[-1]))
    return (
        alignment_gradient.reshape(alignment_rows.shape),
        gain_grad.reshape(features),
        bias_grad.reshape(features),
        lw_grad.T,
        rw_grad.T,
        out_grad,
    )


def solution(mesh):
    rows = P(("grp", "dap"), None, None)
    in_specs = (rows, P(), P(), P(), P(), P(), rows, P("grp"), P("grp"), P("grp"), P("grp"))
    out_specs = (rows, P("grp"), P("grp"), P("grp", None), P("grp", None), P("grp", None))
    return jax.shard_map(
        functools.partial(on_device, mesh.shape[AXIS]),
        mesh=mesh,
        in_specs=in_specs,
        out_specs=out_specs,
        check_vma=False,
    )
```

time: 570 us -> 96.7 us (0.17); the launches traced: 560 us -> 96.3 us
  waiting for transfers between devices: 203 us -> 16.6 us
  matrix products: 169 us -> 0 us
  local copies, waits for them, and re-layouts: 125 us -> 1.34 us
  Pallas kernels: 0 us -> 42.8 us
  between operations: 14.3 us -> 0.77 us
  other arithmetic: 10.5 us -> 0.71 us
  blocking collectives: 24 us -> 16.4 us
    dot_general x12 -> x0, matrix products: 169 us -> none  [the longest x1 115 us: on_device(): jnp.einsum('sci,ijce->jes', left_cols, expanded, preferred_element_type=j...]
    psum x2 -> x0, waiting for transfers between devices: 166 us -> none  [on_device(): lax.psum((left_weight_gradient, right_weight_gradient, out_acc.reshape(pr...]
    convert_element_type x10 -> x0, local copies, waits for them, and re-layouts: 98 us -> none  [the longest x1 96.6 us: expand_pairs(): product.astype(jnp.bfloat16)]
    pallas_call x0 -> x17, Pallas kernels: none -> 42.8 us  [the longest x3 14.8 us: scale(): pl.pallas_call(functools.partial(scale_kernel, z), grid=(steps,), out_sha...]
    unnamed x4 -> x0, waiting for transfers between devices: 29.6 us -> none
    all_gather x1 -> x0, blocking collectives: 24 us -> none  [on_device(): lax.all_gather(right, 'dap', axis=0, tiled=True)]
    unnamed x28 -> x12, local copies, waits for them, and re-layouts: 25.3 us -> 1.33 us
    all_to_all x0 -> x1, blocking collectives: none -> 16.4 us  [on_device(): got = lax.all_to_all(shares, AXIS, 0, 0, tiled=True)]
  transfers between devices with their start and end apart: 6 -> 11, of which waited for: 5 -> 7; matrix products, arithmetic and copies ran while one was open for 28% -> 1% of each run, Pallas kernels for 0% -> 31%
where the time goes in v2:
time: 96.7 us; the launch traced here: 96.3 us
  Pallas kernels  42.8 us (44%)
  starting transfers between devices  17.6 us (18%)
  waiting for transfers between devices  16.6 us (17%)
  blocking collectives  16.4 us (17%)
  local copies, waits for them, and re-layouts  1.34 us (1%)
    all_to_all x1, blocking collectives, on_device(): got = lax.all_to_all(shares, AXIS, 0, 0, tiled=True)  16.4 us
    pallas_call x3, Pallas kernels, scale(): pl.pallas_call(functools.partial(scale_kernel, z), grid=(steps,), out_sha...  14.8 us
    ppermute x9, waiting for transfers between devices, swap_with(): return lax.ppermute(value, AXIS, [(d, d ^ bit) for d in range(size)])  14.2 us
    pallas_call x1, Pallas kernels, left_side(): pl.pallas_call(functools.partial(left_side_kernel, z), out_shape=sds((z.s...  11.3 us
    ppermute x9, starting transfers between devices, swap_with(): return lax.ppermute(value, AXIS, [(d, d ^ bit) for d in range(size)])  10.1 us
    pallas_call x1, Pallas kernels, right_sum(): pl.pallas_call(functools.partial(right_sum_kernel, z), out_shape=(sds(out...  8.95 us
    all_to_all x1, starting transfers between devices, on_device(): lax.all_to_all(of_chip, AXIS, 0, 0, tiled=True, axis_index_groups=same_core)  3.99 us
    all_to_all x1, starting transfers between devices, on_device(): left_all = lax.all_to_all(left, AXIS, 0, 0, tiled=True)  3.5 us
  transfers between devices with their start and end apart: 11, of which 7 were waited for; matrix products, arithmetic and copies ran while one was open for 1% of the time, Pallas kernels for 31%

profile of v2, /device:TPU:0, one launch (start us, length us, event | category | flops | bytes accessed | tf_op | source)
XLA Modules:
  0.0 96.3 jit_solution(8803846363281780170)
XLA Ops:
  0.6 2.4 %project.1 = (bf16[16,16,128]{2,1,0:T(8,128)(2,1)}, bf16[32,768]{1,0:T(8,128)(2,1)S(1)}, f32[768,256]{1,0:T(8,128)S(1)}, f32[768,1]{1,0:T(8,128)S(1)}) custom-call(bf16[768,256]{1,0:T(8,128)(2,1)} %bitcast.26, f32[1,256]{1,0:T(1,128)} %bitcast.21, f32[1,256]{1,0:T(1,128)} %bitcast.24, bf16[32,256]{1,0:T(8,128)(2,1)} %bitcast.15, bf16[32,256]{1,0:T(8,128)(2,1)} %bitcast.17), custom_call_target="tpu_custom_call" | custom-call | tf_op jit(solution)/shard_map/project/pallas_call | solution.py:97
  3.0 4.0 %collective-permute-start = (bf16[1,32,768]{2,1,0:T(8,128)(2,1)S(1)}, bf16[1,32,768]{2,1,0:T(8,128)(2,1)S(1)}, u32[]{:S(2)}, u32[]{:S(2)}) collective-permute-start(bf16[1,32,768]{2,1,0:T(8,128)(2,1)S(1)} %bitcast.19), channel_id=1, source_target_pairs={{0,8},{1,9},{2,10},{3,11},{4,12},{5,13},{6,14},{7,15},{8,0},{9,1},... | collective-permute-start | bytes 147464 | tf_op jit(solution)/shard_map/ppermute | solution.py:543
  7.0 0.7 multiply_add_fusion
  7.8 0.7 copy-done.4
  8.4 0.7 copy-done.5
  9.1 1.4 %cover.1 = (f32[16,768]{1,0:T(8,128)S(1)}, f32[48,16]{1,0:T(8,128)S(1)}, f32[1,768]{1,0:T(1,128)S(1)}, bf16[32,4096]{1,0:T(8,128)(2,1)S(1)}) custom-call(s32[16]{0:T(128)S(1)} %copy-done.4, s32[16]{0:T(128)S(1)} %copy-done.5, s32[1,768]{1,0:T(1,128)S(1)} %reshape.41.code_ref, bf16[1024,128]{1,0:T(8,128)(2,1)} %w_ref.1), custom_call_target="tpu_custom_call" | custom-call | tf_op jit(solution)/shard_map/cover/pallas_call | solution.py:136
  10.5 4.9 %scale.3.refs_0_ = bf16[768,2048]{1,0:T(8,128)(2,1)} custom-call(bf16[48,768,128]{2,1,0:T(8,128)(2,1)} %g_ref.2, f32[6,8,16]{2,1,0:T(8,128)S(1)} %bitcast.12, f32[16,768]{1,0:T(8,128)S(1)} %get-tuple-element.48.cover_ref), custom_call_target="tpu_custom_call" | custom-call | flops 1572864 | bytes 6291456 | tf_op jit(solution)/shard_map/scale/pallas_call | solution.py:172
  15.4 1.6 %collective-permute-start.1 = (bf16[2,32,768]{2,1,0:T(8,128)(2,1)S(1)}, bf16[2,32,768]{2,1,0:T(8,128)(2,1)S(1)}, u32[]{:S(2)}, u32[]{:S(2)}) collective-permute-start(bf16[2,32,768]{2,1,0:T(8,128)(2,1)S(1)} %stack.3.here_ref), channel_id=1, source_target_pairs={{0,4},{1,5},{2,6},{3,7},{4,0},{5,1},{6,2},{7,3},{8,12},{9,13},{10,... | collective-permute-start | bytes 294920 | tf_op jit(solution)/shard_map/ppermute | solution.py:543
  17.1 4.9 %scale.4.refs_1_ = bf16[768,2048]{1,0:T(8,128)(2,1)} custom-call(bf16[48,768,128]{2,1,0:T(8,128)(2,1)} %g_ref.2, f32[6,8,16]{2,1,0:T(8,128)S(1)} %bitcast.13, f32[16,768]{1,0:T(8,128)S(1)} %get-tuple-element.48.cover_ref), custom_call_target="tpu_custom_call" | custom-call | flops 1572864 | bytes 6291456 | tf_op jit(solution)/shard_map/scale/pallas_call | solution.py:172
  22.0 1.6 %collective-permute-start.2 = (bf16[4,32,768]{2,1,0:T(8,128)(2,1)S(1)}, bf16[4,32,768]{2,1,0:T(8,128)(2,1)S(1)}, u32[]{:S(2)}, u32[]{:S(2)}) collective-permute-start(bf16[4,32,768]{2,1,0:T(8,128)(2,1)S(1)} %stack.4.here_ref), channel_id=1, source_target_pairs={{0,2},{1,3},{2,0},{3,1},{4,6},{5,7},{6,4},{7,5},{8,10},{9,11},{10,... | collective-permute-start | bytes 589832 | tf_op jit(solution)/shard_map/ppermute | solution.py:543
  23.6 3.5 %all-to-all-start = ((bf16[16,16,128]{2,1,0:T(8,128)(2,1)}), bf16[16,16,128]{2,1,0:T(8,128)(2,1)S(1)}, u32[]{:S(2)}, u32[]{:S(2)}) async-start(bf16[16,16,128]{2,1,0:T(8,128)(2,1)} %get-tuple-element.43), calls=%async_computation | async-start | bytes 131072 | tf_op jit(solution)/shard_map/all_to_all | solution.py:552
  27.1 5.0 %scale.5.refs_2_ = bf16[768,2048]{1,0:T(8,128)(2,1)} custom-call(bf16[48,768,128]{2,1,0:T(8,128)(2,1)} %g_ref.2, f32[6,8,16]{2,1,0:T(8,128)S(1)} %bitcast.14, f32[16,768]{1,0:T(8,128)S(1)} %get-tuple-element.48.cover_ref), custom_call_target="tpu_custom_call" | custom-call | flops 1572864 | bytes 6291456 | tf_op jit(solution)/shard_map/scale/pallas_call | solution.py:172
  32.1 1.9 %all-to-all-done.l_ref = bf16[16,16,128]{2,1,0:T(8,128)(2,1)S(1)} async-done(((bf16[16,16,128]{2,1,0:T(8,128)(2,1)}), bf16[16,16,128]{2,1,0:T(8,128)(2,1)S(1)}, u32[]{:S(2)}, u32[]{:S(2)}) %all-to-all-start) | async-done | bytes 65568 | tf_op jit(solution)/shard_map/all_to_all | solution.py:552
  34.0 9.0 %right_sum.1 = (bf16[8,32,768]{2,1,0:T(8,128)(2,1)S(1)}, bf16[8,32,768]{2,1,0:T(8,128)(2,1)S(1)}) custom-call(bf16[16,16,128]{2,1,0:T(8,128)(2,1)S(1)} %all-to-all-done.l_ref, f32[48,16]{1,0:T(8,128)S(1)} %get-tuple-element.47.own_ref, bf16[32,4096]{1,0:T(8,128)(2,1)S(1)} %get-tuple-element.57.w_ref, bf16[768,2048]{1,0:T(8,128)(2,1)} %scale.3.refs_0_, ...), custom_call_target="tpu_custom_call" | custom-call | flops 4831838208 | tf_op jit(solution)/shard_map/right_sum/pallas_call | solution.py:255
  42.9 0.1 collective-permute-start.3
  43.0 0.5 collective-permute-start.4
  43.5 1.2 %collective-permute-done.3.there_ref = bf16[8,32,768]{2,1,0:T(8,128)(2,1)S(1)} collective-permute-done((bf16[8,32,768]{2,1,0:T(8,128)(2,1)S(1)}, bf16[8,32,768]{2,1,0:T(8,128)(2,1)S(1)}, u32[]{:S(2)}, u32[]{:S(2)}) %collective-permute-start.3) | collective-permute-done | bytes 393248 | tf_op jit(solution)/shard_map/ppermute | solution.py:543
  44.7 0.8 pair_sum.1
  45.6 4.0 %all-to-all-start.1 = ((bf16[8,32,768]{2,1,0:T(8,128)(2,1)}), bf16[8,32,768]{2,1,0:T(8,128)(2,1)S(1)}, u32[]{:S(2)}, u32[]{:S(2)}) async-start(bf16[8,32,768]{2,1,0:T(8,128)(2,1)} %pair_sum.1), calls=%async_computation.1 | async-start | bytes 786432 | tf_op jit(solution)/shard_map/all_to_all | solution.py:574
  49.6 11.3 %left_side.1 = bf16[16,80,128]{2,1,0:T(8,128)(2,1)S(1)} custom-call(bf16[8,32,768]{2,1,0:T(8,128)(2,1)S(1)} %stack.5.here_ref, bf16[8,32,768]{2,1,0:T(8,128)(2,1)S(1)} %collective-permute-done.4.there_ref, f32[16,768]{1,0:T(8,128)S(1)} %get-tuple-element.48.cover_ref, bf16[16,16,128]{2,1,0:T(8,128)(2,1)S(1)} %all-to-all-done.l_ref, ...), custom_call_target="tpu_custom_call" | custom-call | flops 4831838208 | tf_op jit(solution)/shard_map/left_side/pallas_call | solution.py:332
  60.9 0.6 all-to-all-done.1.parts_ref
  61.6 16.4 %all_to_all.15.got_ref = bf16[16,80,128]{2,1,0:T(8,128)(2,1)S(1)} all-to-all(bf16[16,80,128]{2,1,0:T(8,128)(2,1)S(1)} %left_side.1), channel_id=1, replica_groups=mesh['grp'=2,'dap'=16] {'dap'}, dimensions={0} | all-to-all | bytes 655360 | tf_op jit(solution)/shard_map/all_to_all | solution.py:578
  78.0 0.9 owner.1
  78.9 1.4 %collective-permute-start.5 = (bf16[208,128]{1,0:T(8,128)(2,1)S(1)}, bf16[208,128]{1,0:T(8,128)(2,1)S(1)}, u32[]{:S(2)}, u32[]{:S(2)}) collective-permute-start(bf16[208,128]{1,0:T(8,128)(2,1)S(1)} %get-tuple-element.70.here_ref), channel_id=1, source_target_pairs={{0,8},{1,9},{2,10},{3,11},{4,12},{5,13},{6,14},{7,15},{8,0},{9,1},... | collective-permute-start | bytes 159752 | tf_op jit(solution)/shard_map/ppermute | solution.py:543
  80.3 1.2 %home.1 = bf16[768,256]{1,0:T(8,128)(2,1)} custom-call(f32[768,256]{1,0:T(8,128)S(1)} %get-tuple-element.71.grad_ref, f32[768,256]{1,0:T(8,128)S(1)} %get-tuple-element.69.unit_ref, f32[768,1]{1,0:T(8,128)S(1)} %get-tuple-element.72.inverse_ref, f32[1,256]{1,0:T(1,128)S(1)} %bitcast.23), custom_call_target="tpu_custom_call" | custom-call | tf_op jit(solution)/shard_map/home/pallas_call | solution.py:511
  81.5 3.3 %collective-permute-done.5.there_ref = bf16[208,128]{1,0:T(8,128)(2,1)S(1)} collective-permute-done((bf16[208,128]{1,0:T(8,128)(2,1)S(1)}, bf16[208,128]{1,0:T(8,128)(2,1)S(1)}, u32[]{:S(2)}, u32[]{:S(2)}) %collective-permute-start.5) | collective-permute-done | bytes 53280 | tf_op jit(solution)/shard_map/ppermute | solution.py:543
  84.9 4.3 %collective-permute-done.6.there_ref = bf16[272,128]{1,0:T(8,128)(2,1)S(1)} collective-permute-done((bf16[272,128]{1,0:T(8,128)(2,1)S(1)}, bf16[272,128]{1,0:T(8,128)(2,1)S(1)}, u32[]{:S(2)}, u32[]{:S(2)}) %collective-permute-start.6) | collective-permute-done | bytes 69664 | tf_op jit(solution)/shard_map/ppermute | solution.py:543
  89.2 0.8 collective-permute-start.7
  89.9 4.0 %collective-permute-done.7.there_ref = bf16[400,128]{1,0:T(8,128)(2,1)S(1)} collective-permute-done((bf16[400,128]{1,0:T(8,128)(2,1)S(1)}, bf16[400,128]{1,0:T(8,128)(2,1)S(1)}, u32[]{:S(2)}, u32[]{:S(2)}) %collective-permute-start.7) | collective-permute-done | bytes 102432 | tf_op jit(solution)/shard_map/ppermute | solution.py:543
  93.9 0.1 collective-permute-start.8
  94.0 1.4 %collective-permute-done.8.there_ref = bf16[656,128]{1,0:T(8,128)(2,1)S(1)} collective-permute-done((bf16[656,128]{1,0:T(8,128)(2,1)S(1)}, bf16[656,128]{1,0:T(8,128)(2,1)S(1)}, u32[]{:S(2)}, u32[]{:S(2)}) %collective-permute-start.8) | collective-permute-done | bytes 167968 | tf_op jit(solution)/shard_map/ppermute | solution.py:543
  95.4 0.9 finish.1
  (22 shorter events, 0.2 us)
Async XLA Ops:
  3.0 12.4 %collective-permute-start = (bf16[1,32,768]{2,1,0:T(8,128)(2,1)S(1)}, bf16[1,32,768]{2,1,0:T(8,128)(2,1)S(1)}, u32[]{:S(2)}, u32[]{:S(2)}) collective-permute-start(bf16[1,32,768]{2,1,0:T(8,128)(2,1)S(1)} %bitcast.19), channel_id=1, source_target_pairs={{0,8},{1,9},{2,10},{3,11},{4,12},{5,13},{6,14},{7,15},{8,0},{9,1},... | collective-permute-start | bytes 147464 | tf_op jit(solution)/shard_map/ppermute | solution.py:543
  7.8 0.7 copy-start.4
  8.4 0.7 copy-start.5
  15.4 6.6 %collective-permute-start.1 = (bf16[2,32,768]{2,1,0:T(8,128)(2,1)S(1)}, bf16[2,32,768]{2,1,0:T(8,128)(2,1)S(1)}, u32[]{:S(2)}, u32[]{:S(2)}) collective-permute-start(bf16[2,32,768]{2,1,0:T(8,128)(2,1)S(1)} %stack.3.here_ref), channel_id=1, source_target_pairs={{0,4},{1,5},{2,6},{3,7},{4,0},{5,1},{6,2},{7,3},{8,12},{9,13},{10,... | collective-permute-start | bytes 294920 | tf_op jit(solution)/shard_map/ppermute | solution.py:543
  22.0 10.0 %collective-permute-start.2 = (bf16[4,32,768]{2,1,0:T(8,128)(2,1)S(1)}, bf16[4,32,768]{2,1,0:T(8,128)(2,1)S(1)}, u32[]{:S(2)}, u32[]{:S(2)}) collective-permute-start(bf16[4,32,768]{2,1,0:T(8,128)(2,1)S(1)} %stack.4.here_ref), channel_id=1, source_target_pairs={{0,2},{1,3},{2,0},{3,1},{4,6},{5,7},{6,4},{7,5},{8,10},{9,11},{10,... | collective-permute-start | bytes 589832 | tf_op jit(solution)/shard_map/ppermute | solution.py:543
  23.6 10.4 %all-to-all-start = ((bf16[16,16,128]{2,1,0:T(8,128)(2,1)}), bf16[16,16,128]{2,1,0:T(8,128)(2,1)S(1)}, u32[]{:S(2)}, u32[]{:S(2)}) async-start(bf16[16,16,128]{2,1,0:T(8,128)(2,1)} %get-tuple-element.43), calls=%async_computation | async-start | bytes 131072 | tf_op jit(solution)/shard_map/all_to_all | solution.py:552
  42.9 1.8 %collective-permute-start.3 = (bf16[8,32,768]{2,1,0:T(8,128)(2,1)S(1)}, bf16[8,32,768]{2,1,0:T(8,128)(2,1)S(1)}, u32[]{:S(2)}, u32[]{:S(2)}) collective-permute-start(bf16[8,32,768]{2,1,0:T(8,128)(2,1)S(1)} %get-tuple-element.62), channel_id=1, source_target_pairs={{0,1},{1,0},{2,3},{3,2},{4,5},{5,4},{6,7},{7,6},{8,9},{9,8},{10,11... | collective-permute-start | bytes 1179656 | tf_op jit(solution)/shard_map/ppermute | solution.py:543
  43.0 6.6 %collective-permute-start.4 = (bf16[8,32,768]{2,1,0:T(8,128)(2,1)S(1)}, bf16[8,32,768]{2,1,0:T(8,128)(2,1)S(1)}, u32[]{:S(2)}, u32[]{:S(2)}) collective-permute-start(bf16[8,32,768]{2,1,0:T(8,128)(2,1)S(1)} %stack.5.here_ref), channel_id=1, source_target_pairs={{0,1},{1,0},{2,3},{3,2},{4,5},{5,4},{6,7},{7,6},{8,9},{9,8},{10,11... | collective-permute-start | bytes 1179656 | tf_op jit(solution)/shard_map/ppermute | solution.py:543
  45.6 16.0 %all-to-all-start.1 = ((bf16[8,32,768]{2,1,0:T(8,128)(2,1)}), bf16[8,32,768]{2,1,0:T(8,128)(2,1)S(1)}, u32[]{:S(2)}, u32[]{:S(2)}) async-start(bf16[8,32,768]{2,1,0:T(8,128)(2,1)} %pair_sum.1), calls=%async_computation.1 | async-start | bytes 786432 | tf_op jit(solution)/shard_map/all_to_all | solution.py:574
  49.6 28.4 %copy-start = (bf16[256,32]{0,1:T(8,128)(2,1)S(1)}, bf16[256,32]{0,1:T(8,128)(2,1)}, u32[]{:S(2)}) copy-start(bf16[256,32]{0,1:T(8,128)(2,1)} %param.14) | copy-start | bytes 49156
  49.6 28.4 %copy-start.1 = (bf16[256,32]{0,1:T(8,128)(2,1)S(1)}, bf16[256,32]{0,1:T(8,128)(2,1)}, u32[]{:S(2)}) copy-start(bf16[256,32]{0,1:T(8,128)(2,1)} %param.15) | copy-start | bytes 49156
  49.6 28.4 %copy-start.2 = (f32[256]{0:T(256)S(1)}, f32[256]{0:T(256)}, u32[]{:S(2)}) copy-start(f32[256]{0:T(256)} %param.12) | copy-start | bytes 3076
  49.6 28.4 %copy-start.3 = (f32[256]{0:T(256)S(1)}, f32[256]{0:T(256)}, u32[]{:S(2)}) copy-start(f32[256]{0:T(256)} %param.13) | copy-start | bytes 3076
  78.9 5.9 %collective-permute-start.5 = (bf16[208,128]{1,0:T(8,128)(2,1)S(1)}, bf16[208,128]{1,0:T(8,128)(2,1)S(1)}, u32[]{:S(2)}, u32[]{:S(2)}) collective-permute-start(bf16[208,128]{1,0:T(8,128)(2,1)S(1)} %get-tuple-element.70.here_ref), channel_id=1, source_target_pairs={{0,8},{1,9},{2,10},{3,11},{4,12},{5,13},{6,14},{7,15},{8,0},{9,1},... | collective-permute-start | bytes 159752 | tf_op jit(solution)/shard_map/ppermute | solution.py:543
  84.8 4.4 %collective-permute-start.6 = (bf16[272,128]{1,0:T(8,128)(2,1)S(1)}, bf16[272,128]{1,0:T(8,128)(2,1)S(1)}, u32[]{:S(2)}, u32[]{:S(2)}) collective-permute-start(bf16[272,128]{1,0:T(8,128)(2,1)S(1)} %join.3.here_ref), channel_id=1, source_target_pairs={{0,4},{1,5},{2,6},{3,7},{4,0},{5,1},{6,2},{7,3},{8,12},{9,13},{10,... | collective-permute-start | bytes 208904 | tf_op jit(solution)/shard_map/ppermute | solution.py:543
  89.2 4.7 %collective-permute-start.7 = (bf16[400,128]{1,0:T(8,128)(2,1)S(1)}, bf16[400,128]{1,0:T(8,128)(2,1)S(1)}, u32[]{:S(2)}, u32[]{:S(2)}) collective-permute-start(bf16[400,128]{1,0:T(8,128)(2,1)S(1)} %join.4.here_ref), channel_id=1, source_target_pairs={{0,2},{1,3},{2,0},{3,1},{4,6},{5,7},{6,4},{7,5},{8,10},{9,11},{10,... | collective-permute-start | bytes 307208 | tf_op jit(solution)/shard_map/ppermute | solution.py:543
  93.9 1.5 %collective-permute-start.8 = (bf16[656,128]{1,0:T(8,128)(2,1)S(1)}, bf16[656,128]{1,0:T(8,128)(2,1)S(1)}, u32[]{:S(2)}, u32[]{:S(2)}) collective-permute-start(bf16[656,128]{1,0:T(8,128)(2,1)S(1)} %join.5.here_ref), channel_id=1, source_target_pairs={{0,1},{1,0},{2,3},{3,2},{4,5},{5,4},{6,7},{7,6},{8,9},{9,8},{10,11... | collective-permute-start | bytes 503816 | tf_op jit(solution)/shard_map/ppermute | solution.py:543

commit v3 on v2

--- a/solution.py
+++ b/solution.py
@@ -31,8 +31,9 @@
     return pltpu.CompilerParams(vmem_limit_bytes=mib * MIB)
 
 
-def whole(*shape):
-    return pl.BlockSpec(shape, lambda *_: (0,) * len(shape))
+def cost(microseconds):
+    flops = int(microseconds * 1.15e9)
+    return pl.CostEstimate(flops=flops, bytes_accessed=0, transcendentals=0)
 
 
 def sds(shape, dtype):
@@ -57,10 +58,8 @@
         self.piece_slots = up(self.piece)
         self.sum_rows = up(2 * width + 2, 8) * features // LANES
         self.block = max(b for b in range(1, 9) if res % b == 0)
-        blocks = res // self.block
-        self.pieces = max(n for n in (3, 2, 1) if blocks % n == 0)
-        self.per_piece = blocks // self.pieces
-        self.mib = 28 if self.wide <= 1024 else 56
+        self.blocks = res // self.block
+        self.mib = 40 if self.wide <= 1024 else 56
         bits = size.bit_length() - 1
         self.masks = [size >> (b + 1) for b in range(bits)]
 
@@ -105,6 +104,7 @@
         in_specs=[VMEM] * 5,
         out_specs=(VMEM,) * 4,
         compiler_params=params(16),
+        cost_estimate=cost(2.4),
         name="project",
     )(x, gain, bias, lwt, rwt)
 
@@ -145,44 +145,9 @@
         out_specs=(VMEM,) * 4,
         scratch_shapes=[pltpu.VMEM(weight.shape, F32)],
         compiler_params=params(8),
+        cost_estimate=cost(1.4),
         name="cover",
     )(smask, schain, code, in_hbm(weight))
-
-
-def scale_kernel(z, g_ref, own_ref, cover_ref, out_ref):
-    block, pair = z.block, z.pair
-    count = mm(own_ref[0].astype(BF16), cover_ref[...].astype(BF16))
-    factor = 1.0 / jnp.maximum(count, 1.0)
-    high = factor.astype(BF16)
-    low = (factor - high.astype(F32)).astype(BF16)
-    shape = (block, block * pair)
-    pick = (
-        lax.broadcasted_iota(jnp.int32, shape, 0)
-        == lax.broadcasted_iota(jnp.int32, shape, 1) // pair
-    ).astype(F32).astype(BF16)
-    spread = mm(high, pick, (0, 0)) + mm(low, pick, (0, 0))
-    for b in range(block):
-        at = slice(b * pair, (b + 1) * pair)
-        out_ref[:, at] = (g_ref[b].astype(F32) * spread[:, at]).astype(BF16)
-
-
-def scale(z, gradient, own, cover, piece):
-    steps = z.per_piece
-    size = gradient.size // z.pieces
-    return pl.pallas_call(
-        functools.partial(scale_kernel, z),
-        grid=(steps,),
-        out_shape=pltpu.HBM((z.cols, steps * z.block * z.pair), BF16),
-        in_specs=[
-            pl.BlockSpec((z.block, z.cols, z.pair), lambda b: (piece * steps + b, 0, 0)),
-            pl.BlockSpec((1, z.block, z.seqs), lambda b: (piece * steps + b, 0, 0)),
-            whole(*cover.shape),
-        ],
-        out_specs=pl.BlockSpec((z.cols, z.block * z.pair), lambda b: (0, b)),
-        compiler_params=params(20),
-        cost_estimate=pl.CostEstimate(flops=size, bytes_accessed=4 * size, transcendentals=0),
-        name="scale",
-    )(in_hbm(gradient), own.reshape(z.res // z.block, z.block, z.seqs), cover)
 
 
 def order_left(z, l_ref, own_ref, scratch):
@@ -194,38 +159,39 @@
             scratch[pl.ds(g * z.rows * z.seqs + s, z.rows, stride=z.seqs), :] = part
 
 
-def scaled_copy(z, s_refs, here, arrived, piece, step):
+def block_span(z, step):
     size = z.block * z.pair
-    at = piece * z.per_piece + step
-    source = pl.ds(pl.multiple_of(step * size, size), size)
-    span = pl.ds(pl.multiple_of(at * size, size), size)
-    return pltpu.make_async_copy(s_refs[piece].at[:, source], here.at[:, span], arrived.at[at]), span
-
-
-def fetch_scaled(z, s_refs, here, arrived):
-    for piece in range(z.pieces):
-        for step in range(z.per_piece):
-            scaled_copy(z, s_refs, here, arrived, piece, step)[0].start()
-
-
-def over_scaled(z, s_refs, here, arrived, body):
-    for piece in range(z.pieces):
-
-        @pl.loop(0, z.per_piece)
-        def _(step):
-            copy, span = scaled_copy(z, s_refs, here, arrived, piece, step)
-            copy.wait()
-            body(piece * z.per_piece + step, span)
-
-
-def right_sum_kernel(z, l_ref, own_ref, w_ref, *refs):
-    s_refs = refs[: z.pieces]
-    keep_ref, give_ref, ordered, mixed, total, here, arrived = refs[z.pieces :]
+    return pl.ds(pl.multiple_of(step * size, size), size)
+
+
+def right_sum_kernel(z, l_ref, own_ref, cover_ref, w_ref, g_ref, keep_ref, give_ref, scaled_ref,
+                     ordered, mixed, total, raw, here, arrived, left_for):
     core = lax.axis_index(AXIS) % 2
-    seqs, pair = z.seqs, z.pair
-    fetch_scaled(z, s_refs, here, arrived)
+    seqs, pair, block = z.seqs, z.pair, z.block
+
+    def fetch(step):
+        at = pl.ds(step * block, block)
+        return pltpu.make_async_copy(g_ref.at[at], raw.at[at], arrived.at[step])
+
+    def store(step):
+        span = slice(step * block * pair, (step + 1) * block * pair)
+        return pltpu.make_async_copy(here.at[:, span], scaled_ref.at[:, span], left_for.at[step])
+
+    for step in range(z.blocks):
+        fetch(step).start()
+    count = mm(cover_ref[...].astype(BF16), own_ref[...].astype(BF16), (0, 1))
+    factor = 1.0 / jnp.maximum(count, 1.0)
+
+    def scale(step):
+        for i in range(step * block, (step + 1) * block):
+            here[:, i * pair : (i + 1) * pair] = (
+                raw[i].astype(F32) * factor[:, i : i + 1]
+            ).astype(BF16)
+
     order_left(z, l_ref, own_ref, ordered)
     left = ordered[...].astype(BF16)
+    fetch(0).wait()
+    scale(0)
     group = 8
     for first in range(0, z.width, group):
         part = mm(left, w_ref[:, first * pair : (first + group) * pair]).astype(BF16)
@@ -234,50 +200,63 @@
                 mixed[(first + e) * seqs : (first + e + 1) * seqs, i * pair : (i + 1) * pair] = part[
                     i * seqs : (i + 1) * seqs, e * pair : (e + 1) * pair
                 ]
-
-    total[...] = jnp.zeros_like(total)
-
-    def add(_, span):
+    store(0).start()
+
+    for step in range(z.blocks):
+        if step + 1 < z.blocks:
+            fetch(step + 1).wait()
+            scale(step + 1)
+        span = slice(step * block * pair, (step + 1) * block * pair)
         product = mm(mixed[:, span], here[:, span], (1, 1))
         for c in range(z.planes):
-            total[c] += product[:, c * LANES : (c + 1) * LANES]
-
-    over_scaled(z, s_refs, here, arrived, add)
+            part = product[:, c * LANES : (c + 1) * LANES]
+            total[c] = part if step == 0 else total[c] + part
+        if step + 1 < z.blocks:
+            store(step + 1).start()
+
     for chip in range(z.chips):
         for ref, parity in ((keep_ref, core), (give_ref, 1 - core)):
             at = pl.ds(2 * chip + parity, z.width, stride=seqs)
             for c in range(z.planes):
                 ref[chip, :, c * LANES : (c + 1) * LANES] = total[c, at, :].astype(BF16)
-
-
-def right_sum(z, left, own, weight, scaled):
+    for step in range(z.blocks):
+        store(step).wait()
+
+
+def right_sum(z, left, own, cover, weight, gradient):
     out = (z.chips, z.width, z.cols)
+    hbm = pl.BlockSpec(memory_space=pltpu.HBM)
     return pl.pallas_call(
         functools.partial(right_sum_kernel, z),
-        out_shape=(sds(out, BF16), sds(out, BF16)),
-        in_specs=[VMEM] * 3 + [pl.BlockSpec(memory_space=pltpu.HBM)] * z.pieces,
-        out_specs=(VMEM, VMEM),
+        out_shape=(sds(out, BF16), sds(out, BF16), pltpu.HBM((z.cols, z.res * z.pair), BF16)),
+        in_specs=[VMEM] * 4 + [hbm],
+        out_specs=(VMEM, VMEM, hbm),
         scratch_shapes=[
             pltpu.VMEM((z.res * z.seqs, z.width), F32),
             pltpu.VMEM((z.wide, z.res * z.pair), BF16),
             pltpu.VMEM((z.planes, z.wide, LANES), F32),
+            pltpu.VMEM(gradient.shape, BF16),
             pltpu.VMEM((z.cols, z.res * z.pair), BF16),
-            pltpu.SemaphoreType.DMA((z.res // z.block,)),
+            pltpu.SemaphoreType.DMA((z.blocks,)),
+            pltpu.SemaphoreType.DMA((z.blocks,)),
         ],
         compiler_params=params(z.mib),
-        cost_estimate=pl.CostEstimate(
-            flops=2 * z.wide * z.cols * z.res * z.pair, bytes_accessed=0, transcendentals=0
-        ),
+        cost_estimate=cost(13),
         name="right_sum",
-    )(left, own, weight, *[in_hbm(piece) for piece in scaled])
-
-
-def left_side_kernel(z, here_ref, there_ref, cover_ref, l_ref, own_ref, w_ref, *refs):
-    s_refs = refs[: z.pieces]
-    out_ref, ordered, right, proj, back, wide_rows, here, arrived = refs[z.pieces :]
+    )(left, own, cover, weight, in_hbm(gradient))
+
+
+def left_side_kernel(z, here_ref, there_ref, cover_ref, l_ref, own_ref, w_ref, s_ref,
+                     out_ref, ordered, right, proj, back, wide_rows, here, arrived):
     me = lax.axis_index(AXIS)
     seqs, pair, block, width = z.seqs, z.pair, z.block, z.width
-    fetch_scaled(z, s_refs, here, arrived)
+
+    def fetch(step):
+        span = block_span(z, step)
+        return pltpu.make_async_copy(s_ref.at[:, span], here.at[:, span], arrived.at[step])
+
+    for step in range(z.blocks):
+        fetch(step).start()
     order_left(z, l_ref, own_ref, ordered)
     for side, ref in ((0, here_ref), (z.size // 2, there_ref)):
 
@@ -293,7 +272,10 @@
             lanes = slice(c * LANES, (c + 1) * LANES)
             right[at, lanes] = (wide_rows[c, at, :] * cover_ref[:, lanes]).astype(BF16)
 
-    def project_block(step, span):
+    @pl.loop(0, z.blocks)
+    def _(step):
+        fetch(step).wait()
+        span = block_span(z, step)
         group = width // 4
         for first in range(0, width, group):
             part = mm(right[first * seqs : (first + group) * seqs, :], here[:, span])
@@ -305,7 +287,6 @@
                         e * seqs : (e + 1) * seqs, i * pair : (i + 1) * pair
                     ]
 
-    over_scaled(z, s_refs, here, arrived, project_block)
     back[...] = mm(proj[...], w_ref[...], (1, 1))
     spread = wide_rows.at[0]
     left = ordered[...].astype(BF16)
@@ -332,7 +313,7 @@
     return pl.pallas_call(
         functools.partial(left_side_kernel, z),
         out_shape=sds((z.size, z.piece_slots + z.slots, LANES), BF16),
-        in_specs=[VMEM] * 6 + [pl.BlockSpec(memory_space=pltpu.HBM)] * z.pieces,
+        in_specs=[VMEM] * 6 + [pl.BlockSpec(memory_space=pltpu.HBM)],
         out_specs=VMEM,
         scratch_shapes=[
             pltpu.VMEM((z.res * z.seqs, z.width), F32),
@@ -341,14 +322,12 @@
             pltpu.VMEM((z.res * z.seqs, z.width), F32),
             pltpu.VMEM((z.planes, max(z.wide, z.width * z.width), LANES), F32),
             pltpu.VMEM((z.cols, z.res * z.pair), BF16),
-            pltpu.SemaphoreType.DMA((z.res // z.block,)),
+            pltpu.SemaphoreType.DMA((z.blocks,)),
         ],
         compiler_params=params(z.mib),
-        cost_estimate=pl.CostEstimate(
-            flops=2 * z.wide * z.cols * z.res * z.pair, bytes_accessed=0, transcendentals=0
-        ),
+        cost_estimate=cost(11),
         name="left_side",
-    )(here, there, cover, left, own, weight, *[in_hbm(piece) for piece in scaled])
+    )(here, there, cover, left, own, weight, in_hbm(scaled))
 
 
 def owner_kernel(z, parts_ref, got_ref, cover_ref, unit_ref, gain_ref, bias_ref, lwt_ref, rwt_ref,
@@ -403,25 +382,29 @@
         out_specs=(VMEM, VMEM),
         scratch_shapes=[pltpu.VMEM((z.cols, z.width), F32)],
         compiler_params=params(24),
+        cost_estimate=cost(0.9),
         name="owner",
     )(parts, got, cover, unit, gain, bias, lwt, rwt)
 
 
-def stack_kernel(here_ref, there_ref, out_ref):
-    half = here_ref.shape[0]
-    out_ref[:half] = here_ref[...]
-    out_ref[half:] = there_ref[...]
-
-
-def stack(here, there):
+def stack_kernel(*refs):
+    *parts, out_ref = refs
+    size = parts[0].shape[0]
+    for p, ref in enumerate(parts):
+        out_ref[p * size : (p + 1) * size] = ref[...]
+
+
+def stack(*parts):
+    first = parts[0]
     return pl.pallas_call(
         stack_kernel,
-        out_shape=sds((2 * here.shape[0],) + here.shape[1:], here.dtype),
-        in_specs=[VMEM, VMEM],
+        out_shape=sds((len(parts) * first.shape[0],) + first.shape[1:], first.dtype),
+        in_specs=[VMEM] * len(parts),
         out_specs=VMEM,
         compiler_params=params(16),
+        cost_estimate=cost(0.4),
         name="stack",
-    )(here, there)
+    )(*parts)
 
 
 def pair_sum_kernel(here_ref, there_ref, out_ref):
@@ -436,6 +419,7 @@
         in_specs=[VMEM, VMEM],
         out_specs=VMEM,
         compiler_params=params(24),
+        cost_estimate=cost(0.8),
         name="pair_sum",
     )(here, there)
 
@@ -455,6 +439,7 @@
         in_specs=[VMEM, VMEM],
         out_specs=VMEM,
         compiler_params=params(8),
+        cost_estimate=cost(0.4),
         name="join",
     )(here, there)
 
@@ -490,6 +475,7 @@
         in_specs=[VMEM, VMEM],
         out_specs=(VMEM,) * 5,
         compiler_params=params(8),
+        cost_estimate=cost(0.9),
         name="finish",
     )(here, there)
 
@@ -514,6 +500,7 @@
         in_specs=[VMEM] * 4,
         out_specs=VMEM,
         compiler_params=params(16),
+        cost_estimate=cost(1.2),
         name="home",
     )(grad, unit, inverse, gain)
 
@@ -557,20 +544,16 @@
     )
 
     here = right[None]
-    scaled = []
-    for step in range(max(len(z.masks) - 1, z.pieces)):
-        there = swap_with(here, z.masks[step]) if step < len(z.masks) - 1 else None
-        if step < z.pieces:
-            gradient, here = lax.optimization_barrier((pair_output_gradient, here))
-            scaled.append(scale(z, gradient, own_residues, coverage, step))
-        if there is not None:
-            there, scaled[-1] = lax.optimization_barrier((there, scaled[-1]))
-            here = stack(here, there)
+    for bit in z.masks[:-3]:
+        here = stack(here, swap_with(here, bit))
+    one, two = z.masks[-3:-1]
+    here = stack(here, *[swap_with(here, bit) for bit in (one, two, one ^ two)])
     left_all, here = lax.optimization_barrier((left_all, here))
-    keep, give = right_sum(z, left_all, own_residues, w_mix, scaled)
     there = swap_with(here, z.masks[-1])
+    keep, give, scaled = right_sum(
+        z, left_all, own_residues, coverage, w_mix, pair_output_gradient
+    )
     of_chip = pair_sum(keep, swap_with(give, 1))
-    of_chip, here = lax.optimization_barrier((of_chip, here))
     parts = lax.all_to_all(of_chip, AXIS, 0, 0, tiled=True, axis_index_groups=same_core)
 
     shares = left_side(z, here, there, coverage, left_all, own_residues, w_mix, scaled)

time: 96.7 us -> 87 us (0.90)
  Pallas kernels: 42.8 us -> 32 us
  waiting for transfers between devices: 16.6 us -> 19.4 us
  local copies, waits for them, and re-layouts: 1.34 us -> 0.05 us
    pallas_call x6 -> x2, Pallas kernels: 14.9 us -> 0.04 us  [stack(): pl.pallas_call(stack_kernel, out_shape=sds((len(parts) * first.shape[0],)...]
    pallas_call x1, Pallas kernels: 8.95 us -> 13.3 us  [right_sum(): pl.pallas_call(functools.partial(right_sum_kernel, z), out_shape=(sds(out...]
    ppermute x9 -> x10, waiting for transfers between devices: 14.2 us -> 18.4 us  [swap_with(): return lax.ppermute(value, AXIS, [(d, d ^ bit) for d in range(size)])]
    all_to_all x1, waiting for transfers between devices: 1.87 us -> 0.01 us  [on_device(): left_all = lax.all_to_all(left, AXIS, 0, 0, tiled=True)]
    unnamed x12 -> x16, local copies, waits for them, and re-layouts: 1.33 us -> 0.04 us
    ppermute x9 -> x10, starting transfers between devices: 10.1 us -> 10.5 us  [swap_with(): return lax.ppermute(value, AXIS, [(d, d ^ bit) for d in range(size)])]
  transfers between devices with their start and end apart: 11 -> 12, of which waited for: 7 -> 9; matrix products, arithmetic and copies ran while one was open for 1% -> 0% of each run, Pallas kernels for 31% -> 17%
where the time goes in v3:
time: 87 us; the launch traced here: 86.6 us
  Pallas kernels  32 us (37%)
  waiting for transfers between devices  19.4 us (22%)
  starting transfers between devices  18.4 us (21%)
  blocking collectives  16 us (18%)
    ppermute x10, waiting for transfers between devices, swap_with(): return lax.ppermute(value, AXIS, [(d, d ^ bit) for d in range(size)])  18.4 us
    all_to_all x1, blocking collectives, on_device(): got = lax.all_to_all(shares, AXIS, 0, 0, tiled=True)  16 us
    pallas_call x1, Pallas kernels, right_sum(): pl.pallas_call(functools.partial(right_sum_kernel, z), out_shape=(sds(out...  13.3 us
    pallas_call x1, Pallas kernels, left_side(): pl.pallas_call(functools.partial(left_side_kernel, z), out_shape=sds((z.s...  10.9 us
    ppermute x10, starting transfers between devices, swap_with(): return lax.ppermute(value, AXIS, [(d, d ^ bit) for d in range(size)])  10.5 us
    all_to_all x1, starting transfers between devices, on_device(): lax.all_to_all(of_chip, AXIS, 0, 0, tiled=True, axis_index_groups=same_core)  4.01 us
    all_to_all x1, starting transfers between devices, on_device(): left_all = lax.all_to_all(left, AXIS, 0, 0, tiled=True)  3.91 us
    pallas_call x1, Pallas kernels, project(): pl.pallas_call(functools.partial(project_kernel, z), out_shape=(sds((z.si...  2.4 us
  transfers between devices with their start and end apart: 12, of which 9 were waited for; matrix products, arithmetic and copies ran while one was open for 0% of the time, Pallas kernels for 17%

profile of v3, /device:TPU:0, one launch (start us, length us, event | category | flops | bytes accessed | tf_op | source)
XLA Modules:
  0.0 86.6 jit_solution(15631713976681992072)
XLA Ops:
  0.7 2.4 %project.1 = (bf16[16,16,128]{2,1,0:T(8,128)(2,1)}, bf16[32,768]{1,0:T(8,128)(2,1)S(1)}, f32[768,256]{1,0:T(8,128)S(1)}, f32[768,1]{1,0:T(8,128)S(1)}) custom-call(bf16[768,256]{1,0:T(8,128)(2,1)} %bitcast.22, f32[1,256]{1,0:T(1,128)} %bitcast.19, f32[1,256]{1,0:T(1,128)} %bitcast.17, bf16[32,256]{1,0:T(8,128)(2,1)} %bitcast.13, bf16[32,256]{1,0:T(8,128)(2,1)} %bitcast.15), custom_call_target="tpu_custom_call" | custom-call | flops 2760000000 | tf_op jit(solution)/shard_map/project/pallas_call | solution.py:96
  3.1 4.0 %collective-permute-start = (bf16[1,32,768]{2,1,0:T(8,128)(2,1)S(1)}, bf16[1,32,768]{2,1,0:T(8,128)(2,1)S(1)}, u32[]{:S(2)}, u32[]{:S(2)}) collective-permute-start(bf16[1,32,768]{2,1,0:T(8,128)(2,1)S(1)} %bitcast.11), channel_id=1, source_target_pairs={{0,8},{1,9},{2,10},{3,11},{4,12},{5,13},{6,14},{7,15},{8,0},{9,1},... | collective-permute-start | bytes 147464 | tf_op jit(solution)/shard_map/ppermute | solution.py:530
  7.1 3.9 %all-to-all-start = ((bf16[16,16,128]{2,1,0:T(8,128)(2,1)}), bf16[16,16,128]{2,1,0:T(8,128)(2,1)S(1)}, u32[]{:S(2)}, u32[]{:S(2)}) async-start(bf16[16,16,128]{2,1,0:T(8,128)(2,1)} %get-tuple-element.30), calls=%async_computation | async-start | bytes 131072 | tf_op jit(solution)/shard_map/all_to_all | solution.py:539
  11.1 2.0 %collective-permute-start.1 = (bf16[2,32,768]{2,1,0:T(8,128)(2,1)S(1)}, bf16[2,32,768]{2,1,0:T(8,128)(2,1)S(1)}, u32[]{:S(2)}, u32[]{:S(2)}) collective-permute-start(bf16[2,32,768]{2,1,0:T(8,128)(2,1)S(1)} %stack.2.refs_0_), channel_id=1, source_target_pairs={{0,4},{1,5},{2,6},{3,7},{4,0},{5,1},{6,2},{7,3},{8,12},{9,13},{10,... | collective-permute-start | bytes 294920 | tf_op jit(solution)/shard_map/ppermute | solution.py:530
  13.1 1.5 %collective-permute-start.2 = (bf16[2,32,768]{2,1,0:T(8,128)(2,1)S(1)}, bf16[2,32,768]{2,1,0:T(8,128)(2,1)S(1)}, u32[]{:S(2)}, u32[]{:S(2)}) collective-permute-start(bf16[2,32,768]{2,1,0:T(8,128)(2,1)S(1)} %stack.2.refs_0_), channel_id=1, source_target_pairs={{0,2},{1,3},{2,0},{3,1},{4,6},{5,7},{6,4},{7,5},{8,10},{9,11},{10,... | collective-permute-start | bytes 294920 | tf_op jit(solution)/shard_map/ppermute | solution.py:530
  14.6 0.1 collective-permute-start.3
  14.7 1.4 %cover.1 = (f32[16,768]{1,0:T(8,128)S(1)}, f32[48,16]{1,0:T(8,128)S(1)}, f32[1,768]{1,0:T(1,128)S(1)}, bf16[32,4096]{1,0:T(8,128)(2,1)S(1)}) custom-call(s32[16]{0:T(128)S(1)} %copy-done.4, s32[16]{0:T(128)S(1)} %copy-done.5, s32[1,768]{1,0:T(1,128)S(1)} %reshape.36.code_ref, bf16[1024,128]{1,0:T(8,128)(2,1)} %w_ref.1), custom_call_target="tpu_custom_call" | custom-call | flops 1610000000 | tf_op jit(solution)/shard_map/cover/pallas_call | solution.py:136
  16.1 1.7 %collective-permute-done.1.refs_1_ = bf16[2,32,768]{2,1,0:T(8,128)(2,1)S(1)} collective-permute-done((bf16[2,32,768]{2,1,0:T(8,128)(2,1)S(1)}, bf16[2,32,768]{2,1,0:T(8,128)(2,1)S(1)}, u32[]{:S(2)}, u32[]{:S(2)}) %collective-permute-start.1) | collective-permute-done | bytes 98336 | tf_op jit(solution)/shard_map/ppermute | solution.py:530
  17.8 1.3 %collective-permute-done.2.refs_2_ = bf16[2,32,768]{2,1,0:T(8,128)(2,1)S(1)} collective-permute-done((bf16[2,32,768]{2,1,0:T(8,128)(2,1)S(1)}, bf16[2,32,768]{2,1,0:T(8,128)(2,1)S(1)}, u32[]{:S(2)}, u32[]{:S(2)}) %collective-permute-start.2) | collective-permute-done | bytes 98336 | tf_op jit(solution)/shard_map/ppermute | solution.py:530
  19.0 1.3 %collective-permute-done.3.refs_3_ = bf16[2,32,768]{2,1,0:T(8,128)(2,1)S(1)} collective-permute-done((bf16[2,32,768]{2,1,0:T(8,128)(2,1)S(1)}, bf16[2,32,768]{2,1,0:T(8,128)(2,1)S(1)}, u32[]{:S(2)}, u32[]{:S(2)}) %collective-permute-start.3) | collective-permute-done | bytes 98336 | tf_op jit(solution)/shard_map/ppermute | solution.py:530
  20.4 13.3 %right_sum.1 = (bf16[8,32,768]{2,1,0:T(8,128)(2,1)S(1)}, bf16[8,32,768]{2,1,0:T(8,128)(2,1)S(1)}, bf16[768,6144]{1,0:T(8,128)(2,1)}) custom-call(bf16[16,16,128]{2,1,0:T(8,128)(2,1)S(1)} %all-to-all-done.l_ref, f32[48,16]{1,0:T(8,128)S(1)} %get-tuple-element.35.own_ref, f32[16,768]{1,0:T(8,128)S(1)} %get-tuple-element.33.cover_ref, ...), custom_call_target="tpu_custom_call" | custom-call | flops 14949999616 | tf_op jit(solution)/shard_map/right_sum/pallas_call | solution.py:229
  33.7 0.1 collective-permute-start.5
  33.7 0.5 collective-permute-start.4
  34.2 1.2 %collective-permute-done.5.there_ref = bf16[8,32,768]{2,1,0:T(8,128)(2,1)S(1)} collective-permute-done((bf16[8,32,768]{2,1,0:T(8,128)(2,1)S(1)}, bf16[8,32,768]{2,1,0:T(8,128)(2,1)S(1)}, u32[]{:S(2)}, u32[]{:S(2)}) %collective-permute-start.5) | collective-permute-done | bytes 393248 | tf_op jit(solution)/shard_map/ppermute | solution.py:530
  35.4 0.8 pair_sum.1
  36.3 4.0 %all-to-all-start.1 = ((bf16[8,32,768]{2,1,0:T(8,128)(2,1)}), bf16[8,32,768]{2,1,0:T(8,128)(2,1)S(1)}, u32[]{:S(2)}, u32[]{:S(2)}) async-start(bf16[8,32,768]{2,1,0:T(8,128)(2,1)} %pair_sum.1), calls=%async_computation.1 | async-start | bytes 786432 | tf_op jit(solution)/shard_map/all_to_all | solution.py:557
  40.3 0.0 copy-start
  40.3 0.0 copy-start.1
  40.3 10.9 %left_side.1 = bf16[16,80,128]{2,1,0:T(8,128)(2,1)S(1)} custom-call(bf16[8,32,768]{2,1,0:T(8,128)(2,1)S(1)} %stack.3.here_ref, bf16[8,32,768]{2,1,0:T(8,128)(2,1)S(1)} %collective-permute-done.4.there_ref, f32[16,768]{1,0:T(8,128)S(1)} %get-tuple-element.33.cover_ref, bf16[16,16,128]{2,1,0:T(8,128)(2,1)S(1)} %all-to-all-done.l_ref, ...), custom_call_target="tpu_custom_call" | custom-call | flops 12650000384 | tf_op jit(solution)/shard_map/left_side/pallas_call | solution.py:313
  51.3 1.0 %all-to-all-done.1.parts_ref = bf16[8,32,768]{2,1,0:T(8,128)(2,1)S(1)} async-done(((bf16[8,32,768]{2,1,0:T(8,128)(2,1)}), bf16[8,32,768]{2,1,0:T(8,128)(2,1)S(1)}, u32[]{:S(2)}, u32[]{:S(2)}) %all-to-all-start.1) | async-done | bytes 393248 | tf_op jit(solution)/shard_map/all_to_all | solution.py:557
  52.3 16.0 %all_to_all.15.got_ref = bf16[16,80,128]{2,1,0:T(8,128)(2,1)S(1)} all-to-all(bf16[16,80,128]{2,1,0:T(8,128)(2,1)S(1)} %left_side.1), channel_id=1, replica_groups=mesh['grp'=2,'dap'=16] {'dap'}, dimensions={0} | all-to-all | bytes 655360 | tf_op jit(solution)/shard_map/all_to_all | solution.py:561
  68.3 0.9 %owner.1 = (bf16[208,128]{1,0:T(8,128)(2,1)S(1)}, f32[768,256]{1,0:T(8,128)S(1)}) custom-call(bf16[8,32,768]{2,1,0:T(8,128)(2,1)S(1)} %all-to-all-done.1.parts_ref, bf16[16,80,128]{2,1,0:T(8,128)(2,1)S(1)} %all_to_all.15.got_ref, f32[1,768]{1,0:T(1,128)S(1)} %get-tuple-element.42.cover_ref, f32[768,256]{1,0:T(8,128)S(1)} %get-tuple-element.43.unit_ref, ...), custom_call_target="tpu_custom_call" | custom-call | flops 1035000000 | tf_op jit(solution)/shard_map/owner/pallas_call | solution.py:375
  69.2 1.4 %collective-permute-start.6 = (bf16[208,128]{1,0:T(8,128)(2,1)S(1)}, bf16[208,128]{1,0:T(8,128)(2,1)S(1)}, u32[]{:S(2)}, u32[]{:S(2)}) collective-permute-start(bf16[208,128]{1,0:T(8,128)(2,1)S(1)} %get-tuple-element.44.here_ref), channel_id=1, source_target_pairs={{0,8},{1,9},{2,10},{3,11},{4,12},{5,13},{6,14},{7,15},{8,0},{9,1},... | collective-permute-start | bytes 159752 | tf_op jit(solution)/shard_map/ppermute | solution.py:530
  70.7 1.3 %home.1 = bf16[768,256]{1,0:T(8,128)(2,1)} custom-call(f32[768,256]{1,0:T(8,128)S(1)} %get-tuple-element.45.grad_ref, f32[768,256]{1,0:T(8,128)S(1)} %get-tuple-element.43.unit_ref, f32[768,1]{1,0:T(8,128)S(1)} %get-tuple-element.46.inverse_ref, f32[1,256]{1,0:T(1,128)S(1)} %bitcast.21), custom_call_target="tpu_custom_call" | custom-call | flops 1380000000 | tf_op jit(solution)/shard_map/home/pallas_call | solution.py:497
  71.9 3.2 %collective-permute-done.6.there_ref = bf16[208,128]{1,0:T(8,128)(2,1)S(1)} collective-permute-done((bf16[208,128]{1,0:T(8,128)(2,1)S(1)}, bf16[208,128]{1,0:T(8,128)(2,1)S(1)}, u32[]{:S(2)}, u32[]{:S(2)}) %collective-permute-start.6) | collective-permute-done | bytes 53280 | tf_op jit(solution)/shard_map/ppermute | solution.py:530
  75.2 0.1 collective-permute-start.7
  75.2 4.3 %collective-permute-done.7.there_ref = bf16[272,128]{1,0:T(8,128)(2,1)S(1)} collective-permute-done((bf16[272,128]{1,0:T(8,128)(2,1)S(1)}, bf16[272,128]{1,0:T(8,128)(2,1)S(1)}, u32[]{:S(2)}, u32[]{:S(2)}) %collective-permute-start.7) | collective-permute-done | bytes 69664 | tf_op jit(solution)/shard_map/ppermute | solution.py:530
  79.6 0.8 collective-permute-start.8
  80.3 4.0 %collective-permute-done.8.there_ref = bf16[400,128]{1,0:T(8,128)(2,1)S(1)} collective-permute-done((bf16[400,128]{1,0:T(8,128)(2,1)S(1)}, bf16[400,128]{1,0:T(8,128)(2,1)S(1)}, u32[]{:S(2)}, u32[]{:S(2)}) %collective-permute-start.8) | collective-permute-done | bytes 102432 | tf_op jit(solution)/shard_map/ppermute | solution.py:530
  84.3 0.1 collective-permute-start.9
  84.4 1.4 %collective-permute-done.9.there_ref = bf16[656,128]{1,0:T(8,128)(2,1)S(1)} collective-permute-done((bf16[656,128]{1,0:T(8,128)(2,1)S(1)}, bf16[656,128]{1,0:T(8,128)(2,1)S(1)}, u32[]{:S(2)}, u32[]{:S(2)}) %collective-permute-start.9) | collective-permute-done | bytes 167968 | tf_op jit(solution)/shard_map/ppermute | solution.py:530
  85.8 0.9 finish.1
  (24 shorter events, 0.1 us)
Async XLA Ops:
  0.6 10.4 %copy-start.7 = (s32[768]{0:T(1024)S(1)}, s32[768]{0:T(1024)}, u32[]{:S(2)}) copy-start(s32[768]{0:T(1024)} %param.20) | copy-start | bytes 9220
  0.6 10.4 %copy-start.6 = (s32[768]{0:T(1024)S(1)}, s32[768]{0:T(1024)}, u32[]{:S(2)}) copy-start(s32[768]{0:T(1024)} %param.21) | copy-start | bytes 9220
  0.7 14.0 %copy-start.4 = (s32[16]{0:T(128)S(1)}, s32[16]{0:T(128)}, u32[]{:S(2)}) copy-start(s32[16]{0:T(128)} %smask_ref.1) | copy-start | bytes 196
  0.7 14.0 %copy-start.5 = (s32[16]{0:T(128)S(1)}, s32[16]{0:T(128)}, u32[]{:S(2)}) copy-start(s32[16]{0:T(128)} %schain_ref.1) | copy-start | bytes 196
  3.1 8.0 %collective-permute-start = (bf16[1,32,768]{2,1,0:T(8,128)(2,1)S(1)}, bf16[1,32,768]{2,1,0:T(8,128)(2,1)S(1)}, u32[]{:S(2)}, u32[]{:S(2)}) collective-permute-start(bf16[1,32,768]{2,1,0:T(8,128)(2,1)S(1)} %bitcast.11), channel_id=1, source_target_pairs={{0,8},{1,9},{2,10},{3,11},{4,12},{5,13},{6,14},{7,15},{8,0},{9,1},... | collective-permute-start | bytes 147464 | tf_op jit(solution)/shard_map/ppermute | solution.py:530
  7.1 13.3 %all-to-all-start = ((bf16[16,16,128]{2,1,0:T(8,128)(2,1)}), bf16[16,16,128]{2,1,0:T(8,128)(2,1)S(1)}, u32[]{:S(2)}, u32[]{:S(2)}) async-start(bf16[16,16,128]{2,1,0:T(8,128)(2,1)} %get-tuple-element.30), calls=%async_computation | async-start | bytes 131072 | tf_op jit(solution)/shard_map/all_to_all | solution.py:539
  11.1 6.7 %collective-permute-start.1 = (bf16[2,32,768]{2,1,0:T(8,128)(2,1)S(1)}, bf16[2,32,768]{2,1,0:T(8,128)(2,1)S(1)}, u32[]{:S(2)}, u32[]{:S(2)}) collective-permute-start(bf16[2,32,768]{2,1,0:T(8,128)(2,1)S(1)} %stack.2.refs_0_), channel_id=1, source_target_pairs={{0,4},{1,5},{2,6},{3,7},{4,0},{5,1},{6,2},{7,3},{8,12},{9,13},{10,... | collective-permute-start | bytes 294920 | tf_op jit(solution)/shard_map/ppermute | solution.py:530
  13.1 6.0 %collective-permute-start.2 = (bf16[2,32,768]{2,1,0:T(8,128)(2,1)S(1)}, bf16[2,32,768]{2,1,0:T(8,128)(2,1)S(1)}, u32[]{:S(2)}, u32[]{:S(2)}) collective-permute-start(bf16[2,32,768]{2,1,0:T(8,128)(2,1)S(1)} %stack.2.refs_0_), channel_id=1, source_target_pairs={{0,2},{1,3},{2,0},{3,1},{4,6},{5,7},{6,4},{7,5},{8,10},{9,11},{10,... | collective-permute-start | bytes 294920 | tf_op jit(solution)/shard_map/ppermute | solution.py:530
  14.6 5.8 %collective-permute-start.3 = (bf16[2,32,768]{2,1,0:T(8,128)(2,1)S(1)}, bf16[2,32,768]{2,1,0:T(8,128)(2,1)S(1)}, u32[]{:S(2)}, u32[]{:S(2)}) collective-permute-start(bf16[2,32,768]{2,1,0:T(8,128)(2,1)S(1)} %stack.2.refs_0_), channel_id=1, source_target_pairs={{0,6},{1,7},{2,4},{3,5},{4,2},{5,3},{6,0},{7,1},{8,14},{9,15},{10,... | collective-permute-start | bytes 294920 | tf_op jit(solution)/shard_map/ppermute | solution.py:530
  33.7 1.8 %collective-permute-start.5 = (bf16[8,32,768]{2,1,0:T(8,128)(2,1)S(1)}, bf16[8,32,768]{2,1,0:T(8,128)(2,1)S(1)}, u32[]{:S(2)}, u32[]{:S(2)}) collective-permute-start(bf16[8,32,768]{2,1,0:T(8,128)(2,1)S(1)} %get-tuple-element.39), channel_id=1, source_target_pairs={{0,1},{1,0},{2,3},{3,2},{4,5},{5,4},{6,7},{7,6},{8,9},{9,8},{10,11... | collective-permute-start | bytes 1179656 | tf_op jit(solution)/shard_map/ppermute | solution.py:530
  33.7 6.6 %collective-permute-start.4 = (bf16[8,32,768]{2,1,0:T(8,128)(2,1)S(1)}, bf16[8,32,768]{2,1,0:T(8,128)(2,1)S(1)}, u32[]{:S(2)}, u32[]{:S(2)}) collective-permute-start(bf16[8,32,768]{2,1,0:T(8,128)(2,1)S(1)} %stack.3.here_ref), channel_id=1, source_target_pairs={{0,1},{1,0},{2,3},{3,2},{4,5},{5,4},{6,7},{7,6},{8,9},{9,8},{10,11... | collective-permute-start | bytes 1179656 | tf_op jit(solution)/shard_map/ppermute | solution.py:530
  36.3 16.0 %all-to-all-start.1 = ((bf16[8,32,768]{2,1,0:T(8,128)(2,1)}), bf16[8,32,768]{2,1,0:T(8,128)(2,1)S(1)}, u32[]{:S(2)}, u32[]{:S(2)}) async-start(bf16[8,32,768]{2,1,0:T(8,128)(2,1)} %pair_sum.1), calls=%async_computation.1 | async-start | bytes 786432 | tf_op jit(solution)/shard_map/all_to_all | solution.py:557
  40.3 28.0 %copy-start = (bf16[256,32]{0,1:T(8,128)(2,1)S(1)}, bf16[256,32]{0,1:T(8,128)(2,1)}, u32[]{:S(2)}) copy-start(bf16[256,32]{0,1:T(8,128)(2,1)} %param.14) | copy-start | bytes 49156
  40.3 28.0 %copy-start.1 = (bf16[256,32]{0,1:T(8,128)(2,1)S(1)}, bf16[256,32]{0,1:T(8,128)(2,1)}, u32[]{:S(2)}) copy-start(bf16[256,32]{0,1:T(8,128)(2,1)} %param.15) | copy-start | bytes 49156
  40.3 28.0 %copy-start.2 = (f32[256]{0:T(256)S(1)}, f32[256]{0:T(256)}, u32[]{:S(2)}) copy-start(f32[256]{0:T(256)} %param.13) | copy-start | bytes 3076
  40.3 28.0 %copy-start.3 = (f32[256]{0:T(256)S(1)}, f32[256]{0:T(256)}, u32[]{:S(2)}) copy-start(f32[256]{0:T(256)} %param.12) | copy-start | bytes 3076
  69.2 5.9 %collective-permute-start.6 = (bf16[208,128]{1,0:T(8,128)(2,1)S(1)}, bf16[208,128]{1,0:T(8,128)(2,1)S(1)}, u32[]{:S(2)}, u32[]{:S(2)}) collective-permute-start(bf16[208,128]{1,0:T(8,128)(2,1)S(1)} %get-tuple-element.44.here_ref), channel_id=1, source_target_pairs={{0,8},{1,9},{2,10},{3,11},{4,12},{5,13},{6,14},{7,15},{8,0},{9,1},... | collective-permute-start | bytes 159752 | tf_op jit(solution)/shard_map/ppermute | solution.py:530
  75.2 4.4 %collective-permute-start.7 = (bf16[272,128]{1,0:T(8,128)(2,1)S(1)}, bf16[272,128]{1,0:T(8,128)(2,1)S(1)}, u32[]{:S(2)}, u32[]{:S(2)}) collective-permute-start(bf16[272,128]{1,0:T(8,128)(2,1)S(1)} %join.3.here_ref), channel_id=1, source_target_pairs={{0,4},{1,5},{2,6},{3,7},{4,0},{5,1},{6,2},{7,3},{8,12},{9,13},{10,... | collective-permute-start | bytes 208904 | tf_op jit(solution)/shard_map/ppermute | solution.py:530
  79.6 4.7 %collective-permute-start.8 = (bf16[400,128]{1,0:T(8,128)(2,1)S(1)}, bf16[400,128]{1,0:T(8,128)(2,1)S(1)}, u32[]{:S(2)}, u32[]{:S(2)}) collective-permute-start(bf16[400,128]{1,0:T(8,128)(2,1)S(1)} %join.4.here_ref), channel_id=1, source_target_pairs={{0,2},{1,3},{2,0},{3,1},{4,6},{5,7},{6,4},{7,5},{8,10},{9,11},{10,... | collective-permute-start | bytes 307208 | tf_op jit(solution)/shard_map/ppermute | solution.py:530
  84.3 1.5 %collective-permute-start.9 = (bf16[656,128]{1,0:T(8,128)(2,1)S(1)}, bf16[656,128]{1,0:T(8,128)(2,1)S(1)}, u32[]{:S(2)}, u32[]{:S(2)}) collective-permute-start(bf16[656,128]{1,0:T(8,128)(2,1)S(1)} %join.5.here_ref), channel_id=1, source_target_pairs={{0,1},{1,0},{2,3},{3,2},{4,5},{5,4},{6,7},{7,6},{8,9},{9,8},{10,11... | collective-permute-start | bytes 503816 | tf_op jit(solution)/shard_map/ppermute | solution.py:530

commit v4 on v3

--- a/solution.py
+++ b/solution.py
@@ -190,8 +190,6 @@
 
     order_left(z, l_ref, own_ref, ordered)
     left = ordered[...].astype(BF16)
-    fetch(0).wait()
-    scale(0)
     group = 8
     for first in range(0, z.width, group):
         part = mm(left, w_ref[:, first * pair : (first + group) * pair]).astype(BF16)
@@ -200,6 +198,8 @@
                 mixed[(first + e) * seqs : (first + e + 1) * seqs, i * pair : (i + 1) * pair] = part[
                     i * seqs : (i + 1) * seqs, e * pair : (e + 1) * pair
                 ]
+    fetch(0).wait()
+    scale(0)
     store(0).start()
 
     for step in range(z.blocks):
@@ -424,24 +424,28 @@
     )(here, there)
 
 
-def join_kernel(z, here_ref, there_ref, out_ref):
-    top, more = z.sum_rows, here_ref.shape[0] - z.sum_rows
-    out_ref[:top, :] = (here_ref[:top, :].astype(F32) + there_ref[:top, :].astype(F32)).astype(BF16)
-    out_ref[top : top + more, :] = here_ref[top:, :]
-    out_ref[top + more :, :] = there_ref[top:, :]
-
-
-def join(z, here, there):
-    rows = 2 * here.shape[0] - z.sum_rows
+def join_kernel(z, *refs):
+    *parts, out_ref = refs
+    top, more = z.sum_rows, parts[0].shape[0] - z.sum_rows
+    sums = [ref[:top, :].astype(F32) for ref in parts]
+    while len(sums) > 1:
+        sums = [one + two for one, two in zip(sums[::2], sums[1::2])]
+    out_ref[:top, :] = sums[0].astype(BF16)
+    for p, ref in enumerate(parts):
+        out_ref[top + p * more : top + (p + 1) * more, :] = ref[top:, :]
+
+
+def join(z, *parts):
+    rows = z.sum_rows + len(parts) * (parts[0].shape[0] - z.sum_rows)
     return pl.pallas_call(
         functools.partial(join_kernel, z),
         out_shape=sds((rows, LANES), BF16),
-        in_specs=[VMEM, VMEM],
+        in_specs=[VMEM] * len(parts),
         out_specs=VMEM,
         compiler_params=params(8),
         cost_estimate=cost(0.4),
         name="join",
-    )(here, there)
+    )(*parts)
 
 
 def finish_kernel(z, here_ref, there_ref, lw_ref, rw_ref, gain_ref, bias_ref, out_ref):
@@ -562,11 +566,12 @@
 
     sums, grad = owner(z, parts, got, own_sequence, unit, gain, bias, lwt, rwt)
     alignment_gradient = home(z, grad, unit, inverse, gain)
-    there = swap_with(sums, z.masks[0])
-    there, alignment_gradient = lax.optimization_barrier((there, alignment_gradient))
-    sums = join(z, sums, there)
-    for bit in z.masks[1:-1]:
-        sums = join(z, sums, swap_with(sums, bit))
+    for step, bit in enumerate(z.masks[:-3]):
+        there = swap_with(sums, bit)
+        if step == 0:
+            there, alignment_gradient = lax.optimization_barrier((there, alignment_gradient))
+        sums = join(z, sums, there)
+    sums = join(z, sums, *[swap_with(sums, bit) for bit in (one, two, one ^ two)])
     lw_grad, rw_grad, gain_grad, bias_grad, out_grad = finish(z, sums, swap_with(sums, z.masks[-1]))
     return (
         alignment_gradient.reshape(alignment_rows.shape),

time: 87 us -> 83.4 us (0.959)
  waiting for transfers between devices: 19.4 us -> 13.6 us
  starting transfers between devices: 18.4 us -> 21.1 us
    ppermute x10 -> x11, waiting for transfers between devices: 18.4 us -> 12.6 us  [swap_with(): return lax.ppermute(value, AXIS, [(d, d ^ bit) for d in range(size)])]
    ppermute x10 -> x11, starting transfers between devices: 10.5 us -> 13.2 us  [swap_with(): return lax.ppermute(value, AXIS, [(d, d ^ bit) for d in range(size)])]
  transfers between devices with their start and end apart: 12 -> 13, of which waited for: 9 -> 9; matrix products, arithmetic and copies ran while one was open for 0% -> 0% of each run, Pallas kernels for 17% -> 17%
where the time goes in v4:
time: 83.4 us; the launch traced here: 83 us
  Pallas kernels  31.4 us (38%)
  starting transfers between devices  21.1 us (25%)
  blocking collectives  16 us (19%)
  waiting for transfers between devices  13.6 us (16%)
  between operations  0.84 us (1%)
    all_to_all x1, blocking collectives, on_device(): got = lax.all_to_all(shares, AXIS, 0, 0, tiled=True)  16 us
    ppermute x11, starting transfers between devices, swap_with(): return lax.ppermute(value, AXIS, [(d, d ^ bit) for d in range(size)])  13.2 us
    pallas_call x1, Pallas kernels, right_sum(): pl.pallas_call(functools.partial(right_sum_kernel, z), out_shape=(sds(out...  12.7 us
    ppermute x11, waiting for transfers between devices, swap_with(): return lax.ppermute(value, AXIS, [(d, d ^ bit) for d in range(size)])  12.6 us
    pallas_call x1, Pallas kernels, left_side(): pl.pallas_call(functools.partial(left_side_kernel, z), out_shape=sds((z.s...  10.9 us
    all_to_all x1, starting transfers between devices, on_device(): lax.all_to_all(of_chip, AXIS, 0, 0, tiled=True, axis_index_groups=same_core)  4.01 us
    all_to_all x1, starting transfers between devices, on_device(): left_all = lax.all_to_all(left, AXIS, 0, 0, tiled=True)  3.91 us
    pallas_call x1, Pallas kernels, project(): pl.pallas_call(functools.partial(project_kernel, z), out_shape=(sds((z.si...  2.4 us
  transfers between devices with their start and end apart: 13, of which 9 were waited for; matrix products, arithmetic and copies ran while one was open for 0% of the time, Pallas kernels for 17%

profile of v4, /device:TPU:0, one launch (start us, length us, event | category | flops | bytes accessed | tf_op | source)
XLA Modules:
  0.0 83.0 jit_solution(11831918178819683979)
XLA Ops:
  0.7 2.4 %project.1 = (bf16[16,16,128]{2,1,0:T(8,128)(2,1)}, bf16[32,768]{1,0:T(8,128)(2,1)S(1)}, f32[768,256]{1,0:T(8,128)S(1)}, f32[768,1]{1,0:T(8,128)S(1)}) custom-call(bf16[768,256]{1,0:T(8,128)(2,1)} %bitcast.22, f32[1,256]{1,0:T(1,128)} %bitcast.19, f32[1,256]{1,0:T(1,128)} %bitcast.17, bf16[32,256]{1,0:T(8,128)(2,1)} %bitcast.13, bf16[32,256]{1,0:T(8,128)(2,1)} %bitcast.15), custom_call_target="tpu_custom_call" | custom-call | flops 2760000000 | tf_op jit(solution)/shard_map/project/pallas_call | solution.py:96
  3.1 4.0 %collective-permute-start = (bf16[1,32,768]{2,1,0:T(8,128)(2,1)S(1)}, bf16[1,32,768]{2,1,0:T(8,128)(2,1)S(1)}, u32[]{:S(2)}, u32[]{:S(2)}) collective-permute-start(bf16[1,32,768]{2,1,0:T(8,128)(2,1)S(1)} %bitcast.11), channel_id=1, source_target_pairs={{0,8},{1,9},{2,10},{3,11},{4,12},{5,13},{6,14},{7,15},{8,0},{9,1},... | collective-permute-start | bytes 147464 | tf_op jit(solution)/shard_map/ppermute | solution.py:534
  7.1 3.9 %all-to-all-start = ((bf16[16,16,128]{2,1,0:T(8,128)(2,1)}), bf16[16,16,128]{2,1,0:T(8,128)(2,1)S(1)}, u32[]{:S(2)}, u32[]{:S(2)}) async-start(bf16[16,16,128]{2,1,0:T(8,128)(2,1)} %get-tuple-element.30), calls=%async_computation | async-start | bytes 131072 | tf_op jit(solution)/shard_map/all_to_all | solution.py:543
  11.1 2.0 %collective-permute-start.1 = (bf16[2,32,768]{2,1,0:T(8,128)(2,1)S(1)}, bf16[2,32,768]{2,1,0:T(8,128)(2,1)S(1)}, u32[]{:S(2)}, u32[]{:S(2)}) collective-permute-start(bf16[2,32,768]{2,1,0:T(8,128)(2,1)S(1)} %stack.2.refs_0_), channel_id=1, source_target_pairs={{0,4},{1,5},{2,6},{3,7},{4,0},{5,1},{6,2},{7,3},{8,12},{9,13},{10,... | collective-permute-start | bytes 294920 | tf_op jit(solution)/shard_map/ppermute | solution.py:534
  13.1 1.5 %collective-permute-start.2 = (bf16[2,32,768]{2,1,0:T(8,128)(2,1)S(1)}, bf16[2,32,768]{2,1,0:T(8,128)(2,1)S(1)}, u32[]{:S(2)}, u32[]{:S(2)}) collective-permute-start(bf16[2,32,768]{2,1,0:T(8,128)(2,1)S(1)} %stack.2.refs_0_), channel_id=1, source_target_pairs={{0,2},{1,3},{2,0},{3,1},{4,6},{5,7},{6,4},{7,5},{8,10},{9,11},{10,... | collective-permute-start | bytes 294920 | tf_op jit(solution)/shard_map/ppermute | solution.py:534
  14.6 0.1 collective-permute-start.3
  14.7 1.4 %cover.1 = (f32[16,768]{1,0:T(8,128)S(1)}, f32[48,16]{1,0:T(8,128)S(1)}, f32[1,768]{1,0:T(1,128)S(1)}, bf16[32,4096]{1,0:T(8,128)(2,1)S(1)}) custom-call(s32[16]{0:T(128)S(1)} %copy-done.4, s32[16]{0:T(128)S(1)} %copy-done.5, s32[1,768]{1,0:T(1,128)S(1)} %reshape.36.code_ref, bf16[1024,128]{1,0:T(8,128)(2,1)} %w_ref.1), custom_call_target="tpu_custom_call" | custom-call | flops 1610000000 | tf_op jit(solution)/shard_map/cover/pallas_call | solution.py:136
  16.1 1.7 %collective-permute-done.1.refs_1_ = bf16[2,32,768]{2,1,0:T(8,128)(2,1)S(1)} collective-permute-done((bf16[2,32,768]{2,1,0:T(8,128)(2,1)S(1)}, bf16[2,32,768]{2,1,0:T(8,128)(2,1)S(1)}, u32[]{:S(2)}, u32[]{:S(2)}) %collective-permute-start.1) | collective-permute-done | bytes 98336 | tf_op jit(solution)/shard_map/ppermute | solution.py:534
  17.8 1.3 %collective-permute-done.2.refs_2_ = bf16[2,32,768]{2,1,0:T(8,128)(2,1)S(1)} collective-permute-done((bf16[2,32,768]{2,1,0:T(8,128)(2,1)S(1)}, bf16[2,32,768]{2,1,0:T(8,128)(2,1)S(1)}, u32[]{:S(2)}, u32[]{:S(2)}) %collective-permute-start.2) | collective-permute-done | bytes 98336 | tf_op jit(solution)/shard_map/ppermute | solution.py:534
  19.0 1.3 %collective-permute-done.3.refs_3_ = bf16[2,32,768]{2,1,0:T(8,128)(2,1)S(1)} collective-permute-done((bf16[2,32,768]{2,1,0:T(8,128)(2,1)S(1)}, bf16[2,32,768]{2,1,0:T(8,128)(2,1)S(1)}, u32[]{:S(2)}, u32[]{:S(2)}) %collective-permute-start.3) | collective-permute-done | bytes 98336 | tf_op jit(solution)/shard_map/ppermute | solution.py:534
  20.4 12.7 %right_sum.1 = (bf16[8,32,768]{2,1,0:T(8,128)(2,1)S(1)}, bf16[8,32,768]{2,1,0:T(8,128)(2,1)S(1)}, bf16[768,6144]{1,0:T(8,128)(2,1)}) custom-call(bf16[16,16,128]{2,1,0:T(8,128)(2,1)S(1)} %all-to-all-done.l_ref, f32[48,16]{1,0:T(8,128)S(1)} %get-tuple-element.35.own_ref, f32[16,768]{1,0:T(8,128)S(1)} %get-tuple-element.33.cover_ref, ...), custom_call_target="tpu_custom_call" | custom-call | flops 14949999616 | tf_op jit(solution)/shard_map/right_sum/pallas_call | solution.py:229
  33.1 0.1 collective-permute-start.5
  33.2 0.5 collective-permute-start.4
  33.7 1.2 %collective-permute-done.5.there_ref = bf16[8,32,768]{2,1,0:T(8,128)(2,1)S(1)} collective-permute-done((bf16[8,32,768]{2,1,0:T(8,128)(2,1)S(1)}, bf16[8,32,768]{2,1,0:T(8,128)(2,1)S(1)}, u32[]{:S(2)}, u32[]{:S(2)}) %collective-permute-start.5) | collective-permute-done | bytes 393248 | tf_op jit(solution)/shard_map/ppermute | solution.py:534
  34.9 0.8 %pair_sum.1 = bf16[8,32,768]{2,1,0:T(8,128)(2,1)} custom-call(bf16[8,32,768]{2,1,0:T(8,128)(2,1)S(1)} %get-tuple-element.38.here_ref, bf16[8,32,768]{2,1,0:T(8,128)(2,1)S(1)} %collective-permute-done.5.there_ref), custom_call_target="tpu_custom_call" | custom-call | flops 920000000 | tf_op jit(solution)/shard_map/pair_sum/pallas_call | solution.py:416
  35.7 4.0 %all-to-all-start.1 = ((bf16[8,32,768]{2,1,0:T(8,128)(2,1)}), bf16[8,32,768]{2,1,0:T(8,128)(2,1)S(1)}, u32[]{:S(2)}, u32[]{:S(2)}) async-start(bf16[8,32,768]{2,1,0:T(8,128)(2,1)} %pair_sum.1), calls=%async_computation.1 | async-start | bytes 786432 | tf_op jit(solution)/shard_map/all_to_all | solution.py:561
  39.8 0.0 copy-start.1
  39.8 10.9 %left_side.1 = bf16[16,80,128]{2,1,0:T(8,128)(2,1)S(1)} custom-call(bf16[8,32,768]{2,1,0:T(8,128)(2,1)S(1)} %stack.3.here_ref, bf16[8,32,768]{2,1,0:T(8,128)(2,1)S(1)} %collective-permute-done.4.there_ref, f32[16,768]{1,0:T(8,128)S(1)} %get-tuple-element.33.cover_ref, bf16[16,16,128]{2,1,0:T(8,128)(2,1)S(1)} %all-to-all-done.l_ref, ...), custom_call_target="tpu_custom_call" | custom-call | flops 12650000384 | tf_op jit(solution)/shard_map/left_side/pallas_call | solution.py:313
  50.7 1.0 %all-to-all-done.1.parts_ref = bf16[8,32,768]{2,1,0:T(8,128)(2,1)S(1)} async-done(((bf16[8,32,768]{2,1,0:T(8,128)(2,1)}), bf16[8,32,768]{2,1,0:T(8,128)(2,1)S(1)}, u32[]{:S(2)}, u32[]{:S(2)}) %all-to-all-start.1) | async-done | bytes 393248 | tf_op jit(solution)/shard_map/all_to_all | solution.py:561
  51.7 16.0 %all_to_all.15.got_ref = bf16[16,80,128]{2,1,0:T(8,128)(2,1)S(1)} all-to-all(bf16[16,80,128]{2,1,0:T(8,128)(2,1)S(1)} %left_side.1), channel_id=1, replica_groups=mesh['grp'=2,'dap'=16] {'dap'}, dimensions={0} | all-to-all | bytes 655360 | tf_op jit(solution)/shard_map/all_to_all | solution.py:565
  67.7 0.9 %owner.1 = (bf16[208,128]{1,0:T(8,128)(2,1)S(1)}, f32[768,256]{1,0:T(8,128)S(1)}) custom-call(bf16[8,32,768]{2,1,0:T(8,128)(2,1)S(1)} %all-to-all-done.1.parts_ref, bf16[16,80,128]{2,1,0:T(8,128)(2,1)S(1)} %all_to_all.15.got_ref, f32[1,768]{1,0:T(1,128)S(1)} %get-tuple-element.42.cover_ref, f32[768,256]{1,0:T(8,128)S(1)} %get-tuple-element.43.unit_ref, ...), custom_call_target="tpu_custom_call" | custom-call | flops 1035000000 | tf_op jit(solution)/shard_map/owner/pallas_call | solution.py:375
  68.7 1.4 %collective-permute-start.6 = (bf16[208,128]{1,0:T(8,128)(2,1)S(1)}, bf16[208,128]{1,0:T(8,128)(2,1)S(1)}, u32[]{:S(2)}, u32[]{:S(2)}) collective-permute-start(bf16[208,128]{1,0:T(8,128)(2,1)S(1)} %get-tuple-element.44.refs_0_), channel_id=1, source_target_pairs={{0,8},{1,9},{2,10},{3,11},{4,12},{5,13},{6,14},{7,15},{8,0},{9,1},... | collective-permute-start | bytes 159752 | tf_op jit(solution)/shard_map/ppermute | solution.py:534
  70.1 1.3 %home.1 = bf16[768,256]{1,0:T(8,128)(2,1)} custom-call(f32[768,256]{1,0:T(8,128)S(1)} %get-tuple-element.45.grad_ref, f32[768,256]{1,0:T(8,128)S(1)} %get-tuple-element.43.unit_ref, f32[768,1]{1,0:T(8,128)S(1)} %get-tuple-element.46.inverse_ref, f32[1,256]{1,0:T(1,128)S(1)} %bitcast.21), custom_call_target="tpu_custom_call" | custom-call | flops 1380000000 | tf_op jit(solution)/shard_map/home/pallas_call | solution.py:501
  71.4 3.2 %collective-permute-done.6.refs_1_ = bf16[208,128]{1,0:T(8,128)(2,1)S(1)} collective-permute-done((bf16[208,128]{1,0:T(8,128)(2,1)S(1)}, bf16[208,128]{1,0:T(8,128)(2,1)S(1)}, u32[]{:S(2)}, u32[]{:S(2)}) %collective-permute-start.6) | collective-permute-done | bytes 53280 | tf_op jit(solution)/shard_map/ppermute | solution.py:534
  74.6 0.1 collective-permute-start.7
  74.7 0.8 collective-permute-start.8
  75.4 2.7 %collective-permute-start.9 = (bf16[272,128]{1,0:T(8,128)(2,1)S(1)}, bf16[272,128]{1,0:T(8,128)(2,1)S(1)}, u32[]{:S(2)}, u32[]{:S(2)}) collective-permute-start(bf16[272,128]{1,0:T(8,128)(2,1)S(1)} %join.2.refs_0_), channel_id=1, source_target_pairs={{0,6},{1,7},{2,4},{3,5},{4,2},{5,3},{6,0},{7,1},{8,14},{9,15},{10,... | collective-permute-start | bytes 208904 | tf_op jit(solution)/shard_map/ppermute | solution.py:534
  78.2 1.6 %collective-permute-done.7.refs_1_ = bf16[272,128]{1,0:T(8,128)(2,1)S(1)} collective-permute-done((bf16[272,128]{1,0:T(8,128)(2,1)S(1)}, bf16[272,128]{1,0:T(8,128)(2,1)S(1)}, u32[]{:S(2)}, u32[]{:S(2)}) %collective-permute-start.7) | collective-permute-done | bytes 69664 | tf_op jit(solution)/shard_map/ppermute | solution.py:534
  79.7 0.9 %collective-permute-done.9.refs_3_ = bf16[272,128]{1,0:T(8,128)(2,1)S(1)} collective-permute-done((bf16[272,128]{1,0:T(8,128)(2,1)S(1)}, bf16[272,128]{1,0:T(8,128)(2,1)S(1)}, u32[]{:S(2)}, u32[]{:S(2)}) %collective-permute-start.9) | collective-permute-done | bytes 69664 | tf_op jit(solution)/shard_map/ppermute | solution.py:534
  80.7 0.1 collective-permute-start.10
  80.7 1.4 %collective-permute-done.10.there_ref = bf16[656,128]{1,0:T(8,128)(2,1)S(1)} collective-permute-done((bf16[656,128]{1,0:T(8,128)(2,1)S(1)}, bf16[656,128]{1,0:T(8,128)(2,1)S(1)}, u32[]{:S(2)}, u32[]{:S(2)}) %collective-permute-start.10) | collective-permute-done | bytes 167968 | tf_op jit(solution)/shard_map/ppermute | solution.py:534
  82.1 0.9 %finish.1 = (f32[32,256]{1,0:T(8,128)}, f32[32,256]{1,0:T(8,128)}, f32[1,256]{1,0:T(1,128)}, f32[1,256]{1,0:T(1,128)}, f32[1024,128]{1,0:T(8,128)}) custom-call(bf16[656,128]{1,0:T(8,128)(2,1)S(1)} %join.3.here_ref, bf16[656,128]{1,0:T(8,128)(2,1)S(1)} %collective-permute-done.10.there_ref), custom_call_target="tpu_custom_call" | custom-call | flops 1035000000 | tf_op jit(solution)/shard_map/finish/pallas_call | solution.py:470
  (25 shorter events, 0.1 us)
Async XLA Ops:
  0.6 10.4 %copy-start.7 = (s32[768]{0:T(1024)S(1)}, s32[768]{0:T(1024)}, u32[]{:S(2)}) copy-start(s32[768]{0:T(1024)} %param.20) | copy-start | bytes 9220
  0.6 10.4 %copy-start.6 = (s32[768]{0:T(1024)S(1)}, s32[768]{0:T(1024)}, u32[]{:S(2)}) copy-start(s32[768]{0:T(1024)} %param.21) | copy-start | bytes 9220
  0.7 14.0 %copy-start.4 = (s32[16]{0:T(128)S(1)}, s32[16]{0:T(128)}, u32[]{:S(2)}) copy-start(s32[16]{0:T(128)} %smask_ref.1) | copy-start | bytes 196
  0.7 14.0 %copy-start.5 = (s32[16]{0:T(128)S(1)}, s32[16]{0:T(128)}, u32[]{:S(2)}) copy-start(s32[16]{0:T(128)} %schain_ref.1) | copy-start | bytes 196
  3.1 8.0 %collective-permute-start = (bf16[1,32,768]{2,1,0:T(8,128)(2,1)S(1)}, bf16[1,32,768]{2,1,0:T(8,128)(2,1)S(1)}, u32[]{:S(2)}, u32[]{:S(2)}) collective-permute-start(bf16[1,32,768]{2,1,0:T(8,128)(2,1)S(1)} %bitcast.11), channel_id=1, source_target_pairs={{0,8},{1,9},{2,10},{3,11},{4,12},{5,13},{6,14},{7,15},{8,0},{9,1},... | collective-permute-start | bytes 147464 | tf_op jit(solution)/shard_map/ppermute | solution.py:534
  7.1 13.3 %all-to-all-start = ((bf16[16,16,128]{2,1,0:T(8,128)(2,1)}), bf16[16,16,128]{2,1,0:T(8,128)(2,1)S(1)}, u32[]{:S(2)}, u32[]{:S(2)}) async-start(bf16[16,16,128]{2,1,0:T(8,128)(2,1)} %get-tuple-element.30), calls=%async_computation | async-start | bytes 131072 | tf_op jit(solution)/shard_map/all_to_all | solution.py:543
  11.1 6.7 %collective-permute-start.1 = (bf16[2,32,768]{2,1,0:T(8,128)(2,1)S(1)}, bf16[2,32,768]{2,1,0:T(8,128)(2,1)S(1)}, u32[]{:S(2)}, u32[]{:S(2)}) collective-permute-start(bf16[2,32,768]{2,1,0:T(8,128)(2,1)S(1)} %stack.2.refs_0_), channel_id=1, source_target_pairs={{0,4},{1,5},{2,6},{3,7},{4,0},{5,1},{6,2},{7,3},{8,12},{9,13},{10,... | collective-permute-start | bytes 294920 | tf_op jit(solution)/shard_map/ppermute | solution.py:534
  13.1 6.0 %collective-permute-start.2 = (bf16[2,32,768]{2,1,0:T(8,128)(2,1)S(1)}, bf16[2,32,768]{2,1,0:T(8,128)(2,1)S(1)}, u32[]{:S(2)}, u32[]{:S(2)}) collective-permute-start(bf16[2,32,768]{2,1,0:T(8,128)(2,1)S(1)} %stack.2.refs_0_), channel_id=1, source_target_pairs={{0,2},{1,3},{2,0},{3,1},{4,6},{5,7},{6,4},{7,5},{8,10},{9,11},{10,... | collective-permute-start | bytes 294920 | tf_op jit(solution)/shard_map/ppermute | solution.py:534
  14.6 5.8 %collective-permute-start.3 = (bf16[2,32,768]{2,1,0:T(8,128)(2,1)S(1)}, bf16[2,32,768]{2,1,0:T(8,128)(2,1)S(1)}, u32[]{:S(2)}, u32[]{:S(2)}) collective-permute-start(bf16[2,32,768]{2,1,0:T(8,128)(2,1)S(1)} %stack.2.refs_0_), channel_id=1, source_target_pairs={{0,6},{1,7},{2,4},{3,5},{4,2},{5,3},{6,0},{7,1},{8,14},{9,15},{10,... | collective-permute-start | bytes 294920 | tf_op jit(solution)/shard_map/ppermute | solution.py:534
  33.1 1.8 %collective-permute-start.5 = (bf16[8,32,768]{2,1,0:T(8,128)(2,1)S(1)}, bf16[8,32,768]{2,1,0:T(8,128)(2,1)S(1)}, u32[]{:S(2)}, u32[]{:S(2)}) collective-permute-start(bf16[8,32,768]{2,1,0:T(8,128)(2,1)S(1)} %get-tuple-element.39), channel_id=1, source_target_pairs={{0,1},{1,0},{2,3},{3,2},{4,5},{5,4},{6,7},{7,6},{8,9},{9,8},{10,11... | collective-permute-start | bytes 1179656 | tf_op jit(solution)/shard_map/ppermute | solution.py:534
  33.2 6.6 %collective-permute-start.4 = (bf16[8,32,768]{2,1,0:T(8,128)(2,1)S(1)}, bf16[8,32,768]{2,1,0:T(8,128)(2,1)S(1)}, u32[]{:S(2)}, u32[]{:S(2)}) collective-permute-start(bf16[8,32,768]{2,1,0:T(8,128)(2,1)S(1)} %stack.3.here_ref), channel_id=1, source_target_pairs={{0,1},{1,0},{2,3},{3,2},{4,5},{5,4},{6,7},{7,6},{8,9},{9,8},{10,11... | collective-permute-start | bytes 1179656 | tf_op jit(solution)/shard_map/ppermute | solution.py:534
  35.7 16.0 %all-to-all-start.1 = ((bf16[8,32,768]{2,1,0:T(8,128)(2,1)}), bf16[8,32,768]{2,1,0:T(8,128)(2,1)S(1)}, u32[]{:S(2)}, u32[]{:S(2)}) async-start(bf16[8,32,768]{2,1,0:T(8,128)(2,1)} %pair_sum.1), calls=%async_computation.1 | async-start | bytes 786432 | tf_op jit(solution)/shard_map/all_to_all | solution.py:561
  39.7 28.0 %copy-start = (bf16[256,32]{0,1:T(8,128)(2,1)S(1)}, bf16[256,32]{0,1:T(8,128)(2,1)}, u32[]{:S(2)}) copy-start(bf16[256,32]{0,1:T(8,128)(2,1)} %param.14) | copy-start | bytes 49156
  39.8 28.0 %copy-start.1 = (bf16[256,32]{0,1:T(8,128)(2,1)S(1)}, bf16[256,32]{0,1:T(8,128)(2,1)}, u32[]{:S(2)}) copy-start(bf16[256,32]{0,1:T(8,128)(2,1)} %param.15) | copy-start | bytes 49156
  39.8 28.0 %copy-start.2 = (f32[256]{0:T(256)S(1)}, f32[256]{0:T(256)}, u32[]{:S(2)}) copy-start(f32[256]{0:T(256)} %param.13) | copy-start | bytes 3076
  39.8 27.9 %copy-start.3 = (f32[256]{0:T(256)S(1)}, f32[256]{0:T(256)}, u32[]{:S(2)}) copy-start(f32[256]{0:T(256)} %param.12) | copy-start | bytes 3076
  68.7 5.9 %collective-permute-start.6 = (bf16[208,128]{1,0:T(8,128)(2,1)S(1)}, bf16[208,128]{1,0:T(8,128)(2,1)S(1)}, u32[]{:S(2)}, u32[]{:S(2)}) collective-permute-start(bf16[208,128]{1,0:T(8,128)(2,1)S(1)} %get-tuple-element.44.refs_0_), channel_id=1, source_target_pairs={{0,8},{1,9},{2,10},{3,11},{4,12},{5,13},{6,14},{7,15},{8,0},{9,1},... | collective-permute-start | bytes 159752 | tf_op jit(solution)/shard_map/ppermute | solution.py:534
  74.6 5.1 %collective-permute-start.7 = (bf16[272,128]{1,0:T(8,128)(2,1)S(1)}, bf16[272,128]{1,0:T(8,128)(2,1)S(1)}, u32[]{:S(2)}, u32[]{:S(2)}) collective-permute-start(bf16[272,128]{1,0:T(8,128)(2,1)S(1)} %join.2.refs_0_), channel_id=1, source_target_pairs={{0,4},{1,5},{2,6},{3,7},{4,0},{5,1},{6,2},{7,3},{8,12},{9,13},{10,... | collective-permute-start | bytes 208904 | tf_op jit(solution)/shard_map/ppermute | solution.py:534
  74.7 5.0 %collective-permute-start.8 = (bf16[272,128]{1,0:T(8,128)(2,1)S(1)}, bf16[272,128]{1,0:T(8,128)(2,1)S(1)}, u32[]{:S(2)}, u32[]{:S(2)}) collective-permute-start(bf16[272,128]{1,0:T(8,128)(2,1)S(1)} %join.2.refs_0_), channel_id=1, source_target_pairs={{0,2},{1,3},{2,0},{3,1},{4,6},{5,7},{6,4},{7,5},{8,10},{9,11},{10,... | collective-permute-start | bytes 208904 | tf_op jit(solution)/shard_map/ppermute | solution.py:534
  75.4 5.2 %collective-permute-start.9 = (bf16[272,128]{1,0:T(8,128)(2,1)S(1)}, bf16[272,128]{1,0:T(8,128)(2,1)S(1)}, u32[]{:S(2)}, u32[]{:S(2)}) collective-permute-start(bf16[272,128]{1,0:T(8,128)(2,1)S(1)} %join.2.refs_0_), channel_id=1, source_target_pairs={{0,6},{1,7},{2,4},{3,5},{4,2},{5,3},{6,0},{7,1},{8,14},{9,15},{10,... | collective-permute-start | bytes 208904 | tf_op jit(solution)/shard_map/ppermute | solution.py:534
  80.7 1.5 %collective-permute-start.10 = (bf16[656,128]{1,0:T(8,128)(2,1)S(1)}, bf16[656,128]{1,0:T(8,128)(2,1)S(1)}, u32[]{:S(2)}, u32[]{:S(2)}) collective-permute-start(bf16[656,128]{1,0:T(8,128)(2,1)S(1)} %join.3.here_ref), channel_id=1, source_target_pairs={{0,1},{1,0},{2,3},{3,2},{4,5},{5,4},{6,7},{7,6},{8,9},{9,8},{10,11... | collective-permute-start | bytes 503816 | tf_op jit(solution)/shard_map/ppermute | solution.py:534

commit v5 on v4

--- a/solution.py
+++ b/solution.py
@@ -29,6 +29,10 @@
 
 def params(mib):
     return pltpu.CompilerParams(vmem_limit_bytes=mib * MIB)
+
+
+def in_vmem(value):
+    return pltpu.with_memory_space_constraint(value, pltpu.VMEM)
 
 
 def cost(microseconds):
@@ -164,30 +168,8 @@
     return pl.ds(pl.multiple_of(step * size, size), size)
 
 
-def right_sum_kernel(z, l_ref, own_ref, cover_ref, w_ref, g_ref, keep_ref, give_ref, scaled_ref,
-                     ordered, mixed, total, raw, here, arrived, left_for):
-    core = lax.axis_index(AXIS) % 2
-    seqs, pair, block = z.seqs, z.pair, z.block
-
-    def fetch(step):
-        at = pl.ds(step * block, block)
-        return pltpu.make_async_copy(g_ref.at[at], raw.at[at], arrived.at[step])
-
-    def store(step):
-        span = slice(step * block * pair, (step + 1) * block * pair)
-        return pltpu.make_async_copy(here.at[:, span], scaled_ref.at[:, span], left_for.at[step])
-
-    for step in range(z.blocks):
-        fetch(step).start()
-    count = mm(cover_ref[...].astype(BF16), own_ref[...].astype(BF16), (0, 1))
-    factor = 1.0 / jnp.maximum(count, 1.0)
-
-    def scale(step):
-        for i in range(step * block, (step + 1) * block):
-            here[:, i * pair : (i + 1) * pair] = (
-                raw[i].astype(F32) * factor[:, i : i + 1]
-            ).astype(BF16)
-
+def mix_kernel(z, l_ref, own_ref, w_ref, mixed, ordered):
+    seqs, pair = z.seqs, z.pair
     order_left(z, l_ref, own_ref, ordered)
     left = ordered[...].astype(BF16)
     group = 8
@@ -198,6 +180,45 @@
                 mixed[(first + e) * seqs : (first + e + 1) * seqs, i * pair : (i + 1) * pair] = part[
                     i * seqs : (i + 1) * seqs, e * pair : (e + 1) * pair
                 ]
+
+
+def mix(z, left, own, weight):
+    return pl.pallas_call(
+        functools.partial(mix_kernel, z),
+        out_shape=pltpu.VMEM((z.wide, z.res * z.pair), BF16),
+        in_specs=[VMEM] * 3,
+        out_specs=VMEM,
+        scratch_shapes=[pltpu.VMEM((z.res * z.seqs, z.width), F32)],
+        compiler_params=params(z.mib // 2),
+        cost_estimate=cost(2),
+        name="mix",
+    )(left, own, weight)
+
+
+def right_sum_kernel(z, mixed, own_ref, cover_ref, g_ref, keep_ref, give_ref, scaled_ref, total,
+                     raw, here, arrived, left_for):
+    core = lax.axis_index(AXIS) % 2
+    seqs, pair, block = z.seqs, z.pair, z.block
+
+    def fetch(step):
+        at = pl.ds(step * block, block)
+        return pltpu.make_async_copy(g_ref.at[at], raw.at[at], arrived.at[step])
+
+    def store(step):
+        span = slice(step * block * pair, (step + 1) * block * pair)
+        return pltpu.make_async_copy(here.at[:, span], scaled_ref.at[:, span], left_for.at[step])
+
+    for step in range(z.blocks):
+        fetch(step).start()
+    count = mm(cover_ref[...].astype(BF16), own_ref[...].astype(BF16), (0, 1))
+    factor = 1.0 / jnp.maximum(count, 1.0)
+
+    def scale(step):
+        for i in range(step * block, (step + 1) * block):
+            here[:, i * pair : (i + 1) * pair] = (
+                raw[i].astype(F32) * factor[:, i : i + 1]
+            ).astype(BF16)
+
     fetch(0).wait()
     scale(0)
     store(0).start()
@@ -223,17 +244,15 @@
         store(step).wait()
 
 
-def right_sum(z, left, own, cover, weight, gradient):
+def right_sum(z, mixed, own, cover, gradient):
     out = (z.chips, z.width, z.cols)
     hbm = pl.BlockSpec(memory_space=pltpu.HBM)
     return pl.pallas_call(
         functools.partial(right_sum_kernel, z),
         out_shape=(sds(out, BF16), sds(out, BF16), pltpu.HBM((z.cols, z.res * z.pair), BF16)),
-        in_specs=[VMEM] * 4 + [hbm],
+        in_specs=[VMEM] * 3 + [hbm],
         out_specs=(VMEM, VMEM, hbm),
         scratch_shapes=[
-            pltpu.VMEM((z.res * z.seqs, z.width), F32),
-            pltpu.VMEM((z.wide, z.res * z.pair), BF16),
             pltpu.VMEM((z.planes, z.wide, LANES), F32),
             pltpu.VMEM(gradient.shape, BF16),
             pltpu.VMEM((z.cols, z.res * z.pair), BF16),
@@ -243,11 +262,11 @@
         compiler_params=params(z.mib),
         cost_estimate=cost(13),
         name="right_sum",
-    )(left, own, cover, weight, in_hbm(gradient))
+    )(in_vmem(mixed), own, cover, in_hbm(gradient))
 
 
 def left_side_kernel(z, here_ref, there_ref, cover_ref, l_ref, own_ref, w_ref, s_ref,
-                     out_ref, ordered, right, proj, back, wide_rows, here, arrived):
+                     keep_ref, give_ref, ordered, right, proj, back, wide_rows, here, arrived):
     me = lax.axis_index(AXIS)
     seqs, pair, block, width = z.seqs, z.pair, z.block, z.width
 
@@ -294,27 +313,34 @@
         total = mm(left, proj[:, first * pair : (first + 8) * pair], (0, 0))
         for e in range(8):
             spread[pl.ds(first + e, width, stride=width), :] = total[:, e * pair : (e + 1) * pair]
-    for d in range(z.size):
-        got = spread[d * z.piece : (d + 1) * z.piece, :]
-        if z.piece_slots > z.piece:
-            got = jnp.concatenate([got, jnp.zeros((z.piece_slots - z.piece, pair), F32)], axis=0)
-        out_ref[d, : z.piece_slots] = got.astype(BF16)
-        parts = [
-            back[pl.ds(g * z.rows * seqs + d, z.rows, stride=seqs), :] for g in range(z.groups)
-        ]
-        parts.append(jnp.zeros((z.rows, LANES - z.groups * width), F32))
-        packed = jnp.concatenate(parts, axis=1)
-        if z.slots > z.rows:
-            packed = jnp.concatenate([packed, jnp.zeros((z.slots - z.rows, LANES), F32)], axis=0)
-        out_ref[d, z.piece_slots :] = packed.astype(BF16)
+    for chip in range(z.chips):
+        for ref, parity in ((keep_ref, me % 2), (give_ref, 1 - me % 2)):
+            d = 2 * chip + parity
+            got = spread[pl.ds(pl.multiple_of(d * z.piece, z.piece), z.piece), :]
+            if z.piece_slots > z.piece:
+                got = jnp.concatenate(
+                    [got, jnp.zeros((z.piece_slots - z.piece, pair), F32)], axis=0
+                )
+            ref[chip, : z.piece_slots] = got.astype(BF16)
+            parts = [
+                back[pl.ds(g * z.rows * seqs + d, z.rows, stride=seqs), :]
+                for g in range(z.groups)
+            ]
+            parts.append(jnp.zeros((z.rows, LANES - z.groups * width), F32))
+            packed = jnp.concatenate(parts, axis=1)
+            if z.slots > z.rows:
+                packed = jnp.concatenate(
+                    [packed, jnp.zeros((z.slots - z.rows, LANES), F32)], axis=0
+                )
+            ref[chip, z.piece_slots :] = packed.astype(BF16)
 
 
 def left_side(z, here, there, cover, left, own, weight, scaled):
     return pl.pallas_call(
         functools.partial(left_side_kernel, z),
-        out_shape=sds((z.size, z.piece_slots + z.slots, LANES), BF16),
+        out_shape=(sds((z.chips, z.piece_slots + z.slots, LANES), BF16),) * 2,
         in_specs=[VMEM] * 6 + [pl.BlockSpec(memory_space=pltpu.HBM)],
-        out_specs=VMEM,
+        out_specs=(VMEM, VMEM),
         scratch_shapes=[
             pltpu.VMEM((z.res * z.seqs, z.width), F32),
             pltpu.VMEM((z.wide, z.cols), BF16),
@@ -339,13 +365,23 @@
         right = right + parts_ref[p].astype(F32)
     right = (right * cover).astype(BF16)
     piece = got_ref[0, : z.piece_slots].astype(F32)
-    for d in range(1, z.size):
-        piece = piece + got_ref[d, : z.piece_slots].astype(F32)
-    for d in range(z.size):
-        got = got_ref[d, z.piece_slots :].astype(F32)
-        for g in range(z.groups):
-            first = d * z.res + g * z.rows
-            rows[first : first + z.rows, :] = got[: z.rows, g * width : (g + 1) * width]
+    for chip in range(1, z.chips):
+        piece = piece + got_ref[chip, : z.piece_slots].astype(F32)
+    core = lax.axis_index(AXIS) % 2
+    for parity in (0, 1):
+
+        @pl.when(core == parity)
+        def _():
+            for chip in range(z.chips):
+                for other in (0, 1):
+                    at = z.piece_slots + other * z.slots
+                    got = got_ref[chip, at : at + z.slots].astype(F32)
+                    for g in range(z.groups):
+                        first = (2 * chip + (parity ^ other)) * z.res + g * z.rows
+                        rows[first : first + z.rows, :] = got[
+                            : z.rows, g * width : (g + 1) * width
+                        ]
+
     column = jnp.transpose(jnp.broadcast_to(cover, (8, z.cols)))[:, :1]
     left = (rows[...] * column).astype(BF16)
     unit = unit_ref[...]
@@ -424,6 +460,28 @@
     )(here, there)
 
 
+def chip_share_kernel(z, here_ref, there_ref, out_ref):
+    top, both = z.piece_slots, z.piece_slots + z.slots
+    for chip in range(z.chips):
+        out_ref[chip, :top] = (
+            here_ref[chip, :top].astype(F32) + there_ref[chip, :top].astype(F32)
+        ).astype(BF16)
+        out_ref[chip, top:both] = here_ref[chip, top:]
+        out_ref[chip, both:] = there_ref[chip, top:]
+
+
+def chip_share(z, here, there):
+    return pl.pallas_call(
+        functools.partial(chip_share_kernel, z),
+        out_shape=sds((z.chips, z.piece_slots + 2 * z.slots, LANES), BF16),
+        in_specs=[VMEM, VMEM],
+        out_specs=VMEM,
+        compiler_params=params(16),
+        cost_estimate=cost(0.5),
+        name="chip_share",
+    )(here, there)
+
+
 def join_kernel(z, *refs):
     *parts, out_ref = refs
     top, more = z.sum_rows, parts[0].shape[0] - z.sum_rows
@@ -542,27 +600,29 @@
     )
     left_all = lax.all_to_all(left, AXIS, 0, 0, tiled=True)
 
-    code = (residue_chain_index + 8 * residue_real_mask).reshape(1, cols)
-    coverage, own_residues, own_sequence, w_mix = cover_all(
-        z, sequence_real_mask, sequence_chain_index, code, output_weight
-    )
-
     here = right[None]
     for bit in z.masks[:-3]:
         here = stack(here, swap_with(here, bit))
     one, two = z.masks[-3:-1]
+    code = (residue_chain_index + 8 * residue_real_mask).reshape(1, cols)
+    code, here = lax.optimization_barrier((code, here))
+    coverage, own_residues, own_sequence, w_mix = cover_all(
+        z, sequence_real_mask, sequence_chain_index, code, output_weight
+    )
     here = stack(here, *[swap_with(here, bit) for bit in (one, two, one ^ two)])
-    left_all, here = lax.optimization_barrier((left_all, here))
+    mixed = mix(z, left_all, own_residues, w_mix)
+    mixed, here = lax.optimization_barrier((mixed, here))
     there = swap_with(here, z.masks[-1])
     keep, give, scaled = right_sum(
-        z, left_all, own_residues, coverage, w_mix, pair_output_gradient
+        z, mixed, own_residues, coverage, pair_output_gradient
     )
     of_chip = pair_sum(keep, swap_with(give, 1))
     parts = lax.all_to_all(of_chip, AXIS, 0, 0, tiled=True, axis_index_groups=same_core)
 
-    shares = left_side(z, here, there, coverage, left_all, own_residues, w_mix, scaled)
+    keep, give = left_side(z, here, there, coverage, left_all, own_residues, w_mix, scaled)
+    shares = chip_share(z, keep, swap_with(give, 1))
     shares, parts = lax.optimization_barrier((shares, parts))
-    got = lax.all_to_all(shares, AXIS, 0, 0, tiled=True)
+    got = lax.all_to_all(shares, AXIS, 0, 0, tiled=True, axis_index_groups=same_core)
 
     sums, grad = owner(z, parts, got, own_sequence, unit, gain, bias, lwt, rwt)
     alignment_gradient = home(z, grad, unit, inverse, gain)

time: 83.4 us -> 80.8 us (0.969)
  blocking collectives: 16 us -> 14.1 us
    all_to_all x1, waiting for transfers between devices: 0.01 us -> 2.32 us  [on_device(): left_all = lax.all_to_all(left, AXIS, 0, 0, tiled=True)]
    pallas_call x1 -> x3, Pallas kernels: 10.9 us -> 13.1 us  [the longest x1 11 us: left_side(): pl.pallas_call(functools.partial(left_side_kernel, z), out_shape=(sds((z....]
    all_to_all x1, blocking collectives: 16 us -> 14.1 us  [on_device(): lax.all_to_all(shares, AXIS, 0, 0, tiled=True, axis_index_groups=same_core)]
    ppermute x11 -> x12, waiting for transfers between devices: 12.6 us -> 10.7 us  [swap_with(): return lax.ppermute(value, AXIS, [(d, d ^ bit) for d in range(size)])]
    pallas_call x1, Pallas kernels: 12.7 us -> 11.2 us  [right_sum(): pl.pallas_call(functools.partial(right_sum_kernel, z), out_shape=(sds(out...]
    all_to_all x1, waiting for transfers between devices: 0.99 us -> 0.01 us  [on_device(): lax.all_to_all(of_chip, AXIS, 0, 0, tiled=True, axis_index_groups=same_core)]
    ppermute x11 -> x12, starting transfers between devices: 13.2 us -> 12.6 us  [swap_with(): return lax.ppermute(value, AXIS, [(d, d ^ bit) for d in range(size)])]
  transfers between devices with their start and end apart: 13 -> 14, of which waited for: 9 -> 8; matrix products, arithmetic and copies ran while one was open for 0% -> 0% of each run, Pallas kernels for 17% -> 21%
where the time goes in v5:
time: 80.8 us; the launch traced here: 80.4 us
  Pallas kernels  32.1 us (40%)
  starting transfers between devices  20.3 us (25%)
  blocking collectives  14.1 us (17%)
  waiting for transfers between devices  13.1 us (16%)
  between operations  0.88 us (1%)
    all_to_all x1, blocking collectives, on_device(): lax.all_to_all(shares, AXIS, 0, 0, tiled=True, axis_index_groups=same_core)  14.1 us
    ppermute x12, starting transfers between devices, swap_with(): return lax.ppermute(value, AXIS, [(d, d ^ bit) for d in range(size)])  12.6 us
    pallas_call x1, Pallas kernels, right_sum(): pl.pallas_call(functools.partial(right_sum_kernel, z), out_shape=(sds(out...  11.2 us
    pallas_call x1, Pallas kernels, left_side(): pl.pallas_call(functools.partial(left_side_kernel, z), out_shape=(sds((z....  11 us
    ppermute x12, waiting for transfers between devices, swap_with(): return lax.ppermute(value, AXIS, [(d, d ^ bit) for d in range(size)])  10.7 us
    all_to_all x1, starting transfers between devices, on_device(): left_all = lax.all_to_all(left, AXIS, 0, 0, tiled=True)  3.91 us
    all_to_all x1, starting transfers between devices, on_device(): lax.all_to_all(of_chip, AXIS, 0, 0, tiled=True, axis_index_groups=same_core)  3.86 us
    pallas_call x1, Pallas kernels, project(): pl.pallas_call(functools.partial(project_kernel, z), out_shape=(sds((z.si...  2.4 us
  transfers between devices with their start and end apart: 14, of which 8 were waited for; matrix products, arithmetic and copies ran while one was open for 0% of the time, Pallas kernels for 21%

profile of v5, /device:TPU:0, one launch (start us, length us, event | category | flops | bytes accessed | tf_op | source)
XLA Modules:
  0.0 80.4 jit_solution(3322579369332820949)
XLA Ops:
  0.7 2.4 %project.1 = (bf16[16,16,128]{2,1,0:T(8,128)(2,1)}, bf16[32,768]{1,0:T(8,128)(2,1)S(1)}, f32[768,256]{1,0:T(8,128)S(1)}, f32[768,1]{1,0:T(8,128)S(1)}) custom-call(bf16[768,256]{1,0:T(8,128)(2,1)} %bitcast.22, f32[1,256]{1,0:T(1,128)} %bitcast.19, f32[1,256]{1,0:T(1,128)} %bitcast.17, bf16[32,256]{1,0:T(8,128)(2,1)} %bitcast.13, bf16[32,256]{1,0:T(8,128)(2,1)} %bitcast.15), custom_call_target="tpu_custom_call" | custom-call | flops 2760000000 | tf_op jit(solution)/shard_map/project/pallas_call | solution.py:100
  3.1 4.0 %collective-permute-start = (bf16[1,32,768]{2,1,0:T(8,128)(2,1)S(1)}, bf16[1,32,768]{2,1,0:T(8,128)(2,1)S(1)}, u32[]{:S(2)}, u32[]{:S(2)}) collective-permute-start(bf16[1,32,768]{2,1,0:T(8,128)(2,1)S(1)} %bitcast.11), channel_id=1, source_target_pairs={{0,8},{1,9},{2,10},{3,11},{4,12},{5,13},{6,14},{7,15},{8,0},{9,1},... | collective-permute-start | bytes 147464 | tf_op jit(solution)/shard_map/ppermute | solution.py:592
  7.1 3.9 %all-to-all-start = ((bf16[16,16,128]{2,1,0:T(8,128)(2,1)}), bf16[16,16,128]{2,1,0:T(8,128)(2,1)S(1)}, u32[]{:S(2)}, u32[]{:S(2)}) async-start(bf16[16,16,128]{2,1,0:T(8,128)(2,1)} %get-tuple-element.34), calls=%async_computation | async-start | bytes 131072 | tf_op jit(solution)/shard_map/all_to_all | solution.py:601
  11.1 2.0 %collective-permute-start.1 = (bf16[2,32,768]{2,1,0:T(8,128)(2,1)S(1)}, bf16[2,32,768]{2,1,0:T(8,128)(2,1)S(1)}, u32[]{:S(2)}, u32[]{:S(2)}) collective-permute-start(bf16[2,32,768]{2,1,0:T(8,128)(2,1)S(1)} %stack.2.refs_0_), channel_id=1, source_target_pairs={{0,4},{1,5},{2,6},{3,7},{4,0},{5,1},{6,2},{7,3},{8,12},{9,13},{10,... | collective-permute-start | bytes 294920 | tf_op jit(solution)/shard_map/ppermute | solution.py:592
  13.1 1.5 %collective-permute-start.2 = (bf16[2,32,768]{2,1,0:T(8,128)(2,1)S(1)}, bf16[2,32,768]{2,1,0:T(8,128)(2,1)S(1)}, u32[]{:S(2)}, u32[]{:S(2)}) collective-permute-start(bf16[2,32,768]{2,1,0:T(8,128)(2,1)S(1)} %stack.2.refs_0_), channel_id=1, source_target_pairs={{0,2},{1,3},{2,0},{3,1},{4,6},{5,7},{6,4},{7,5},{8,10},{9,11},{10,... | collective-permute-start | bytes 294920 | tf_op jit(solution)/shard_map/ppermute | solution.py:592
  14.6 0.1 collective-permute-start.3
  14.7 1.4 %cover.1 = (f32[16,768]{1,0:T(8,128)S(1)}, f32[48,16]{1,0:T(8,128)S(1)}, f32[1,768]{1,0:T(1,128)S(1)}, bf16[32,4096]{1,0:T(8,128)(2,1)S(1)}) custom-call(s32[16]{0:T(128)S(1)} %copy-done.4, s32[16]{0:T(128)S(1)} %copy-done.5, s32[1,768]{1,0:T(1,128)S(1)} %reshape.36.code_ref, bf16[1024,128]{1,0:T(8,128)(2,1)} %w_ref.1), custom_call_target="tpu_custom_call" | custom-call | flops 1610000000 | tf_op jit(solution)/shard_map/cover/pallas_call | solution.py:140
  16.1 2.3 %all-to-all-done.l_ref = bf16[16,16,128]{2,1,0:T(8,128)(2,1)S(1)} async-done(((bf16[16,16,128]{2,1,0:T(8,128)(2,1)}), bf16[16,16,128]{2,1,0:T(8,128)(2,1)S(1)}, u32[]{:S(2)}, u32[]{:S(2)}) %all-to-all-start) | async-done | bytes 65568 | tf_op jit(solution)/shard_map/all_to_all | solution.py:601
  18.4 2.1 %mix.1.mixed = bf16[512,6144]{1,0:T(8,128)(2,1)S(1)} custom-call(bf16[16,16,128]{2,1,0:T(8,128)(2,1)S(1)} %all-to-all-done.l_ref, f32[48,16]{1,0:T(8,128)S(1)} %get-tuple-element.37.own_ref, bf16[32,4096]{1,0:T(8,128)(2,1)S(1)} %get-tuple-element.38.w_ref), custom_call_target="tpu_custom_call" | custom-call | flops 2300000000 | tf_op jit(solution)/shard_map/mix/pallas_call | solution.py:186
  20.5 11.2 %right_sum.1 = (bf16[8,32,768]{2,1,0:T(8,128)(2,1)S(1)}, bf16[8,32,768]{2,1,0:T(8,128)(2,1)S(1)}, bf16[768,6144]{1,0:T(8,128)(2,1)}) custom-call(bf16[512,6144]{1,0:T(8,128)(2,1)S(1)} %mix.1.mixed, f32[48,16]{1,0:T(8,128)S(1)} %get-tuple-element.37.own_ref, f32[16,768]{1,0:T(8,128)S(1)} %get-tuple-element.41.cover_ref, bf16[48,768,128]{2,1,0:T(8,128)(2,1)} %g_ref.1), custom_call_target="tpu_custom_call" | custom-call | flops 14949999616 | tf_op jit(solution)/shard_map/right_sum/pallas_call | solution.py:250
  31.7 0.1 collective-permute-start.6
  31.8 0.5 collective-permute-start.4
  32.3 1.2 %collective-permute-done.6.there_ref = bf16[8,32,768]{2,1,0:T(8,128)(2,1)S(1)} collective-permute-done((bf16[8,32,768]{2,1,0:T(8,128)(2,1)S(1)}, bf16[8,32,768]{2,1,0:T(8,128)(2,1)S(1)}, u32[]{:S(2)}, u32[]{:S(2)}) %collective-permute-start.6) | collective-permute-done | bytes 393248 | tf_op jit(solution)/shard_map/ppermute | solution.py:592
  33.5 0.8 %pair_sum.1 = bf16[8,32,768]{2,1,0:T(8,128)(2,1)} custom-call(bf16[8,32,768]{2,1,0:T(8,128)(2,1)S(1)} %get-tuple-element.46.here_ref, bf16[8,32,768]{2,1,0:T(8,128)(2,1)S(1)} %collective-permute-done.6.there_ref), custom_call_target="tpu_custom_call" | custom-call | flops 920000000 | tf_op jit(solution)/shard_map/pair_sum/pallas_call | solution.py:452
  34.4 3.9 %all-to-all-start.1 = ((bf16[8,32,768]{2,1,0:T(8,128)(2,1)}), bf16[8,32,768]{2,1,0:T(8,128)(2,1)S(1)}, u32[]{:S(2)}, u32[]{:S(2)}) async-start(bf16[8,32,768]{2,1,0:T(8,128)(2,1)} %pair_sum.1), calls=%async_computation.1 | async-start | bytes 786432 | tf_op jit(solution)/shard_map/all_to_all | solution.py:620
  38.3 11.0 %left_side.1 = (bf16[8,80,128]{2,1,0:T(8,128)(2,1)S(1)}, bf16[8,80,128]{2,1,0:T(8,128)(2,1)S(1)}) custom-call(bf16[8,32,768]{2,1,0:T(8,128)(2,1)S(1)} %stack.3.here_ref, bf16[8,32,768]{2,1,0:T(8,128)(2,1)S(1)} %collective-permute-done.4.there_ref, f32[16,768]{1,0:T(8,128)S(1)} %get-tuple-element.41.cover_ref, bf16[16,16,128]{2,1,0:T(8,128)(2,1)S(1)} %all-to-all-done.l_ref, ...), custom_call_target="tpu_custom_call" | custom-call | flops 12650000384 | tf_op jit(solution)/shard_map/left_side/pallas_call | solution.py:339
  49.3 0.1 collective-permute-start.5
  49.3 1.4 %collective-permute-done.5.there_ref = bf16[8,80,128]{2,1,0:T(8,128)(2,1)S(1)} collective-permute-done((bf16[8,80,128]{2,1,0:T(8,128)(2,1)S(1)}, bf16[8,80,128]{2,1,0:T(8,128)(2,1)S(1)}, u32[]{:S(2)}, u32[]{:S(2)}) %collective-permute-start.5) | collective-permute-done | bytes 163872 | tf_op jit(solution)/shard_map/ppermute | solution.py:592
  50.8 14.1 %all_to_all.15.got_ref = bf16[8,96,128]{2,1,0:T(8,128)(2,1)S(1)} all-to-all(bf16[8,96,128]{2,1,0:T(8,128)(2,1)S(1)} %chip_share.1), channel_id=1, replica_groups={{0,2,4,6,8,10,12,14},{1,3,5,7,9,11,13,15},{16,18,20,22,24,26,28,30},{17..., dimensions={0} | all-to-all | bytes 393216 | tf_op jit(solution)/shard_map/all_to_all | solution.py:625
  64.8 1.0 %owner.1 = (bf16[208,128]{1,0:T(8,128)(2,1)S(1)}, f32[768,256]{1,0:T(8,128)S(1)}) custom-call(bf16[8,32,768]{2,1,0:T(8,128)(2,1)S(1)} %all-to-all-done.1.parts_ref, bf16[8,96,128]{2,1,0:T(8,128)(2,1)S(1)} %all_to_all.15.got_ref, f32[1,768]{1,0:T(1,128)S(1)} %get-tuple-element.50.cover_ref, f32[768,256]{1,0:T(8,128)S(1)} %get-tuple-element.51.unit_ref, ...), custom_call_target="tpu_custom_call" | custom-call | flops 1035000000 | tf_op jit(solution)/shard_map/owner/pallas_call | solution.py:411
  65.8 0.7 collective-permute-start.7
  66.5 1.3 %home.1 = bf16[768,256]{1,0:T(8,128)(2,1)} custom-call(f32[768,256]{1,0:T(8,128)S(1)} %get-tuple-element.53.grad_ref, f32[768,256]{1,0:T(8,128)S(1)} %get-tuple-element.51.unit_ref, f32[768,1]{1,0:T(8,128)S(1)} %get-tuple-element.54.inverse_ref, f32[1,256]{1,0:T(1,128)S(1)} %bitcast.21), custom_call_target="tpu_custom_call" | custom-call | flops 1380000000 | tf_op jit(solution)/shard_map/home/pallas_call | solution.py:559
  67.8 3.4 %collective-permute-done.7.refs_1_ = bf16[208,128]{1,0:T(8,128)(2,1)S(1)} collective-permute-done((bf16[208,128]{1,0:T(8,128)(2,1)S(1)}, bf16[208,128]{1,0:T(8,128)(2,1)S(1)}, u32[]{:S(2)}, u32[]{:S(2)}) %collective-permute-start.7) | collective-permute-done | bytes 53280 | tf_op jit(solution)/shard_map/ppermute | solution.py:592
  71.2 0.6 collective-permute-start.10
  71.8 2.0 %collective-permute-start.8 = (bf16[272,128]{1,0:T(8,128)(2,1)S(1)}, bf16[272,128]{1,0:T(8,128)(2,1)S(1)}, u32[]{:S(2)}, u32[]{:S(2)}) collective-permute-start(bf16[272,128]{1,0:T(8,128)(2,1)S(1)} %join.2.refs_0_), channel_id=1, source_target_pairs={{0,4},{1,5},{2,6},{3,7},{4,0},{5,1},{6,2},{7,3},{8,12},{9,13},{10,... | collective-permute-start | bytes 208904 | tf_op jit(solution)/shard_map/ppermute | solution.py:592
  73.8 0.9 %collective-permute-start.9 = (bf16[272,128]{1,0:T(8,128)(2,1)S(1)}, bf16[272,128]{1,0:T(8,128)(2,1)S(1)}, u32[]{:S(2)}, u32[]{:S(2)}) collective-permute-start(bf16[272,128]{1,0:T(8,128)(2,1)S(1)} %join.2.refs_0_), channel_id=1, source_target_pairs={{0,2},{1,3},{2,0},{3,1},{4,6},{5,7},{6,4},{7,5},{8,10},{9,11},{10,... | collective-permute-start | bytes 208904 | tf_op jit(solution)/shard_map/ppermute | solution.py:592
  74.7 1.7 %collective-permute-done.10.refs_3_ = bf16[272,128]{1,0:T(8,128)(2,1)S(1)} collective-permute-done((bf16[272,128]{1,0:T(8,128)(2,1)S(1)}, bf16[272,128]{1,0:T(8,128)(2,1)S(1)}, u32[]{:S(2)}, u32[]{:S(2)}) %collective-permute-start.10) | collective-permute-done | bytes 69664 | tf_op jit(solution)/shard_map/ppermute | solution.py:592
  76.4 0.4 collective-permute-done.8.refs_1_
  76.8 1.3 %collective-permute-done.9.refs_2_ = bf16[272,128]{1,0:T(8,128)(2,1)S(1)} collective-permute-done((bf16[272,128]{1,0:T(8,128)(2,1)S(1)}, bf16[272,128]{1,0:T(8,128)(2,1)S(1)}, u32[]{:S(2)}, u32[]{:S(2)}) %collective-permute-start.9) | collective-permute-done | bytes 69664 | tf_op jit(solution)/shard_map/ppermute | solution.py:592
  78.1 0.1 collective-permute-start.11
  78.2 1.4 %collective-permute-done.11.there_ref = bf16[656,128]{1,0:T(8,128)(2,1)S(1)} collective-permute-done((bf16[656,128]{1,0:T(8,128)(2,1)S(1)}, bf16[656,128]{1,0:T(8,128)(2,1)S(1)}, u32[]{:S(2)}, u32[]{:S(2)}) %collective-permute-start.11) | collective-permute-done | bytes 167968 | tf_op jit(solution)/shard_map/ppermute | solution.py:592
  79.6 0.9 %finish.1 = (f32[32,256]{1,0:T(8,128)}, f32[32,256]{1,0:T(8,128)}, f32[1,256]{1,0:T(1,128)}, f32[1,256]{1,0:T(1,128)}, f32[1024,128]{1,0:T(8,128)}) custom-call(bf16[656,128]{1,0:T(8,128)(2,1)S(1)} %join.3.here_ref, bf16[656,128]{1,0:T(8,128)(2,1)S(1)} %collective-permute-done.11.there_ref), custom_call_target="tpu_custom_call" | custom-call | flops 1035000000 | tf_op jit(solution)/shard_map/finish/pallas_call | solution.py:528
  (29 shorter events, 0.2 us)
Async XLA Ops:
  0.6 10.4 %copy-start.7 = (s32[768]{0:T(1024)S(1)}, s32[768]{0:T(1024)}, u32[]{:S(2)}) copy-start(s32[768]{0:T(1024)} %param.20) | copy-start | bytes 9220
  0.6 10.4 %copy-start.6 = (s32[768]{0:T(1024)S(1)}, s32[768]{0:T(1024)}, u32[]{:S(2)}) copy-start(s32[768]{0:T(1024)} %param.21) | copy-start | bytes 9220
  0.7 14.0 %copy-start.4 = (s32[16]{0:T(128)S(1)}, s32[16]{0:T(128)}, u32[]{:S(2)}) copy-start(s32[16]{0:T(128)} %smask_ref.1) | copy-start | bytes 196
  0.7 14.0 %copy-start.5 = (s32[16]{0:T(128)S(1)}, s32[16]{0:T(128)}, u32[]{:S(2)}) copy-start(s32[16]{0:T(128)} %schain_ref.1) | copy-start | bytes 196
  3.1 8.0 %collective-permute-start = (bf16[1,32,768]{2,1,0:T(8,128)(2,1)S(1)}, bf16[1,32,768]{2,1,0:T(8,128)(2,1)S(1)}, u32[]{:S(2)}, u32[]{:S(2)}) collective-permute-start(bf16[1,32,768]{2,1,0:T(8,128)(2,1)S(1)} %bitcast.11), channel_id=1, source_target_pairs={{0,8},{1,9},{2,10},{3,11},{4,12},{5,13},{6,14},{7,15},{8,0},{9,1},... | collective-permute-start | bytes 147464 | tf_op jit(solution)/shard_map/ppermute | solution.py:592
  7.1 11.3 %all-to-all-start = ((bf16[16,16,128]{2,1,0:T(8,128)(2,1)}), bf16[16,16,128]{2,1,0:T(8,128)(2,1)S(1)}, u32[]{:S(2)}, u32[]{:S(2)}) async-start(bf16[16,16,128]{2,1,0:T(8,128)(2,1)} %get-tuple-element.34), calls=%async_computation | async-start | bytes 131072 | tf_op jit(solution)/shard_map/all_to_all | solution.py:601
  11.1 9.4 %collective-permute-start.1 = (bf16[2,32,768]{2,1,0:T(8,128)(2,1)S(1)}, bf16[2,32,768]{2,1,0:T(8,128)(2,1)S(1)}, u32[]{:S(2)}, u32[]{:S(2)}) collective-permute-start(bf16[2,32,768]{2,1,0:T(8,128)(2,1)S(1)} %stack.2.refs_0_), channel_id=1, source_target_pairs={{0,4},{1,5},{2,6},{3,7},{4,0},{5,1},{6,2},{7,3},{8,12},{9,13},{10,... | collective-permute-start | bytes 294920 | tf_op jit(solution)/shard_map/ppermute | solution.py:592
  13.1 7.4 %collective-permute-start.2 = (bf16[2,32,768]{2,1,0:T(8,128)(2,1)S(1)}, bf16[2,32,768]{2,1,0:T(8,128)(2,1)S(1)}, u32[]{:S(2)}, u32[]{:S(2)}) collective-permute-start(bf16[2,32,768]{2,1,0:T(8,128)(2,1)S(1)} %stack.2.refs_0_), channel_id=1, source_target_pairs={{0,2},{1,3},{2,0},{3,1},{4,6},{5,7},{6,4},{7,5},{8,10},{9,11},{10,... | collective-permute-start | bytes 294920 | tf_op jit(solution)/shard_map/ppermute | solution.py:592
  14.6 5.9 %collective-permute-start.3 = (bf16[2,32,768]{2,1,0:T(8,128)(2,1)S(1)}, bf16[2,32,768]{2,1,0:T(8,128)(2,1)S(1)}, u32[]{:S(2)}, u32[]{:S(2)}) collective-permute-start(bf16[2,32,768]{2,1,0:T(8,128)(2,1)S(1)} %stack.2.refs_0_), channel_id=1, source_target_pairs={{0,6},{1,7},{2,4},{3,5},{4,2},{5,3},{6,0},{7,1},{8,14},{9,15},{10,... | collective-permute-start | bytes 294920 | tf_op jit(solution)/shard_map/ppermute | solution.py:592
  31.7 1.8 %collective-permute-start.6 = (bf16[8,32,768]{2,1,0:T(8,128)(2,1)S(1)}, bf16[8,32,768]{2,1,0:T(8,128)(2,1)S(1)}, u32[]{:S(2)}, u32[]{:S(2)}) collective-permute-start(bf16[8,32,768]{2,1,0:T(8,128)(2,1)S(1)} %get-tuple-element.47), channel_id=1, source_target_pairs={{0,1},{1,0},{2,3},{3,2},{4,5},{5,4},{6,7},{7,6},{8,9},{9,8},{10,11... | collective-permute-start | bytes 1179656 | tf_op jit(solution)/shard_map/ppermute | solution.py:592
  31.8 6.4 %collective-permute-start.4 = (bf16[8,32,768]{2,1,0:T(8,128)(2,1)S(1)}, bf16[8,32,768]{2,1,0:T(8,128)(2,1)S(1)}, u32[]{:S(2)}, u32[]{:S(2)}) collective-permute-start(bf16[8,32,768]{2,1,0:T(8,128)(2,1)S(1)} %stack.3.here_ref), channel_id=1, source_target_pairs={{0,1},{1,0},{2,3},{3,2},{4,5},{5,4},{6,7},{7,6},{8,9},{9,8},{10,11... | collective-permute-start | bytes 1179656 | tf_op jit(solution)/shard_map/ppermute | solution.py:592
  34.4 16.4 %all-to-all-start.1 = ((bf16[8,32,768]{2,1,0:T(8,128)(2,1)}), bf16[8,32,768]{2,1,0:T(8,128)(2,1)S(1)}, u32[]{:S(2)}, u32[]{:S(2)}) async-start(bf16[8,32,768]{2,1,0:T(8,128)(2,1)} %pair_sum.1), calls=%async_computation.1 | async-start | bytes 786432 | tf_op jit(solution)/shard_map/all_to_all | solution.py:620
  38.2 26.6 %copy-start = (bf16[256,32]{0,1:T(8,128)(2,1)S(1)}, bf16[256,32]{0,1:T(8,128)(2,1)}, u32[]{:S(2)}) copy-start(bf16[256,32]{0,1:T(8,128)(2,1)} %param.14) | copy-start | bytes 49156
  38.3 26.6 %copy-start.1 = (bf16[256,32]{0,1:T(8,128)(2,1)S(1)}, bf16[256,32]{0,1:T(8,128)(2,1)}, u32[]{:S(2)}) copy-start(bf16[256,32]{0,1:T(8,128)(2,1)} %param.15) | copy-start | bytes 49156
  38.3 26.6 %copy-start.2 = (f32[256]{0:T(256)S(1)}, f32[256]{0:T(256)}, u32[]{:S(2)}) copy-start(f32[256]{0:T(256)} %param.13) | copy-start | bytes 3076
  38.3 26.6 %copy-start.3 = (f32[256]{0:T(256)S(1)}, f32[256]{0:T(256)}, u32[]{:S(2)}) copy-start(f32[256]{0:T(256)} %param.12) | copy-start | bytes 3076
  49.3 1.5 %collective-permute-start.5 = (bf16[8,80,128]{2,1,0:T(8,128)(2,1)S(1)}, bf16[8,80,128]{2,1,0:T(8,128)(2,1)S(1)}, u32[]{:S(2)}, u32[]{:S(2)}) collective-permute-start(bf16[8,80,128]{2,1,0:T(8,128)(2,1)S(1)} %get-tuple-element.45), channel_id=1, source_target_pairs={{0,1},{1,0},{2,3},{3,2},{4,5},{5,4},{6,7},{7,6},{8,9},{9,8},{10,11... | collective-permute-start | bytes 491528 | tf_op jit(solution)/shard_map/ppermute | solution.py:592
  65.8 5.3 %collective-permute-start.7 = (bf16[208,128]{1,0:T(8,128)(2,1)S(1)}, bf16[208,128]{1,0:T(8,128)(2,1)S(1)}, u32[]{:S(2)}, u32[]{:S(2)}) collective-permute-start(bf16[208,128]{1,0:T(8,128)(2,1)S(1)} %get-tuple-element.52.refs_0_), channel_id=1, source_target_pairs={{0,8},{1,9},{2,10},{3,11},{4,12},{5,13},{6,14},{7,15},{8,0},{9,1},... | collective-permute-start | bytes 159752 | tf_op jit(solution)/shard_map/ppermute | solution.py:592
  71.2 5.3 %collective-permute-start.10 = (bf16[272,128]{1,0:T(8,128)(2,1)S(1)}, bf16[272,128]{1,0:T(8,128)(2,1)S(1)}, u32[]{:S(2)}, u32[]{:S(2)}) collective-permute-start(bf16[272,128]{1,0:T(8,128)(2,1)S(1)} %join.2.refs_0_), channel_id=1, source_target_pairs={{0,6},{1,7},{2,4},{3,5},{4,2},{5,3},{6,0},{7,1},{8,14},{9,15},{10,... | collective-permute-start | bytes 208904 | tf_op jit(solution)/shard_map/ppermute | solution.py:592
  71.8 5.0 %collective-permute-start.8 = (bf16[272,128]{1,0:T(8,128)(2,1)S(1)}, bf16[272,128]{1,0:T(8,128)(2,1)S(1)}, u32[]{:S(2)}, u32[]{:S(2)}) collective-permute-start(bf16[272,128]{1,0:T(8,128)(2,1)S(1)} %join.2.refs_0_), channel_id=1, source_target_pairs={{0,4},{1,5},{2,6},{3,7},{4,0},{5,1},{6,2},{7,3},{8,12},{9,13},{10,... | collective-permute-start | bytes 208904 | tf_op jit(solution)/shard_map/ppermute | solution.py:592
  73.8 4.3 %collective-permute-start.9 = (bf16[272,128]{1,0:T(8,128)(2,1)S(1)}, bf16[272,128]{1,0:T(8,128)(2,1)S(1)}, u32[]{:S(2)}, u32[]{:S(2)}) collective-permute-start(bf16[272,128]{1,0:T(8,128)(2,1)S(1)} %join.2.refs_0_), channel_id=1, source_target_pairs={{0,2},{1,3},{2,0},{3,1},{4,6},{5,7},{6,4},{7,5},{8,10},{9,11},{10,... | collective-permute-start | bytes 208904 | tf_op jit(solution)/shard_map/ppermute | solution.py:592
  78.1 1.5 %collective-permute-start.11 = (bf16[656,128]{1,0:T(8,128)(2,1)S(1)}, bf16[656,128]{1,0:T(8,128)(2,1)S(1)}, u32[]{:S(2)}, u32[]{:S(2)}) collective-permute-start(bf16[656,128]{1,0:T(8,128)(2,1)S(1)} %join.3.here_ref), channel_id=1, source_target_pairs={{0,1},{1,0},{2,3},{3,2},{4,5},{5,4},{6,7},{7,6},{8,9},{9,8},{10,11... | collective-permute-start | bytes 503816 | tf_op jit(solution)/shard_map/ppermute | solution.py:592
